TPU v7x, 256 devices: a whole 4x4x8 slice. The times are simulated.
256 devices in a mesh: seq: 64 (over z, y, core), head: 4 (over x).
Axes of the slice: x: 4, y: 4, z: 8, core: 2. Of those that a mesh axis runs over, the one named last changes fastest.
Arguments:
- query_rows: bfloat16 [16384, 8192], P('seq', 'head'), may hold values from -1.796875 to 1.796875
- key_rows: bfloat16 [16384, 8192], P('seq', 'head'), may hold values from -1.796875 to 1.796875
- value_rows: bfloat16 [16384, 8192], P('seq', 'head'), may hold values from -20 to 20, as said below
- gate: bfloat16 [16384, 8192], P('seq', 'head'), may hold values from -6 to 6
- log_decay: float32 [16384, 64], P('seq', 'head'), may hold values from -1 to 0, as said below
- gain: float32 [8192], P('head'), may hold values from 0.1 to 1.9
- grad_mixed: bfloat16 [16384, 8192], P('seq', 'head'), may hold values from -6 to 6
Outputs:
- mixed: bfloat16 [16384, 8192], P('seq', 'head')
- grad_query: bfloat16 [16384, 8192], P('seq', 'head')
- grad_key: bfloat16 [16384, 8192], P('seq', 'head')
- grad_value: bfloat16 [16384, 8192], P('seq', 'head')
- grad_gate: bfloat16 [16384, 8192], P('seq', 'head')
Inputs may be any that keep to these rules, and one draw needn't show every extreme that they name: `value_rows`: values of the heads differ in scale. `log_decay`: Per-token log decays; rates differ over heads and tokens.
All inputs are finite; a program needn't handle non-finite values.
Results may differ from a plain program's by a relative error of at most 0.006.
Values sent between devices are 32-bit elements; how exact they have to be, the bound alone decides.
No kernel may reach another device: no remote copies, remote signals or barrier semaphores. Data moves between devices by JAX's collectives and lax.ppermute only.
A program may use at most 192 MiB of HBM per device.

v0:
```python
import jax
import jax.numpy as jnp
from jax import lax
from jax.sharding import PartitionSpec as P

HEAD_COUNT = 64
DH = 128
GROUP = 256


EPSILON = 1e-06


def shifted(array, axis, by):
    length = lax.axis_size(axis)
    pairs = [(i, i + by) for i in range(length) if 0 <= i + by < length]
    return lax.ppermute(array, axis, pairs)


def decay_table(decays):
    cumulative = jnp.cumsum(decays, axis=0)
    across = cumulative.T
    length = across.shape[1]
    rows = lax.broadcasted_iota(jnp.int32, (length, length), 0)
    columns = lax.broadcasted_iota(jnp.int32, (length, length), 1)
    gaps = across[:, :, None] - across[:, None, :]
    weights = jnp.exp(jnp.where((rows >= columns)[None], gaps, -jnp.inf))
    return (cumulative, weights)


def combine(earlier, later):
    return (earlier[0] * later[0], later[0][:, None, None] * earlier[1] + later[1])


def doubling(decay_own, state_own, direction):
    count = lax.axis_size("seq")
    index = lax.axis_index("seq")
    decay_part, state_part = shifted((decay_own, state_own), "seq", direction)
    if direction > 0:
        first_present = index >= 1
    else:
        first_present = index + 1 < count
    decay_part = jnp.where(first_present, decay_part, 1.0)
    span = 1
    while span < count:
        far_decay, far_state = shifted((decay_part, state_part), "seq", direction * span)
        if direction > 0:
            present = index >= span + 1
        else:
            present = index + span + 1 < count
        far_decay = jnp.where(present, far_decay, 1.0)
        state_part = decay_part[:, None, None] * far_state + state_part
        decay_part = far_decay * decay_part
        span = span * 2
    return state_part


def on_device(query_rows, key_rows, value_rows, gate, log_decay, gain, grad_mixed):
    rows_here = log_decay.shape[0]
    local_heads = log_decay.shape[1]
    blocks = rows_here // GROUP
    features = HEAD_COUNT * DH

    def split(values):
        return values.reshape(blocks, GROUP, local_heads, DH)

    query = split(query_rows)
    keys = split(key_rows)
    value = split(value_rows)
    decays = log_decay.reshape(blocks, GROUP, local_heads)
    unit = jnp.ones((local_heads,), jnp.float32)
    zero_state = jnp.zeros((local_heads, DH, DH), jnp.float32)

    def summarize(carry, inputs):
        block_keys, block_value, block_decays = inputs
        cumulative = jnp.cumsum(block_decays, axis=0)
        last = cumulative[-1]
        keyed = (block_keys * jnp.exp(last[None, :] - cumulative)[:, :, None]).astype(jnp.bfloat16)
        local = jnp.einsum("thd,the->hde", keyed, block_value, preferred_element_type=jnp.float32)
        factor = jnp.exp(last)
        return (combine(carry, (factor, local)), (factor, local))

    (total_decay, total_state), (factors, pieces) = lax.scan(
        summarize, (unit, zero_state), (keys, value, decays)
    )
    entering = doubling(total_decay, total_state, 1)

    def advance(state, inputs):
        block_query, block_keys, block_value, block_decays, factor, piece = inputs
        cumulative, weights = decay_table(block_decays)
        scores = jnp.einsum(
            "thd,shd->hts", block_query, block_keys, preferred_element_type=jnp.float32
        )
        probs = (scores * weights).astype(jnp.bfloat16)
        intra = jnp.einsum("hts,shd->thd", probs, block_value, preferred_element_type=jnp.float32)
        inter = jnp.einsum(
            "thd,hde->the",
            block_query,
            state.astype(jnp.bfloat16),
            preferred_element_type=jnp.float32,
        )
        inter = inter * jnp.exp(cumulative)[:, :, None]
        return (factor[:, None, None] * state + piece, (intra + inter, state))

    unused, (attention, befores) = lax.scan(
        advance, entering, (query, keys, value, decays, factors, pieces)
    )
    attention = attention.reshape(rows_here, local_heads * DH)
    opening = jax.nn.sigmoid(gate.astype(jnp.float32))
    upstream = grad_mixed.astype(jnp.float32)
    grad_normed = upstream * opening * gain
    squares = lax.psum(jnp.sum(attention * attention, axis=1), "head")
    scale = lax.rsqrt(squares / features + EPSILON)[:, None]
    normed = attention * scale
    products = lax.psum(jnp.sum(grad_normed * normed, axis=1), "head")
    projection = (products / features)[:, None]
    shaped = normed * gain
    mixed = (shaped * opening).astype(jnp.bfloat16)
    grad_gate = (upstream * shaped * opening * (1.0 - opening)).astype(jnp.bfloat16)
    grad_attention = (scale * (grad_normed - normed * projection)).astype(jnp.bfloat16)
    grad_attention = split(grad_attention)

    def gradient_terms(carry, inputs):
        block_query, block_decays, block_grad, factor = inputs
        cumulative = jnp.cumsum(block_decays, axis=0)
        weighted = (block_query * jnp.exp(cumulative)[:, :, None]).astype(jnp.bfloat16)
        term = jnp.einsum("thd,the->hde", weighted, block_grad, preferred_element_type=jnp.float32)
        return ((carry[0] * factor, term + factor[:, None, None] * carry[1]), term)

    (suffix_decay, suffix_state), terms = lax.scan(
        gradient_terms, (unit, zero_state), (query, decays, grad_attention, factors), reverse=True
    )
    leaving = doubling(suffix_decay, suffix_state, -1)

    def retreat(after, inputs):
        block_query, block_keys, block_value, block_decays, block_grad, before, factor, term = (
            inputs
        )
        cumulative, weights = decay_table(block_decays)
        last = cumulative[-1]
        scores = jnp.einsum(
            "thd,shd->hts", block_query, block_keys, preferred_element_type=jnp.float32
        )
        probs = (scores * weights).astype(jnp.bfloat16)
        grad_raw = jnp.einsum(
            "thd,shd->hts", block_grad, block_value, preferred_element_type=jnp.float32
        )
        grad_scores = (grad_raw * weights).astype(jnp.bfloat16)
        toward_start = jnp.exp(cumulative)[:, :, None]
        toward_end = jnp.exp(last[None, :] - cumulative)[:, :, None]
        after_low = after.astype(jnp.bfloat16)
        grad_q = jnp.einsum(
            "hts,shd->thd", grad_scores, block_keys, preferred_element_type=jnp.float32
        )
        grad_q = (
            grad_q
            + jnp.einsum(
                "the,hde->thd",
                block_grad,
                before.astype(jnp.bfloat16),
                preferred_element_type=jnp.float32,
            )
            * toward_start
        )
        grad_k = jnp.einsum(
            "hts,thd->shd", grad_scores, block_query, preferred_element_type=jnp.float32
        )
        grad_k = (
            grad_k
            + jnp.einsum("she,hde->shd", block_value, after_low, preferred_element_type=jnp.float32)
            * toward_end
        )
        grad_v = jnp.einsum("hts,the->she", probs, block_grad, preferred_element_type=jnp.float32)
        grad_v = (
            grad_v
            + jnp.einsum("shd,hde->she", block_keys, after_low, preferred_element_type=jnp.float32)
            * toward_end
        )
        updated = factor[:, None, None] * after + term
        return (
            updated,
            (grad_q.astype(jnp.bfloat16), grad_k.astype(jnp.bfloat16), grad_v.astype(jnp.bfloat16)),
        )

    unused_after, (grad_q, grad_k, grad_v) = lax.scan(
        retreat,
        leaving,
        (query, keys, value, decays, grad_attention, befores, factors, terms),
        reverse=True,
    )
    width = local_heads * DH
    return (
        mixed,
        grad_q.reshape(rows_here, width),
        grad_k.reshape(rows_here, width),
        grad_v.reshape(rows_here, width),
        grad_gate,
    )


def solution(mesh):
    in_specs = (
        P("seq", "head"),
        P("seq", "head"),
        P("seq", "head"),
        P("seq", "head"),
        P("seq", "head"),
        P("head"),
        P("seq", "head"),
    )
    out_specs = (
        P("seq", "head"),
        P("seq", "head"),
        P("seq", "head"),
        P("seq", "head"),
        P("seq", "head"),
    )
    return jax.shard_map(
        on_device, mesh=mesh, in_specs=in_specs, out_specs=out_specs, check_vma=False
    )
```

profile of v0, /device:TPU:83, one launch (start us, length us, event | category | flops | bytes accessed | tf_op | source)
XLA Modules:
  0.0 532.8 jit_solution(14082344600722251947)
XLA Ops:
  4.5 3.5 collective-permute-start.6
  8.0 11.7 %collective-permute-done.6 = f32[16,128,128]{2,1,0:T(8,128)S(1)} collective-permute-done((f32[16,128,128]{2,1,0:T(8,128)S(1)}, f32[16,128,128]{2,1,0:T(8,128)S(1)}, u32[]{:S(2)}, u32[]{:S(2)}) %collective-permute-start.6) | collective-permute-done | bytes 1048608 | tf_op jit(solution)/shard_map/ppermute | solution.py:17
  19.7 4.4 collective-permute-start.7
  26.1 9.8 %collective-permute-done = f32[16]{0:T(128)S(1)} collective-permute-done((f32[16]{0:T(128)S(1)}, f32[16]{0:T(128)S(1)}, u32[]{:S(2)}, u32[]{:S(2)}) %collective-permute-start) | collective-permute-done | bytes 96 | tf_op jit(solution)/shard_map/ppermute | solution.py:17
  37.6 5.3 collective-permute-start.8
  42.9 6.8 %collective-permute-start.1 = (f32[16]{0:T(128)S(1)}, f32[16]{0:T(128)S(1)}, u32[]{:S(2)}, u32[]{:S(2)}) collective-permute-start(f32[16]{0:T(128)S(1)} %broadcast_select_fusion.6), channel_id=1, source_target_pairs={{0,4},{4,8},{8,12},{12,16},{16,20},{20,24},{24,28},{28,32},{32,36}... | collective-permute-start | bytes 200 | tf_op jit(solution)/shard_map/ppermute | solution.py:17
  49.8 15.9 %collective-permute-done.1 = f32[16]{0:T(128)S(1)} collective-permute-done((f32[16]{0:T(128)S(1)}, f32[16]{0:T(128)S(1)}, u32[]{:S(2)}, u32[]{:S(2)}) %collective-permute-start.1) | collective-permute-done | bytes 96 | tf_op jit(solution)/shard_map/ppermute | solution.py:17
  65.7 2.4 multiply_add_fusion.8
  69.9 3.9 collective-permute-start.2
  73.8 2.5 collective-permute-done.2
  76.4 20.1 %collective-permute-done.9 = f32[16,128,128]{2,1,0:T(8,128)} collective-permute-done((f32[16,128,128]{2,1,0:T(8,128)}, f32[16,128,128]{2,1,0:T(8,128)}, u32[]{:S(2)}, u32[]{:S(2)}) %collective-permute-start.9) | collective-permute-done | bytes 1048608 | tf_op jit(solution)/shard_map/ppermute | solution.py:17
  98.2 3.9 collective-permute-start.10
  104.1 20.1 %collective-permute-done.3 = f32[16]{0:T(128)S(1)} collective-permute-done((f32[16]{0:T(128)S(1)}, f32[16]{0:T(128)S(1)}, u32[]{:S(2)}, u32[]{:S(2)}) %collective-permute-start.3) | collective-permute-done | bytes 96 | tf_op jit(solution)/shard_map/ppermute | solution.py:17
  124.2 2.4 multiply_add_fusion.6
  126.6 3.3 collective-permute-start.11
  129.9 2.7 collective-permute-start.4
  132.7 44.1 %collective-permute-done.4 = f32[16]{0:T(128)S(1)} collective-permute-done((f32[16]{0:T(128)S(1)}, f32[16]{0:T(128)S(1)}, u32[]{:S(2)}, u32[]{:S(2)}) %collective-permute-start.4) | collective-permute-done | bytes 96 | tf_op jit(solution)/shard_map/ppermute | solution.py:17
  176.8 2.4 multiply_add_fusion.5
  179.2 2.8 collective-permute-start.12
  187.1 2.3 collective-permute-start.5
  189.4 35.1 %collective-permute-done.5 = f32[16]{0:T(128)S(1)} collective-permute-done((f32[16]{0:T(128)S(1)}, f32[16]{0:T(128)S(1)}, u32[]{:S(2)}, u32[]{:S(2)}) %collective-permute-start.5) | collective-permute-done | bytes 96 | tf_op jit(solution)/shard_map/ppermute | solution.py:17
  228.1 6.5 %psum.14 = f32[256]{0:T(256)S(1)} all-reduce(f32[256]{0:T(256)S(1)} %get-tuple-element.133), channel_id=1, replica_groups=mesh['seq'=64,'head'=4] {'head'}, use_global_device_ids=true, to_apply=%region_3.4 | all-reduce | flops 256 | bytes 2048 | tf_op jit(solution)/shard_map/psum | solution.py:112
  236.6 2.4 multiply_reduce_fusion
  239.0 8.5 %psum.15 = f32[256]{0:T(256)S(1)} all-reduce(f32[256]{0:T(256)S(1)} %multiply_reduce_fusion), channel_id=1, replica_groups=mesh['seq'=64,'head'=4] {'head'}, use_global_device_ids=true, to_apply=%region_5.6 | all-reduce | flops 256 | bytes 2048 | tf_op jit(solution)/shard_map/psum | solution.py:115
  247.4 4.6 fusion.3
  254.1 8.3 %collective-permute-start.19 = (f32[16,128,128]{2,1,0:T(8,128)S(1)}, f32[16,128,128]{2,1,0:T(8,128)}, u32[]{:S(2)}, u32[]{:S(2)}) collective-permute-start(f32[16,128,128]{2,1,0:T(8,128)S(1)} %convolution_add_fusion), channel_id=1, source_target_pairs={{4,0},{8,4},{12,8},{16,12},{20,16},{24,20},{28,24},{32,28},{36,32}... | collective-permute-start | bytes 3145736 | tf_op jit(solution)/shard_map/ppermute | solution.py:17
  262.4 14.3 %collective-permute-done.19 = f32[16,128,128]{2,1,0:T(8,128)} collective-permute-done((f32[16,128,128]{2,1,0:T(8,128)S(1)}, f32[16,128,128]{2,1,0:T(8,128)}, u32[]{:S(2)}, u32[]{:S(2)}) %collective-permute-start.19) | collective-permute-done | bytes 1048608 | tf_op jit(solution)/shard_map/ppermute | solution.py:17
  280.6 12.6 %collective-permute-done.13 = f32[16]{0:T(128)S(1)} collective-permute-done((f32[16]{0:T(128)S(1)}, f32[16]{0:T(128)S(1)}, u32[]{:S(2)}, u32[]{:S(2)}) %collective-permute-start.13) | collective-permute-done | bytes 96 | tf_op jit(solution)/shard_map/ppermute | solution.py:17
  293.2 2.7 multiply_add_fusion.4
  297.8 2.3 collective-permute-start.14
  300.1 20.4 %collective-permute-done.14 = f32[16]{0:T(128)S(1)} collective-permute-done((f32[16]{0:T(128)S(1)}, f32[16]{0:T(128)S(1)}, u32[]{:S(2)}, u32[]{:S(2)}) %collective-permute-start.14) | collective-permute-done | bytes 96 | tf_op jit(solution)/shard_map/ppermute | solution.py:17
  321.6 2.7 multiply_add_fusion.3
  324.3 4.9 collective-permute-start.22
  329.2 5.0 collective-permute-start.15
  334.1 19.6 %collective-permute-done.15 = f32[16]{0:T(128)S(1)} collective-permute-done((f32[16]{0:T(128)S(1)}, f32[16]{0:T(128)S(1)}, u32[]{:S(2)}, u32[]{:S(2)}) %collective-permute-start.15) | collective-permute-done | bytes 96 | tf_op jit(solution)/shard_map/ppermute | solution.py:17
  353.8 2.7 multiply_add_fusion.2
  356.5 4.4 collective-permute-start.23
  360.9 2.5 collective-permute-start.16
  363.4 19.5 %collective-permute-done.16 = f32[16]{0:T(128)S(1)} collective-permute-done((f32[16]{0:T(128)S(1)}, f32[16]{0:T(128)S(1)}, u32[]{:S(2)}, u32[]{:S(2)}) %collective-permute-start.16) | collective-permute-done | bytes 96 | tf_op jit(solution)/shard_map/ppermute | solution.py:17
  382.9 3.5 collective-permute-start.17
  386.4 2.7 multiply_add_fusion.1
  392.9 71.3 %collective-permute-done.18 = f32[16]{0:T(128)S(1)} collective-permute-done((f32[16]{0:T(128)S(1)}, f32[16]{0:T(128)S(1)}, u32[]{:S(2)}, u32[]{:S(2)}) %collective-permute-start.18) | collective-permute-done | bytes 96 | tf_op jit(solution)/shard_map/ppermute | solution.py:17
  467.0 2.7 multiply_add_fusion
  472.7 2.3 copy.78
  478.9 43.5 %collective-permute-done.25 = f32[16,128,128]{2,1,0:T(8,128)} collective-permute-done((f32[16,128,128]{2,1,0:T(8,128)}, f32[16,128,128]{2,1,0:T(8,128)}, u32[]{:S(2)}, u32[]{:S(2)}) %collective-permute-start.25) | collective-permute-done | bytes 1048608 | tf_op jit(solution)/shard_map/ppermute | solution.py:17
  525.6 2.4 copy.80
  528.0 2.5 fusion.7
  530.5 2.3 copy.79
  (95 shorter events, 49.2 us)
Async XLA Ops:
  0.6 3.5 copy-start
  4.1 179.4 %copy-start.3 = (bf16[256,2048]{0,1:T(8,128)(2,1)}, bf16[256,2048]{0,1:T(8,128)(2,1)S(1)}, u32[]{:S(2)}) copy-start(bf16[256,2048]{0,1:T(8,128)(2,1)S(1)} %copy.60) | copy-start | bytes 3145732
  4.5 15.2 %collective-permute-start.6 = (f32[16,128,128]{2,1,0:T(8,128)S(1)}, f32[16,128,128]{2,1,0:T(8,128)S(1)}, u32[]{:S(2)}, u32[]{:S(2)}) collective-permute-start(f32[16,128,128]{2,1,0:T(8,128)S(1)} %convolution_add_fusion.1), channel_id=1, source_target_pairs={{0,4},{4,8},{8,12},{12,16},{16,20},{20,24},{24,28},{28,32},{32,36}... | collective-permute-start | bytes 3145736 | tf_op jit(solution)/shard_map/ppermute | solution.py:17
  19.7 16.2 %copy-start.14 = (f32[16,128,128]{2,1,0:T(8,128)}, f32[16,128,128]{2,1,0:T(8,128)S(1)}, u32[]{:S(2)}) copy-start(f32[16,128,128]{2,1,0:T(8,128)S(1)} %collective-permute-done.6) | copy-start | bytes 3145732
  19.7 16.2 %collective-permute-start.7 = (f32[16,128,128]{2,1,0:T(8,128)S(1)}, f32[16,128,128]{2,1,0:T(8,128)}, u32[]{:S(2)}, u32[]{:S(2)}) collective-permute-start(f32[16,128,128]{2,1,0:T(8,128)S(1)} %collective-permute-done.6), channel_id=1, source_target_pairs={{0,4},{4,8},{8,12},{12,16},{16,20},{20,24},{24,28},{28,32},{32,36}... | collective-permute-start | bytes 3145736 | tf_op jit(solution)/shard_map/ppermute | solution.py:17
  24.1 11.8 %collective-permute-start = (f32[16]{0:T(128)S(1)}, f32[16]{0:T(128)S(1)}, u32[]{:S(2)}, u32[]{:S(2)}) collective-permute-start(f32[16]{0:T(128)S(1)} %get-tuple-element.131), channel_id=1, source_target_pairs={{0,4},{4,8},{8,12},{12,16},{16,20},{20,24},{24,28},{28,32},{32,36}... | collective-permute-start | bytes 200 | tf_op jit(solution)/shard_map/ppermute | solution.py:17
  37.6 28.0 %collective-permute-start.8 = (f32[16,128,128]{2,1,0:T(8,128)S(1)}, f32[16,128,128]{2,1,0:T(8,128)}, u32[]{:S(2)}, u32[]{:S(2)}) collective-permute-start(f32[16,128,128]{2,1,0:T(8,128)S(1)} %multiply_add_fusion.9), channel_id=1, source_target_pairs={{0,8},{4,12},{8,16},{12,20},{16,24},{20,28},{24,32},{28,36},{32,40... | collective-permute-start | bytes 3145736 | tf_op jit(solution)/shard_map/ppermute | solution.py:17
  42.9 22.7 %collective-permute-start.1 = (f32[16]{0:T(128)S(1)}, f32[16]{0:T(128)S(1)}, u32[]{:S(2)}, u32[]{:S(2)}) collective-permute-start(f32[16]{0:T(128)S(1)} %broadcast_select_fusion.6), channel_id=1, source_target_pairs={{0,4},{4,8},{8,12},{12,16},{16,20},{20,24},{24,28},{28,32},{32,36}... | collective-permute-start | bytes 200 | tf_op jit(solution)/shard_map/ppermute | solution.py:17
  68.0 28.4 %collective-permute-start.9 = (f32[16,128,128]{2,1,0:T(8,128)}, f32[16,128,128]{2,1,0:T(8,128)}, u32[]{:S(2)}, u32[]{:S(2)}) collective-permute-start(f32[16,128,128]{2,1,0:T(8,128)} %multiply_add_fusion.8), channel_id=1, source_target_pairs={{0,16},{4,20},{8,24},{12,28},{16,32},{20,36},{24,40},{28,44},{32,4... | collective-permute-start | bytes 3145736 | tf_op jit(solution)/shard_map/ppermute | solution.py:17
  69.9 6.4 %collective-permute-start.2 = (f32[16]{0:T(128)S(1)}, f32[16]{0:T(128)S(1)}, u32[]{:S(2)}, u32[]{:S(2)}) collective-permute-start(f32[16]{0:T(128)S(1)} %fusion.26), channel_id=1, source_target_pairs={{0,8},{4,12},{8,16},{12,20},{16,24},{20,28},{24,32},{28,36},{32,40... | collective-permute-start | bytes 200 | tf_op jit(solution)/shard_map/ppermute | solution.py:17
  98.2 26.1 %collective-permute-start.10 = (f32[16,128,128]{2,1,0:T(8,128)S(1)}, f32[16,128,128]{2,1,0:T(8,128)}, u32[]{:S(2)}, u32[]{:S(2)}) collective-permute-start(f32[16,128,128]{2,1,0:T(8,128)S(1)} %multiply_add_fusion.7), channel_id=1, source_target_pairs={{0,32},{4,36},{8,40},{12,44},{16,48},{20,52},{24,56},{28,60},{32,6... | collective-permute-start | bytes 3145736 | tf_op jit(solution)/shard_map/ppermute | solution.py:17
  102.1 22.1 %collective-permute-start.3 = (f32[16]{0:T(128)S(1)}, f32[16]{0:T(128)S(1)}, u32[]{:S(2)}, u32[]{:S(2)}) collective-permute-start(f32[16]{0:T(128)S(1)} %fusion.25), channel_id=1, source_target_pairs={{0,16},{4,20},{8,24},{12,28},{16,32},{20,36},{24,40},{28,44},{32,4... | collective-permute-start | bytes 200 | tf_op jit(solution)/shard_map/ppermute | solution.py:17
  126.6 50.2 %collective-permute-start.11 = (f32[16,128,128]{2,1,0:T(8,128)}, f32[16,128,128]{2,1,0:T(8,128)S(1)}, u32[]{:S(2)}, u32[]{:S(2)}) collective-permute-start(f32[16,128,128]{2,1,0:T(8,128)} %multiply_add_fusion.6), channel_id=1, source_target_pairs={{0,64},{4,68},{8,72},{12,76},{16,80},{20,84},{24,88},{28,92},{32,9... | collective-permute-start | bytes 3145736 | tf_op jit(solution)/shard_map/ppermute | solution.py:17
  129.9 46.9 %collective-permute-start.4 = (f32[16]{0:T(128)S(1)}, f32[16]{0:T(128)S(1)}, u32[]{:S(2)}, u32[]{:S(2)}) collective-permute-start(f32[16]{0:T(128)S(1)} %fusion.24), channel_id=1, source_target_pairs={{0,32},{4,36},{8,40},{12,44},{16,48},{20,52},{24,56},{28,60},{32,6... | collective-permute-start | bytes 200 | tf_op jit(solution)/shard_map/ppermute | solution.py:17
  179.2 45.3 %collective-permute-start.12 = (f32[16,128,128]{2,1,0:T(8,128)}, f32[16,128,128]{2,1,0:T(8,128)}, u32[]{:S(2)}, u32[]{:S(2)}) collective-permute-start(f32[16,128,128]{2,1,0:T(8,128)} %multiply_add_fusion.5), channel_id=1, source_target_pairs={{0,128},{4,132},{8,136},{12,140},{16,144},{20,148},{24,152},{28,15... | collective-permute-start | bytes 3145736 | tf_op jit(solution)/shard_map/ppermute | solution.py:17
  183.4 42.8 %copy-start.1 = (bf16[256,2048]{0,1:T(8,128)(2,1)}, bf16[256,2048]{0,1:T(8,128)(2,1)S(1)}, u32[]{:S(2)}) copy-start(bf16[256,2048]{0,1:T(8,128)(2,1)S(1)} %copy.59) | copy-start | bytes 3145732
  184.9 2.2 copy-start.7
  187.1 37.4 %collective-permute-start.5 = (f32[16]{0:T(128)S(1)}, f32[16]{0:T(128)S(1)}, u32[]{:S(2)}, u32[]{:S(2)}) collective-permute-start(f32[16]{0:T(128)S(1)} %fusion.23), channel_id=1, source_target_pairs={{0,64},{4,68},{8,72},{12,76},{16,80},{20,84},{24,88},{28,92},{32,9... | collective-permute-start | bytes 200 | tf_op jit(solution)/shard_map/ppermute | solution.py:17
  189.4 36.8 %copy-start.6 = (f32[16,256,128]{1,2,0:T(8,128)S(1)}, f32[16,256,128]{1,2,0:T(8,128)}, u32[]{:S(2)}) copy-start(f32[16,256,128]{1,2,0:T(8,128)} %fusion.11) | copy-start | bytes 6291460
  226.2 1.9 copy-start.11
  234.6 1.9 copy-start.15
  252.1 1.6 copy-start.2
  254.1 22.6 %collective-permute-start.19 = (f32[16,128,128]{2,1,0:T(8,128)S(1)}, f32[16,128,128]{2,1,0:T(8,128)}, u32[]{:S(2)}, u32[]{:S(2)}) collective-permute-start(f32[16,128,128]{2,1,0:T(8,128)S(1)} %convolution_add_fusion), channel_id=1, source_target_pairs={{4,0},{8,4},{12,8},{16,12},{20,16},{24,20},{28,24},{32,28},{36,32}... | collective-permute-start | bytes 3145736 | tf_op jit(solution)/shard_map/ppermute | solution.py:17
  276.7 16.4 %collective-permute-start.20 = (f32[16,128,128]{2,1,0:T(8,128)}, f32[16,128,128]{2,1,0:T(8,128)}, u32[]{:S(2)}, u32[]{:S(2)}) collective-permute-start(f32[16,128,128]{2,1,0:T(8,128)} %collective-permute-done.19), channel_id=1, source_target_pairs={{4,0},{8,4},{12,8},{16,12},{20,16},{24,20},{28,24},{32,28},{36,32}... | collective-permute-start | bytes 3145736 | tf_op jit(solution)/shard_map/ppermute | solution.py:17
  278.6 14.5 %collective-permute-start.13 = (f32[16]{0:T(128)S(1)}, f32[16]{0:T(128)S(1)}, u32[]{:S(2)}, u32[]{:S(2)}) collective-permute-start(f32[16]{0:T(128)S(1)} %get-tuple-element.131), channel_id=1, source_target_pairs={{4,0},{8,4},{12,8},{16,12},{20,16},{24,20},{28,24},{32,28},{36,32}... | collective-permute-start | bytes 200 | tf_op jit(solution)/shard_map/ppermute | solution.py:17
  295.8 25.8 %collective-permute-start.21 = (f32[16,128,128]{2,1,0:T(8,128)}, f32[16,128,128]{2,1,0:T(8,128)}, u32[]{:S(2)}, u32[]{:S(2)}) collective-permute-start(f32[16,128,128]{2,1,0:T(8,128)} %multiply_add_fusion.4), channel_id=1, source_target_pairs={{8,0},{12,4},{16,8},{20,12},{24,16},{28,20},{32,24},{36,28},{40,32... | collective-permute-start | bytes 3145736 | tf_op jit(solution)/shard_map/ppermute | solution.py:17
  297.8 22.8 %collective-permute-start.14 = (f32[16]{0:T(128)S(1)}, f32[16]{0:T(128)S(1)}, u32[]{:S(2)}, u32[]{:S(2)}) collective-permute-start(f32[16]{0:T(128)S(1)} %broadcast_select_fusion), channel_id=1, source_target_pairs={{4,0},{8,4},{12,8},{16,12},{20,16},{24,20},{28,24},{32,28},{36,32}... | collective-permute-start | bytes 200 | tf_op jit(solution)/shard_map/ppermute | solution.py:17
  324.3 29.5 %collective-permute-start.22 = (f32[16,128,128]{2,1,0:T(8,128)}, f32[16,128,128]{2,1,0:T(8,128)}, u32[]{:S(2)}, u32[]{:S(2)}) collective-permute-start(f32[16,128,128]{2,1,0:T(8,128)} %multiply_add_fusion.3), channel_id=1, source_target_pairs={{16,0},{20,4},{24,8},{28,12},{32,16},{36,20},{40,24},{44,28},{48,3... | collective-permute-start | bytes 3145736 | tf_op jit(solution)/shard_map/ppermute | solution.py:17
  329.2 24.6 %collective-permute-start.15 = (f32[16]{0:T(128)S(1)}, f32[16]{0:T(128)S(1)}, u32[]{:S(2)}, u32[]{:S(2)}) collective-permute-start(f32[16]{0:T(128)S(1)} %fusion.31), channel_id=1, source_target_pairs={{8,0},{12,4},{16,8},{20,12},{24,16},{28,20},{32,24},{36,28},{40,32... | collective-permute-start | bytes 200 | tf_op jit(solution)/shard_map/ppermute | solution.py:17
  356.5 29.9 %collective-permute-start.23 = (f32[16,128,128]{2,1,0:T(8,128)}, f32[16,128,128]{2,1,0:T(8,128)}, u32[]{:S(2)}, u32[]{:S(2)}) collective-permute-start(f32[16,128,128]{2,1,0:T(8,128)} %multiply_add_fusion.2), channel_id=1, source_target_pairs={{32,0},{36,4},{40,8},{44,12},{48,16},{52,20},{56,24},{60,28},{64,3... | collective-permute-start | bytes 3145736 | tf_op jit(solution)/shard_map/ppermute | solution.py:17
  360.9 22.0 %collective-permute-start.16 = (f32[16]{0:T(128)S(1)}, f32[16]{0:T(128)S(1)}, u32[]{:S(2)}, u32[]{:S(2)}) collective-permute-start(f32[16]{0:T(128)S(1)} %fusion.30), channel_id=1, source_target_pairs={{16,0},{20,4},{24,8},{28,12},{32,16},{36,20},{40,24},{44,28},{48,3... | collective-permute-start | bytes 200 | tf_op jit(solution)/shard_map/ppermute | solution.py:17
  382.9 8.1 %collective-permute-start.17 = (f32[16]{0:T(128)S(1)}, f32[16]{0:T(128)S(1)}, u32[]{:S(2)}, u32[]{:S(2)}) collective-permute-start(f32[16]{0:T(128)S(1)} %fusion.29), channel_id=1, source_target_pairs={{32,0},{36,4},{40,8},{44,12},{48,16},{52,20},{56,24},{60,28},{64,3... | collective-permute-start | bytes 200 | tf_op jit(solution)/shard_map/ppermute | solution.py:17
  389.0 78.0 %collective-permute-start.24 = (f32[16,128,128]{2,1,0:T(8,128)}, f32[16,128,128]{2,1,0:T(8,128)}, u32[]{:S(2)}, u32[]{:S(2)}) collective-permute-start(f32[16,128,128]{2,1,0:T(8,128)} %multiply_add_fusion.1), channel_id=1, source_target_pairs={{64,0},{68,4},{72,8},{76,12},{80,16},{84,20},{88,24},{92,28},{96,3... | collective-permute-start | bytes 3145736 | tf_op jit(solution)/shard_map/ppermute | solution.py:17
  391.0 73.3 %collective-permute-start.18 = (f32[16]{0:T(128)S(1)}, f32[16]{0:T(128)S(1)}, u32[]{:S(2)}, u32[]{:S(2)}) collective-permute-start(f32[16]{0:T(128)S(1)} %fusion.28), channel_id=1, source_target_pairs={{64,0},{68,4},{72,8},{76,12},{80,16},{84,20},{88,24},{92,28},{96,3... | collective-permute-start | bytes 200 | tf_op jit(solution)/shard_map/ppermute | solution.py:17
  464.3 1.4 copy-start.4
  465.7 1.3 copy-start.8
  467.0 4.2 copy-start.12
  469.8 52.6 %collective-permute-start.25 = (f32[16,128,128]{2,1,0:T(8,128)}, f32[16,128,128]{2,1,0:T(8,128)}, u32[]{:S(2)}, u32[]{:S(2)}) collective-permute-start(f32[16,128,128]{2,1,0:T(8,128)} %multiply_add_fusion), channel_id=1, source_target_pairs={{128,0},{132,4},{136,8},{140,12},{144,16},{148,20},{152,24},{156,2... | collective-permute-start | bytes 3145736 | tf_op jit(solution)/shard_map/ppermute | solution.py:17
  474.9 2.2 copy-start.9
  478.9 45.2 %copy-start.5 = (bf16[256,2048]{0,1:T(8,128)(2,1)S(1)}, bf16[256,2048]{0,1:T(8,128)(2,1)}, u32[]{:S(2)}) copy-start(bf16[256,2048]{0,1:T(8,128)(2,1)} %copy-done.3) | copy-start | bytes 3145732
  524.1 1.5 copy-start.13
  525.6 2.4 copy-start.10
where the time goes:
time: 534 us; the launch traced here: 533 us
  waiting for transfers between devices  362 us (68%)
  starting transfers between devices  86.6 us (16%)
  other arithmetic  35.3 us (7%)
  matrix products  17.9 us (3%)
  local copies, waits for them, and re-layouts  15.1 us (3%)
  blocking collectives  15 us (3%)
    ppermute x26, waiting for transfers between devices, shifted(): return lax.ppermute(array, axis, pairs)  362 us
    ppermute x26, starting transfers between devices, shifted(): return lax.ppermute(array, axis, pairs)  86.6 us
    add x10, other arithmetic, doubling(): state_part = decay_part[:, None, None] * far_state + state_part  24 us
  transfers between devices with their start and end apart: 26, of which 16 were waited for; matrix products, arithmetic and copies ran while one was open for 3% of the time, Pallas kernels for 0%

commit v1 on v0

v1 whole, which is shorter than its diff:
```python
import functools

import jax
import jax.numpy as jnp
from jax import lax
from jax.experimental import pallas as pl
from jax.experimental.pallas import tpu as pltpu
from jax.sharding import Mesh, PartitionSpec as P

DH = 128
GROUP = 256
HALF = 8
WIDE = HALF * DH
FEATURES = 64 * DH
EPSILON = 1e-06
F32 = jnp.float32
BF16 = jnp.bfloat16
PLANE = ("z0", "y")
VMEM = pl.BlockSpec(memory_space=pltpu.VMEM)
SMEM = pl.BlockSpec(memory_space=pltpu.SMEM)


def call(kernel, out, *args, flops=0, smem=1, limit=12, name=None):
    moved = sum(a.size * a.dtype.itemsize for a in args)
    moved += sum(o.size * o.dtype.itemsize for o in jax.tree.leaves(out))
    return pl.pallas_call(
        kernel,
        out_shape=out,
        in_specs=[SMEM] * smem + [VMEM] * (len(args) - smem),
        out_specs=jax.tree.map(lambda _: VMEM, out),
        compiler_params=pltpu.CompilerParams(vmem_limit_bytes=limit << 20),
        cost_estimate=pl.CostEstimate(flops=flops, bytes_accessed=moved, transcendentals=0),
        name=name,
    )(*args)


def shape(*dims, dtype=F32):
    return jax.ShapeDtypeStruct(dims, dtype)


def dot(a, b, ca, cb, precision=None):
    return lax.dot_general(
        a, b, (((ca,), (cb,)), ((), ())), precision=precision, preferred_element_type=F32
    )


def columns(role, core, i):
    side = core if role == 0 else 1 - core
    return pl.ds(pl.multiple_of(side * WIDE + i * DH, DH), DH)


def lanes(tab, which, role, i):
    at = which * 16 + role * HALF + i
    return tab[:, at : at + 1]


def tables(core, decays):
    rows = lax.broadcasted_iota(jnp.int32, (GROUP, GROUP), 0)
    cols = lax.broadcasted_iota(jnp.int32, (GROUP, GROUP), 1)
    tri = (rows >= cols).astype(F32)
    down = dot(tri, decays, 1, 0, lax.Precision.HIGHEST)
    across = dot(decays, tri, 0, 1, lax.Precision.HIGHEST)
    swapped = jnp.concatenate([down[:, HALF:], down[:, :HALF]], axis=1)
    down = jnp.where(core == 0, down, swapped)
    across = jnp.where(core == 0, across, jnp.concatenate([across[HALF:], across[:HALF]], axis=0))
    return down, across


def state_term(core, role, i, keys_ref, value_ref, tab):
    at = columns(role, core, i)
    keyed = (keys_ref[:, at].astype(F32) * lanes(tab, 2, role, i)).astype(BF16)
    return dot(keyed, value_ref[:, at], 0, 0)


def first_kernel(core_ref, keys_ref, value_ref, decay_ref, tab_ref, across_ref, send_ref):
    core = core_ref[0]
    down, across = tables(core, decay_ref[...])
    last = down[GROUP - 1 :, :]
    blank = jnp.zeros((GROUP, 128 - 48), F32)
    tab = jnp.concatenate([down, jnp.exp(down), jnp.exp(last - down), blank], axis=1)
    tab_ref[...] = tab
    across_ref[...] = across
    for i in range(HALF):
        send_ref[i * DH : (i + 1) * DH, :] = state_term(core, 1, i, keys_ref, value_ref, tab)
    send_ref[WIDE:, :] = jnp.broadcast_to(tab[GROUP - 1 :, :], (8, 128))


def second_kernel(core_ref, keys_ref, value_ref, tab_ref, keep_ref):
    core = core_ref[0]
    tab = tab_ref[...]
    for i in range(HALF):
        keep_ref[i * DH : (i + 1) * DH, :] = state_term(core, 0, i, keys_ref, value_ref, tab)


def merge_forward(core_ref, own_ref, other_ref, tab_ref, out_ref, dec_ref):
    zero = core_ref[0] == 0
    mine = tab_ref[GROUP - 1 :, :HALF]
    theirs = other_ref[WIDE : WIDE + 1, HALF : 2 * HALF]
    last_a = jnp.where(zero, mine, theirs)
    last_b = jnp.where(zero, theirs, mine)
    for i in range(HALF):
        own = own_ref[i * DH : (i + 1) * DH, :]
        other = other_ref[i * DH : (i + 1) * DH, :]
        a, b = jnp.where(zero, own, other), jnp.where(zero, other, own)
        here_a = jnp.broadcast_to(last_a[:, i : i + 1], (1, 128))
        here_b = jnp.broadcast_to(last_b[:, i : i + 1], (1, 128))
        dec_ref[i : i + 1, :] = jnp.exp(here_a)
        dec_ref[HALF + i : HALF + i + 1, :] = jnp.exp(here_b)
        out_ref[i, :DH, :] = jnp.exp(here_b) * a + b
        out_ref[i, DH:, :] = jnp.broadcast_to(here_a + here_b, (8, 128))


def merge_backward(core_ref, own_ref, other_ref, dec_ref, out_ref):
    zero = core_ref[0] == 0
    for i in range(HALF):
        own = own_ref[i * DH : (i + 1) * DH, :]
        other = other_ref[i * DH : (i + 1) * DH, :]
        a, b = jnp.where(zero, own, other), jnp.where(zero, other, own)
        out_ref[i] = a + dec_ref[i : i + 1, :] * b


def total_kernel(reverse, parts_ref, decays_ref, out_ref):
    order = list(range(8))[:: -1 if reverse else 1]
    total = parts_ref[order[0], :DH, :]
    for at in order[1:]:
        total = jnp.exp(decays_ref[at, DH : DH + 1, :]) * total + parts_ref[at, :DH, :]
    out_ref[:DH, :] = total
    decay = decays_ref[0, DH:, :]
    for at in range(1, 8):
        decay = decay + decays_ref[at, DH:, :]
    out_ref[DH:, :] = decay


def enter_kernel(reverse, parts_ref, decays_ref, near_ref, mid_ref, far_ref, out_ref):
    state = far_ref[:DH, :]
    for ref in (mid_ref, near_ref):
        state = jnp.exp(ref[DH : DH + 1, :]) * state + ref[:DH, :]
    order = list(range(8))[:: -1 if reverse else 1]
    for at in order:
        out_ref[at] = state
        if at != order[-1]:
            state = jnp.exp(decays_ref[at, DH : DH + 1, :]) * state + parts_ref[at, :DH, :]


def leave_kernel(reverse, core_ref, enter_ref, own_ref, other_ref, dec_ref, keep_ref, send_ref):
    first = core_ref[0] == (1 if reverse else 0)
    base = HALF if reverse else 0
    for i in range(HALF):
        own = own_ref[i * DH : (i + 1) * DH, :]
        other = other_ref[i * DH : (i + 1) * DH, :]
        nearer = jnp.where(first, own, other)
        x = enter_ref[i]
        y = dec_ref[base + i : base + i + 1, :] * x + nearer
        keep_ref[i] = jnp.where(first, x, y)
        send_ref[i] = jnp.where(first, y, x)


def weights_of(tab, across_ref, role, i):
    rows = lax.broadcasted_iota(jnp.int32, (GROUP, GROUP), 0)
    cols = lax.broadcasted_iota(jnp.int32, (GROUP, GROUP), 1)
    at = role * HALF + i
    gaps = lanes(tab, 0, role, i) - across_ref[at : at + 1, :]
    return jnp.exp(jnp.where(rows >= cols, gaps, -jnp.inf))


def intra_kernel(
    role, core_ref, query_ref, keys_ref, value_ref, gate_ref, gain_ref, mixed_ref, tab_ref, across_ref,
    intra_ref, normed_ref,
):
    core = core_ref[0]
    tab = tab_ref[...]
    for i in range(HALF):
        at = columns(role, core, i)
        to = slice(i * DH, (i + 1) * DH)
        scores = dot(query_ref[:, at], keys_ref[:, at], 1, 1)
        probs = (scores * weights_of(tab, across_ref, role, i)).astype(BF16)
        intra_ref[:, to] = dot(probs, value_ref[:, at], 1, 0)
        opening = jax.nn.sigmoid(gate_ref[:, at].astype(F32))
        normed_ref[:, to] = mixed_ref[:, at].astype(F32) * opening * gain_ref[:, at]


def attend_kernel(role, core_ref, query_ref, state_ref, intra_ref, normed_ref, tab_ref, sums_ref, out_ref, add_ref):
    core = core_ref[0]
    tab = tab_ref[...]
    squares = jnp.zeros((GROUP, DH), F32)
    products = jnp.zeros((GROUP, DH), F32)
    for i in range(HALF):
        at = columns(role, core, i)
        to = slice(i * DH, (i + 1) * DH)
        inter = dot(query_ref[:, at], state_ref[i].astype(BF16), 1, 0)
        attention = intra_ref[:, to] + inter * lanes(tab, 1, role, i)
        out_ref[:, to] = attention
        squares = squares + attention * attention
        products = products + normed_ref[:, to] * attention
    ones = jnp.ones((8, DH), F32)
    squares = dot(ones, squares, 1, 1, lax.Precision.HIGHEST)
    products = dot(ones, products, 1, 1, lax.Precision.HIGHEST)
    row = lax.broadcasted_iota(jnp.int32, (8, GROUP), 0)
    both = jnp.where(row == 0, squares, products)
    add_ref[...] = both if sums_ref is None else sums_ref[...] + both


def upright(row):
    rows = lax.broadcasted_iota(jnp.int32, (GROUP, GROUP), 0)
    cols = lax.broadcasted_iota(jnp.int32, (GROUP, GROUP), 1)
    return jnp.sum(jnp.where(rows == cols, row, 0.0), axis=1, keepdims=True)


def norm_terms(sums_ref):
    scale = lax.rsqrt(sums_ref[0:1, :] / FEATURES + EPSILON)
    projection = scale * sums_ref[1:2, :] / FEATURES
    return upright(scale), upright(projection)


def grad_kernel(role, core_ref, query_ref, attention_ref, normed_ref, tab_ref, sums_ref, grad_ref, term_ref):
    core = core_ref[0]
    tab = tab_ref[...]
    scale, projection = norm_terms(sums_ref)
    for i in range(HALF):
        at = columns(role, core, i)
        to = slice(i * DH, (i + 1) * DH)
        normed = attention_ref[:, to] * scale
        grad = (scale * (normed_ref[:, to] - normed * projection)).astype(BF16)
        grad_ref[:, to] = grad
        weighted = (query_ref[:, at].astype(F32) * lanes(tab, 1, role, i)).astype(BF16)
        term_ref[i * DH : (i + 1) * DH, :] = dot(weighted, grad, 0, 0)


def inner_kernel(
    role, core_ref, query_ref, keys_ref, value_ref, state_ref, grad_ref, tab_ref, across_ref,
    query_out, keys_out, value_out,
):
    core = core_ref[0]
    tab = tab_ref[...]
    for i in range(HALF):
        at = columns(role, core, i)
        to = slice(i * DH, (i + 1) * DH)
        query, keys, value, grad = query_ref[:, at], keys_ref[:, at], value_ref[:, at], grad_ref[:, to]
        weights = weights_of(tab, across_ref, role, i)
        probs = (dot(query, keys, 1, 1) * weights).astype(BF16)
        grad_scores = (dot(grad, value, 1, 1) * weights).astype(BF16)
        grad_query = dot(grad_scores, keys, 1, 0)
        grad_query = grad_query + dot(grad, state_ref[i].astype(BF16), 1, 1) * lanes(tab, 1, role, i)
        query_out[:, to] = grad_query.astype(BF16)
        keys_out[:, to] = dot(grad_scores, query, 0, 0)
        value_out[:, to] = dot(probs, grad, 0, 0)


def gate_kernel(
    core_ref, gate_ref, gain_ref, upstream_ref, own_ref, other_ref, own_query, other_query, sums_ref,
    mixed_out, gate_out, query_out,
):
    core = core_ref[0]
    scale, _ = norm_terms(sums_ref)
    for role, ref, grad_query in ((0, own_ref, own_query), (1, other_ref, other_query)):
        for i in range(HALF):
            at = columns(role, core, i)
            to = slice(i * DH, (i + 1) * DH)
            shaped = ref[:, to] * scale * gain_ref[:, at]
            opening = jax.nn.sigmoid(gate_ref[:, at].astype(F32))
            mixed_out[:, at] = (shaped * opening).astype(BF16)
            upstream = upstream_ref[:, at].astype(F32)
            gate_out[:, at] = (upstream * shaped * opening * (1.0 - opening)).astype(BF16)
            query_out[:, at] = grad_query[:, to]


def last_kernel(
    core_ref, keys_ref, value_ref, own_state, other_state, own_keys, other_keys, own_value, other_value, tab_ref,
    keys_out, value_out,
):
    core = core_ref[0]
    tab = tab_ref[...]
    parts = ((0, own_state, own_keys, own_value), (1, other_state, other_keys, other_value))
    for role, state_ref, part_keys, part_value in parts:
        for i in range(HALF):
            at = columns(role, core, i)
            to = slice(i * DH, (i + 1) * DH)
            state = state_ref[i].astype(BF16)
            toward_end = lanes(tab, 2, role, i)
            grad_keys = part_keys[:, to] + dot(value_ref[:, at], state, 1, 1) * toward_end
            grad_value = part_value[:, to] + dot(keys_ref[:, at], state, 1, 0) * toward_end
            keys_out[:, at] = grad_keys.astype(BF16)
            value_out[:, at] = grad_value.astype(BF16)


def swap(array):
    return lax.ppermute(array, "core", [(0, 1), (1, 0)])


def shifted(array, by):
    return lax.ppermute(array, "z1", [(i, i + by) for i in range(4) if 0 <= i + by < 4])


def spread(array):
    return lax.all_to_all(array, PLANE, 0, 0, tiled=True)


def across_heads(array):
    for flip in (1, 3):
        array = array + lax.ppermute(array, "head", [(i, i ^ flip) for i in range(4)])
    return array


def scan(core, own, other, tab, dec, decays, reverse):
    if reverse:
        totals = call(merge_backward, shape(HALF, DH, DH), core, own, other, dec, name="merge_b")
    else:
        totals, dec = call(
            merge_forward, (shape(HALF, DH + 8, DH), shape(2 * HALF, DH)), core, own, other, tab, name="merge_f"
        )
    parts = spread(totals)
    decays = parts if decays is None else decays
    row = call(
        functools.partial(total_kernel, reverse), shape(DH + 8, DH), parts, decays, smem=0, name="row_total"
    )
    step = -1 if reverse else 1
    near, mid, far = (shifted(row, step * by) for by in (1, 2, 3))
    entering = call(
        functools.partial(enter_kernel, reverse), shape(8, DH, DH), parts, decays, near, mid, far, smem=0, name="enter"
    )
    entering = spread(entering)
    keep, send = call(
        functools.partial(leave_kernel, reverse),
        (shape(HALF, DH, DH), shape(HALF, DH, DH)),
        core, entering, own, other, dec, name="leave",
    )
    return keep, swap(send), dec, decays


def on_device(query, keys, value, gate, decay, gain, upstream):
    core = lax.axis_index("core").astype(jnp.int32).reshape(1)
    gain = gain.reshape(1, -1)
    big = 2 * GROUP * GROUP * DH * HALF
    small = big // 2

    tab, across, send = call(
        first_kernel,
        (shape(GROUP, 128), shape(16, GROUP), shape(WIDE + 8, DH)),
        core, keys, value, decay, flops=small, name="first",
    )
    other = swap(send)
    own = call(second_kernel, shape(WIDE, DH), core, keys, value, tab, flops=small, name="second")

    wide = shape(GROUP, WIDE)
    intra = [
        call(
            functools.partial(intra_kernel, role), (wide, wide),
            core, query, keys, value, gate, gain, upstream, tab, across, flops=2 * big, name=f"intra{role}",
        )
        for role in (0, 1)
    ]

    state_own, state_other, dec, decays = scan(core, own, other, tab, None, None, False)

    def attend_first(core_ref, query_ref, state_ref, intra_ref, normed_ref, tab_ref, out_ref, add_ref):
        attend_kernel(0, core_ref, query_ref, state_ref, intra_ref, normed_ref, tab_ref, None, out_ref, add_ref)

    sums_shape = shape(8, GROUP)
    att_own, sums = call(
        attend_first, (wide, sums_shape), core, query, state_own, *intra[0], tab, flops=small, name="attend0"
    )
    att_other, sums = call(
        functools.partial(attend_kernel, 1), (wide, sums_shape),
        core, query, state_other, *intra[1], tab, sums, flops=small, name="attend1",
    )
    sums = across_heads(sums)

    grads_shape = (shape(GROUP, WIDE, dtype=BF16), shape(WIDE, DH))
    grad_other, term_send = call(
        functools.partial(grad_kernel, 1), grads_shape, core, query, att_other, intra[1][1], tab, sums,
        flops=small, name="grad1",
    )
    term_other = swap(term_send)
    grad_own, term_own = call(
        functools.partial(grad_kernel, 0), grads_shape, core, query, att_own, intra[0][1], tab, sums,
        flops=small, name="grad0",
    )

    inner = [
        call(
            functools.partial(inner_kernel, role), (shape(GROUP, WIDE, dtype=BF16), wide, wide),
            core, query, keys, value, state, grad, tab, across, flops=6 * big, name=f"inner{role}",
        )
        for role, state, grad in ((0, state_own, grad_own), (1, state_other, grad_other))
    ]
    full = shape(GROUP, 2 * WIDE, dtype=BF16)
    mixed, grad_gate, grad_query = call(
        gate_kernel, (full, full, full),
        core, gate, gain, upstream, att_own, att_other, inner[0][0], inner[1][0], sums, name="gates", limit=20,
    )

    after_own, after_other, _, _ = scan(core, term_own, term_other, tab, dec, decays, True)
    grad_keys, grad_value = call(
        last_kernel, (full, full),
        core, keys, value, after_own, after_other, inner[0][1], inner[1][1], inner[0][2], inner[1][2], tab,
        flops=4 * small, name="last", limit=20,
    )
    return mixed, grad_query, grad_keys, grad_value, grad_gate


def solution(mesh):
    levels = Mesh(mesh.devices.reshape(4, 2, 4, 2, 4), ("z1", "z0", "y", "core", "head"))
    seq = ("z1", "z0", "y", "core")
    both = P(seq, "head")
    return jax.shard_map(
        on_device,
        mesh=levels,
        in_specs=(both, both, both, both, both, P("head"), both),
        out_specs=(both,) * 5,
        check_vma=False,
    )
```

time: 534 us -> 120 us (0.22)
  the two profiles are of different devices: /device:TPU:83 before, /device:TPU:1 now
where the time goes in v1:
time: 120 us; the launch traced here: 119 us
  blocking collectives  47.3 us (39%)
  starting transfers between devices  34.8 us (29%)
  Pallas kernels  21.3 us (18%)
  waiting for transfers between devices  11.3 us (9%)
  local copies, waits for them, and re-layouts  3.29 us (3%)
    all_to_all x4, blocking collectives, spread(): return lax.all_to_all(array, PLANE, 0, 0, tiled=True)  47.3 us
    pallas_call x20, Pallas kernels, call(): pl.pallas_call(kernel, out_shape=out, in_specs=[SMEM] * smem + [VMEM] * (...  21.3 us
    ppermute x6, starting transfers between devices, shifted(): lax.ppermute(array, 'z1', [(i, i + by) for i in range(4) if 0 <= i + by <...  16.3 us
    ppermute x4, starting transfers between devices, swap(): return lax.ppermute(array, 'core', [(0, 1), (1, 0)])  14.7 us
    ppermute x6, waiting for transfers between devices, shifted(): lax.ppermute(array, 'z1', [(i, i + by) for i in range(4) if 0 <= i + by <...  7.85 us
    ppermute x2, starting transfers between devices, across_heads(): lax.ppermute(array, 'head', [(i, i ^ flip) for i in range(4)])  3.72 us
    unnamed x17, local copies, waits for them, and re-layouts  3.29 us
    ppermute x2, waiting for transfers between devices, across_heads(): lax.ppermute(array, 'head', [(i, i ^ flip) for i in range(4)])  2.52 us
  transfers between devices with their start and end apart: 12, of which 7 were waited for; matrix products, arithmetic and copies ran while one was open for 0% of the time, Pallas kernels for 12%

profile of v1, /device:TPU:1, one launch (start us, length us, event | category | flops | bytes accessed | tf_op | source)
XLA Modules:
  0.0 118.7 jit_solution(10768348567619145303)
XLA Ops:
  0.6 0.8 copy.12.decay_ref
  1.5 1.2 %copy-done.1 = bf16[256,2048]{1,0:T(8,128)(2,1)S(1)} copy-done((bf16[256,2048]{1,0:T(8,128)(2,1)S(1)}, bf16[256,2048]{1,0:T(8,128)(2,1)}, u32[]{:S(2)}) %copy-start.1) | copy-done | bytes 1048600
  2.7 1.2 %copy-done.3 = bf16[256,2048]{1,0:T(8,128)(2,1)S(1)} copy-done((bf16[256,2048]{1,0:T(8,128)(2,1)S(1)}, bf16[256,2048]{1,0:T(8,128)(2,1)}, u32[]{:S(2)}) %copy-start.3) | copy-done | bytes 1048600
  3.9 1.4 %first.1 = (f32[256,128]{1,0:T(8,128)S(1)}, f32[16,256]{1,0:T(8,128)S(1)}, f32[1032,128]{1,0:T(8,128)S(1)}) custom-call(s32[1]{0:T(128)} %bitcast.core_ref, bf16[256,2048]{1,0:T(8,128)(2,1)S(1)} %copy-done.1, bf16[256,2048]{1,0:T(8,128)(2,1)S(1)} %copy-done.3, f32[256,16]{1,0:T(8,128)S(1)} %copy.12.decay_ref), custom_call_target="tpu_custom_call" | custom-call | flops 67108864 | bytes 2789380 | tf_op jit(solution)/shard_map/first/pallas_call | solution.py:26
  5.3 3.3 %collective-permute-start = (f32[1032,128]{1,0:T(8,128)S(1)}, f32[1032,128]{1,0:T(8,128)S(1)}, u32[]{:S(2)}, u32[]{:S(2)}) collective-permute-start(f32[1032,128]{1,0:T(8,128)S(1)} %get-tuple-element.38), channel_id=1, source_target_pairs={{0,4},{4,0},{1,5},{5,1},{2,6},{6,2},{3,7},{7,3},{8,12},{12,8},{9,1... | collective-permute-start | bytes 1585160 | tf_op jit(solution)/shard_map/ppermute | solution.py:287
  8.7 0.9 second.1.own_ref
  9.6 0.6 collective-permute-done.other_ref
  10.2 0.2 merge_f.1
  10.4 13.6 %all_to_all.20.parts_ref.decays_ref = f32[8,136,128]{2,1,0:T(8,128)S(1)} all-to-all(f32[8,136,128]{2,1,0:T(8,128)S(1)} %get-tuple-element.39), channel_id=1, replica_groups=mesh['z1'=4,'z0'=2,'y'=4,'core'=2,'head'=4] {'z0','y'}, dimensions={0} | all-to-all | bytes 1114112 | tf_op jit(solution)/shard_map/all_to_all | solution.py:295
  24.1 7.2 %collective-permute-start.3 = (f32[136,128]{1,0:T(8,128)S(1)}, f32[136,128]{1,0:T(8,128)S(1)}, u32[]{:S(2)}, u32[]{:S(2)}) collective-permute-start(f32[136,128]{1,0:T(8,128)S(1)} %row_total.2), channel_id=1, source_target_pairs={{0,192},{1,193},{2,194},{3,195},{4,196},{5,197},{6,198},{7,199},{8... | collective-permute-start | bytes 208904 | tf_op jit(solution)/shard_map/ppermute | solution.py:291
  31.3 1.6 %collective-permute-start.2 = (f32[136,128]{1,0:T(8,128)S(1)}, f32[136,128]{1,0:T(8,128)S(1)}, u32[]{:S(2)}, u32[]{:S(2)}) collective-permute-start(f32[136,128]{1,0:T(8,128)S(1)} %row_total.2), channel_id=1, source_target_pairs={{0,128},{64,192},{1,129},{65,193},{2,130},{66,194},{3,131},{67,195... | collective-permute-start | bytes 208904 | tf_op jit(solution)/shard_map/ppermute | solution.py:291
  32.8 3.7 %collective-permute-start.1 = (f32[136,128]{1,0:T(8,128)S(1)}, f32[136,128]{1,0:T(8,128)S(1)}, u32[]{:S(2)}, u32[]{:S(2)}) collective-permute-start(f32[136,128]{1,0:T(8,128)S(1)} %row_total.2), channel_id=1, source_target_pairs={{0,64},{64,128},{128,192},{1,65},{65,129},{129,193},{2,66},{66,130... | collective-permute-start | bytes 208904 | tf_op jit(solution)/shard_map/ppermute | solution.py:291
  36.6 0.0 collective-permute-done.2.mid_ref
  36.6 1.3 %collective-permute-done.1.near_ref = f32[136,128]{1,0:T(8,128)S(1)} collective-permute-done((f32[136,128]{1,0:T(8,128)S(1)}, f32[136,128]{1,0:T(8,128)S(1)}, u32[]{:S(2)}, u32[]{:S(2)}) %collective-permute-start.1) | collective-permute-done | bytes 69664 | tf_op jit(solution)/shard_map/ppermute | solution.py:291
  37.9 0.1 enter.2
  38.0 0.0 copy-start.2
  38.0 11.2 %all_to_all.21.enter_ref = f32[8,128,128]{2,1,0:T(8,128)S(1)} all-to-all(f32[8,128,128]{2,1,0:T(8,128)S(1)} %enter.2), channel_id=1, replica_groups=mesh['z1'=4,'z0'=2,'y'=4,'core'=2,'head'=4] {'z0','y'}, dimensions={0} | all-to-all | bytes 1048576 | tf_op jit(solution)/shard_map/all_to_all | solution.py:295
  49.2 0.1 leave.2
  49.3 3.5 %collective-permute-start.4 = (f32[8,128,128]{2,1,0:T(8,128)S(1)}, f32[8,128,128]{2,1,0:T(8,128)S(1)}, u32[]{:S(2)}, u32[]{:S(2)}) collective-permute-start(f32[8,128,128]{2,1,0:T(8,128)S(1)} %get-tuple-element.46), channel_id=1, source_target_pairs={{0,4},{4,0},{1,5},{5,1},{2,6},{6,2},{3,7},{7,3},{8,12},{12,8},{9,1... | collective-permute-start | bytes 1572872 | tf_op jit(solution)/shard_map/ppermute | solution.py:287
  52.9 1.3 %intra1.1 = (f32[256,1024]{1,0:T(8,128)S(1)}, f32[256,1024]{1,0:T(8,128)S(1)}) custom-call(s32[1]{0:T(128)} %bitcast.core_ref, bf16[256,2048]{1,0:T(8,128)(2,1)S(1)} %copy-done, bf16[256,2048]{1,0:T(8,128)(2,1)S(1)} %copy-done.2, bf16[256,2048]{1,0:T(8,128)(2,1)S(1)} %copy-done.4, bf16[256,2048]{1,0:T(8,128)(2,1)S(1)} %copy-done.5, f32[1,2048]{1,0:T(1,128)S(1)} %bitcast.2, ...), custom_call_target="tpu_custom_call" | custom-call | flops 268435456 | bytes 7495684 | tf_op jit(solution)/shard_map/intra1/pallas_call | solution.py:26
  54.2 1.3 %intra0.1 = (f32[256,1024]{1,0:T(8,128)S(1)}, f32[256,1024]{1,0:T(8,128)S(1)}) custom-call(s32[1]{0:T(128)} %bitcast.core_ref, bf16[256,2048]{1,0:T(8,128)(2,1)S(1)} %copy-done, bf16[256,2048]{1,0:T(8,128)(2,1)S(1)} %copy-done.2, bf16[256,2048]{1,0:T(8,128)(2,1)S(1)} %copy-done.4, bf16[256,2048]{1,0:T(8,128)(2,1)S(1)} %copy-done.5, f32[1,2048]{1,0:T(1,128)S(1)} %bitcast.3, ...), custom_call_target="tpu_custom_call" | custom-call | flops 268435456 | bytes 7495684 | tf_op jit(solution)/shard_map/intra0/pallas_call | solution.py:26
  55.5 0.8 attend0.1
  56.3 0.0 collective-permute-done.4.state_ref
  56.3 0.9 attend1.1
  57.2 1.2 %collective-permute-start.5 = (f32[8,256]{1,0:T(8,128)S(1)}, f32[8,256]{1,0:T(8,128)S(1)}, u32[]{:S(2)}, u32[]{:S(2)}) collective-permute-start(f32[8,256]{1,0:T(8,128)S(1)} %get-tuple-element.51), channel_id=1, source_target_pairs={{0,1},{1,0},{2,3},{3,2},{4,5},{5,4},{6,7},{7,6},{8,9},{9,8},{10,11... | collective-permute-start | bytes 24584 | tf_op jit(solution)/shard_map/ppermute | solution.py:300
  58.4 1.3 %collective-permute-done.5 = f32[8,256]{1,0:T(8,128)S(1)} collective-permute-done((f32[8,256]{1,0:T(8,128)S(1)}, f32[8,256]{1,0:T(8,128)S(1)}, u32[]{:S(2)}, u32[]{:S(2)}) %collective-permute-start.5) | collective-permute-done | bytes 8224 | tf_op jit(solution)/shard_map/ppermute | solution.py:300
  59.7 2.5 %collective-permute-start.6 = (f32[8,256]{1,0:T(8,128)S(1)}, f32[8,256]{1,0:T(8,128)S(1)}, u32[]{:S(2)}, u32[]{:S(2)}) collective-permute-start(f32[8,256]{1,0:T(8,128)S(1)} %add.6), channel_id=1, source_target_pairs={{0,3},{1,2},{2,1},{3,0},{4,7},{5,6},{6,5},{7,4},{8,11},{9,10},{10,... | collective-permute-start | bytes 24584 | tf_op jit(solution)/shard_map/ppermute | solution.py:300
  62.2 1.2 %collective-permute-done.6 = f32[8,256]{1,0:T(8,128)S(1)} collective-permute-done((f32[8,256]{1,0:T(8,128)S(1)}, f32[8,256]{1,0:T(8,128)S(1)}, u32[]{:S(2)}, u32[]{:S(2)}) %collective-permute-start.6) | collective-permute-done | bytes 8224 | tf_op jit(solution)/shard_map/ppermute | solution.py:300
  63.4 1.3 %grad1.1 = (bf16[256,1024]{1,0:T(8,128)(2,1)S(1)}, f32[1024,128]{1,0:T(8,128)S(1)}) custom-call(s32[1]{0:T(128)} %bitcast.core_ref, bf16[256,2048]{1,0:T(8,128)(2,1)S(1)} %copy-done, f32[256,1024]{1,0:T(8,128)S(1)} %get-tuple-element.50.attention_ref.other_ref, f32[256,1024]{1,0:T(8,128)S(1)} %get-tuple-element.48.normed_ref, ...), custom_call_target="tpu_custom_call" | custom-call | flops 67108864 | bytes 4333572 | tf_op jit(solution)/shard_map/grad1/pallas_call | solution.py:26
  64.7 3.3 %collective-permute-start.7 = (f32[1024,128]{1,0:T(8,128)S(1)}, f32[1024,128]{1,0:T(8,128)S(1)}, u32[]{:S(2)}, u32[]{:S(2)}) collective-permute-start(f32[1024,128]{1,0:T(8,128)S(1)} %get-tuple-element.59), channel_id=1, source_target_pairs={{0,4},{4,0},{1,5},{5,1},{2,6},{6,2},{3,7},{7,3},{8,12},{12,8},{9,1... | collective-permute-start | bytes 1572872 | tf_op jit(solution)/shard_map/ppermute | solution.py:287
  68.1 1.3 %grad0.1 = (bf16[256,1024]{1,0:T(8,128)(2,1)S(1)}, f32[1024,128]{1,0:T(8,128)S(1)}) custom-call(s32[1]{0:T(128)} %bitcast.core_ref, bf16[256,2048]{1,0:T(8,128)(2,1)S(1)} %copy-done, f32[256,1024]{1,0:T(8,128)S(1)} %get-tuple-element.45.attention_ref.own_ref, f32[256,1024]{1,0:T(8,128)S(1)} %get-tuple-element.44.normed_ref, ...), custom_call_target="tpu_custom_call" | custom-call | flops 67108864 | bytes 4333572 | tf_op jit(solution)/shard_map/grad0/pallas_call | solution.py:26
  69.3 0.3 collective-permute-done.7.other_ref
  69.6 0.1 merge_b.1
  69.7 11.1 %all_to_all.22.parts_ref = f32[8,128,128]{2,1,0:T(8,128)S(1)} all-to-all(f32[8,128,128]{2,1,0:T(8,128)S(1)} %merge_b.1), channel_id=1, replica_groups=mesh['z1'=4,'z0'=2,'y'=4,'core'=2,'head'=4] {'z0','y'}, dimensions={0} | all-to-all | bytes 1048576 | tf_op jit(solution)/shard_map/all_to_all | solution.py:295
  80.8 1.3 %collective-permute-start.10 = (f32[136,128]{1,0:T(8,128)S(1)}, f32[136,128]{1,0:T(8,128)S(1)}, u32[]{:S(2)}, u32[]{:S(2)}) collective-permute-start(f32[136,128]{1,0:T(8,128)S(1)} %row_total.3), channel_id=1, source_target_pairs={{192,0},{193,1},{194,2},{195,3},{196,4},{197,5},{198,6},{199,7},{2... | collective-permute-start | bytes 208904 | tf_op jit(solution)/shard_map/ppermute | solution.py:291
  82.1 1.3 %collective-permute-start.9 = (f32[136,128]{1,0:T(8,128)S(1)}, f32[136,128]{1,0:T(8,128)S(1)}, u32[]{:S(2)}, u32[]{:S(2)}) collective-permute-start(f32[136,128]{1,0:T(8,128)S(1)} %row_total.3), channel_id=1, source_target_pairs={{128,0},{192,64},{129,1},{193,65},{130,2},{194,66},{131,3},{195,67... | collective-permute-start | bytes 208904 | tf_op jit(solution)/shard_map/ppermute | solution.py:291
  83.4 1.3 %collective-permute-start.8 = (f32[136,128]{1,0:T(8,128)S(1)}, f32[136,128]{1,0:T(8,128)S(1)}, u32[]{:S(2)}, u32[]{:S(2)}) collective-permute-start(f32[136,128]{1,0:T(8,128)S(1)} %row_total.3), channel_id=1, source_target_pairs={{64,0},{128,64},{192,128},{65,1},{129,65},{193,129},{66,2},{130,66... | collective-permute-start | bytes 208904 | tf_op jit(solution)/shard_map/ppermute | solution.py:291
  84.7 3.4 %collective-permute-done.10.far_ref = f32[136,128]{1,0:T(8,128)S(1)} collective-permute-done((f32[136,128]{1,0:T(8,128)S(1)}, f32[136,128]{1,0:T(8,128)S(1)}, u32[]{:S(2)}, u32[]{:S(2)}) %collective-permute-start.10) | collective-permute-done | bytes 69664 | tf_op jit(solution)/shard_map/ppermute | solution.py:291
  88.1 3.1 %collective-permute-done.9.mid_ref = f32[136,128]{1,0:T(8,128)S(1)} collective-permute-done((f32[136,128]{1,0:T(8,128)S(1)}, f32[136,128]{1,0:T(8,128)S(1)}, u32[]{:S(2)}, u32[]{:S(2)}) %collective-permute-start.9) | collective-permute-done | bytes 69664 | tf_op jit(solution)/shard_map/ppermute | solution.py:291
  91.3 0.0 collective-permute-done.8.near_ref
  91.3 0.1 enter.3
  91.3 11.4 %all_to_all.23.enter_ref = f32[8,128,128]{2,1,0:T(8,128)S(1)} all-to-all(f32[8,128,128]{2,1,0:T(8,128)S(1)} %enter.3), channel_id=1, replica_groups=mesh['z1'=4,'z0'=2,'y'=4,'core'=2,'head'=4] {'z0','y'}, dimensions={0} | all-to-all | bytes 1048576 | tf_op jit(solution)/shard_map/all_to_all | solution.py:295
  102.8 0.1 leave.3
  102.9 4.5 %collective-permute-start.11 = (f32[8,128,128]{2,1,0:T(8,128)S(1)}, f32[8,128,128]{2,1,0:T(8,128)S(1)}, u32[]{:S(2)}, u32[]{:S(2)}) collective-permute-start(f32[8,128,128]{2,1,0:T(8,128)S(1)} %get-tuple-element.61), channel_id=1, source_target_pairs={{0,4},{4,0},{1,5},{5,1},{2,6},{6,2},{3,7},{7,3},{8,12},{12,8},{9,1... | collective-permute-start | bytes 1572872 | tf_op jit(solution)/shard_map/ppermute | solution.py:287
  107.4 2.8 %inner0.1 = (bf16[256,1024]{1,0:T(8,128)(2,1)S(1)}, f32[256,1024]{1,0:T(8,128)S(1)}, f32[256,1024]{1,0:T(8,128)S(1)}) custom-call(s32[1]{0:T(128)} %bitcast.core_ref, bf16[256,2048]{1,0:T(8,128)(2,1)S(1)} %copy-done, bf16[256,2048]{1,0:T(8,128)(2,1)S(1)} %copy-done.2, bf16[256,2048]{1,0:T(8,128)(2,1)S(1)} %copy-done.4, ...), custom_call_target="tpu_custom_call" | custom-call | flops 805306368 | bytes 6963204 | tf_op jit(solution)/shard_map/inner0/pallas_call | solution.py:26
  110.2 2.8 %inner1.1 = (bf16[256,1024]{1,0:T(8,128)(2,1)S(1)}, f32[256,1024]{1,0:T(8,128)S(1)}, f32[256,1024]{1,0:T(8,128)S(1)}) custom-call(s32[1]{0:T(128)} %bitcast.core_ref, bf16[256,2048]{1,0:T(8,128)(2,1)S(1)} %copy-done, bf16[256,2048]{1,0:T(8,128)(2,1)S(1)} %copy-done.2, bf16[256,2048]{1,0:T(8,128)(2,1)S(1)} %copy-done.4, ...), custom_call_target="tpu_custom_call" | custom-call | flops 805306368 | bytes 6963204 | tf_op jit(solution)/shard_map/inner1/pallas_call | solution.py:26
  113.0 3.2 %gates.1 = (bf16[256,2048]{1,0:T(8,128)(2,1)}, bf16[256,2048]{1,0:T(8,128)(2,1)}, bf16[256,2048]{1,0:T(8,128)(2,1)}) custom-call(s32[1]{0:T(128)} %bitcast.core_ref, bf16[256,2048]{1,0:T(8,128)(2,1)S(1)} %copy-done.5, f32[1,2048]{1,0:T(1,128)S(1)} %bitcast.4, bf16[256,2048]{1,0:T(8,128)(2,1)S(1)} %copy-done.6, ...), custom_call_target="tpu_custom_call" | custom-call | bytes 8404996 | tf_op jit(solution)/shard_map/gates/pallas_call | solution.py:26
  116.2 2.5 %last.1 = (bf16[256,2048]{1,0:T(8,128)(2,1)}, bf16[256,2048]{1,0:T(8,128)(2,1)}) custom-call(s32[1]{0:T(128)} %bitcast.core_ref, bf16[256,2048]{1,0:T(8,128)(2,1)S(1)} %copy-done.2, bf16[256,2048]{1,0:T(8,128)(2,1)S(1)} %copy-done.4, f32[8,128,128]{2,1,0:T(8,128)S(1)} %get-tuple-element.60.own_state, f32[8,128,128]{2,1,0:T(8,128)S(1)} %collective-permute-done.11.other_state, ...), custom_call_target="tpu_custom_call" | custom-call | flops 268435456 | bytes 9568260 | tf_op jit(solution)/shard_map/last/pallas_call | solution.py:26
  (19 shorter events, 0.1 us)
Async XLA Ops:
  1.5 1.2 %copy-start.1 = (bf16[256,2048]{1,0:T(8,128)(2,1)S(1)}, bf16[256,2048]{1,0:T(8,128)(2,1)}, u32[]{:S(2)}) copy-start(bf16[256,2048]{1,0:T(8,128)(2,1)} %keys_ref.13) | copy-start | bytes 3145732
  2.7 1.2 %copy-start.3 = (bf16[256,2048]{1,0:T(8,128)(2,1)S(1)}, bf16[256,2048]{1,0:T(8,128)(2,1)}, u32[]{:S(2)}) copy-start(bf16[256,2048]{1,0:T(8,128)(2,1)} %value_ref.13) | copy-start | bytes 3145732
  5.3 4.9 %collective-permute-start = (f32[1032,128]{1,0:T(8,128)S(1)}, f32[1032,128]{1,0:T(8,128)S(1)}, u32[]{:S(2)}, u32[]{:S(2)}) collective-permute-start(f32[1032,128]{1,0:T(8,128)S(1)} %get-tuple-element.38), channel_id=1, source_target_pairs={{0,4},{4,0},{1,5},{5,1},{2,6},{6,2},{3,7},{7,3},{8,12},{12,8},{9,1... | collective-permute-start | bytes 1585160 | tf_op jit(solution)/shard_map/ppermute | solution.py:287
  24.0 28.8 %copy-start.6 = (bf16[256,2048]{1,0:T(8,128)(2,1)S(1)}, bf16[256,2048]{1,0:T(8,128)(2,1)}, u32[]{:S(2)}) copy-start(bf16[256,2048]{1,0:T(8,128)(2,1)} %upstream_ref.1) | copy-start | bytes 3145732
  24.1 12.5 %collective-permute-start.3 = (f32[136,128]{1,0:T(8,128)S(1)}, f32[136,128]{1,0:T(8,128)S(1)}, u32[]{:S(2)}, u32[]{:S(2)}) collective-permute-start(f32[136,128]{1,0:T(8,128)S(1)} %row_total.2), channel_id=1, source_target_pairs={{0,192},{1,193},{2,194},{3,195},{4,196},{5,197},{6,198},{7,199},{8... | collective-permute-start | bytes 208904 | tf_op jit(solution)/shard_map/ppermute | solution.py:291
  31.3 5.3 %collective-permute-start.2 = (f32[136,128]{1,0:T(8,128)S(1)}, f32[136,128]{1,0:T(8,128)S(1)}, u32[]{:S(2)}, u32[]{:S(2)}) collective-permute-start(f32[136,128]{1,0:T(8,128)S(1)} %row_total.2), channel_id=1, source_target_pairs={{0,128},{64,192},{1,129},{65,193},{2,130},{66,194},{3,131},{67,195... | collective-permute-start | bytes 208904 | tf_op jit(solution)/shard_map/ppermute | solution.py:291
  32.8 5.1 %collective-permute-start.1 = (f32[136,128]{1,0:T(8,128)S(1)}, f32[136,128]{1,0:T(8,128)S(1)}, u32[]{:S(2)}, u32[]{:S(2)}) collective-permute-start(f32[136,128]{1,0:T(8,128)S(1)} %row_total.2), channel_id=1, source_target_pairs={{0,64},{64,128},{128,192},{1,65},{65,129},{129,193},{2,66},{66,130... | collective-permute-start | bytes 208904 | tf_op jit(solution)/shard_map/ppermute | solution.py:291
  37.9 14.9 %copy-start.4 = (bf16[256,2048]{1,0:T(8,128)(2,1)S(1)}, bf16[256,2048]{1,0:T(8,128)(2,1)}, u32[]{:S(2)}) copy-start(bf16[256,2048]{1,0:T(8,128)(2,1)} %value_ref.13) | copy-start | bytes 3145732
  37.9 14.9 %copy-start.5 = (bf16[256,2048]{1,0:T(8,128)(2,1)S(1)}, bf16[256,2048]{1,0:T(8,128)(2,1)}, u32[]{:S(2)}) copy-start(bf16[256,2048]{1,0:T(8,128)(2,1)} %gate_ref.5) | copy-start | bytes 3145732
  38.0 14.9 %copy-start.2 = (bf16[256,2048]{1,0:T(8,128)(2,1)S(1)}, bf16[256,2048]{1,0:T(8,128)(2,1)}, u32[]{:S(2)}) copy-start(bf16[256,2048]{1,0:T(8,128)(2,1)} %keys_ref.13) | copy-start | bytes 3145732
  49.2 3.7 %copy-start = (bf16[256,2048]{1,0:T(8,128)(2,1)S(1)}, bf16[256,2048]{1,0:T(8,128)(2,1)}, u32[]{:S(2)}) copy-start(bf16[256,2048]{1,0:T(8,128)(2,1)} %query_ref.15) | copy-start | bytes 3145732
  49.2 3.7 %copy-start.7 = (f32[2048]{0:T(1024)S(1)}, f32[2048]{0:T(1024)}, u32[]{:S(2)}) copy-start(f32[2048]{0:T(1024)} %param.12) | copy-start | bytes 24580
  49.3 7.0 %collective-permute-start.4 = (f32[8,128,128]{2,1,0:T(8,128)S(1)}, f32[8,128,128]{2,1,0:T(8,128)S(1)}, u32[]{:S(2)}, u32[]{:S(2)}) collective-permute-start(f32[8,128,128]{2,1,0:T(8,128)S(1)} %get-tuple-element.46), channel_id=1, source_target_pairs={{0,4},{4,0},{1,5},{5,1},{2,6},{6,2},{3,7},{7,3},{8,12},{12,8},{9,1... | collective-permute-start | bytes 1572872 | tf_op jit(solution)/shard_map/ppermute | solution.py:287
  57.2 2.5 %collective-permute-start.5 = (f32[8,256]{1,0:T(8,128)S(1)}, f32[8,256]{1,0:T(8,128)S(1)}, u32[]{:S(2)}, u32[]{:S(2)}) collective-permute-start(f32[8,256]{1,0:T(8,128)S(1)} %get-tuple-element.51), channel_id=1, source_target_pairs={{0,1},{1,0},{2,3},{3,2},{4,5},{5,4},{6,7},{7,6},{8,9},{9,8},{10,11... | collective-permute-start | bytes 24584 | tf_op jit(solution)/shard_map/ppermute | solution.py:300
  59.7 3.7 %collective-permute-start.6 = (f32[8,256]{1,0:T(8,128)S(1)}, f32[8,256]{1,0:T(8,128)S(1)}, u32[]{:S(2)}, u32[]{:S(2)}) collective-permute-start(f32[8,256]{1,0:T(8,128)S(1)} %add.6), channel_id=1, source_target_pairs={{0,3},{1,2},{2,1},{3,0},{4,7},{5,6},{6,5},{7,4},{8,11},{9,10},{10,... | collective-permute-start | bytes 24584 | tf_op jit(solution)/shard_map/ppermute | solution.py:300
  64.7 4.9 %collective-permute-start.7 = (f32[1024,128]{1,0:T(8,128)S(1)}, f32[1024,128]{1,0:T(8,128)S(1)}, u32[]{:S(2)}, u32[]{:S(2)}) collective-permute-start(f32[1024,128]{1,0:T(8,128)S(1)} %get-tuple-element.59), channel_id=1, source_target_pairs={{0,4},{4,0},{1,5},{5,1},{2,6},{6,2},{3,7},{7,3},{8,12},{12,8},{9,1... | collective-permute-start | bytes 1572872 | tf_op jit(solution)/shard_map/ppermute | solution.py:287
  80.8 7.3 %collective-permute-start.10 = (f32[136,128]{1,0:T(8,128)S(1)}, f32[136,128]{1,0:T(8,128)S(1)}, u32[]{:S(2)}, u32[]{:S(2)}) collective-permute-start(f32[136,128]{1,0:T(8,128)S(1)} %row_total.3), channel_id=1, source_target_pairs={{192,0},{193,1},{194,2},{195,3},{196,4},{197,5},{198,6},{199,7},{2... | collective-permute-start | bytes 208904 | tf_op jit(solution)/shard_map/ppermute | solution.py:291
  82.1 9.1 %collective-permute-start.9 = (f32[136,128]{1,0:T(8,128)S(1)}, f32[136,128]{1,0:T(8,128)S(1)}, u32[]{:S(2)}, u32[]{:S(2)}) collective-permute-start(f32[136,128]{1,0:T(8,128)S(1)} %row_total.3), channel_id=1, source_target_pairs={{128,0},{192,64},{129,1},{193,65},{130,2},{194,66},{131,3},{195,67... | collective-permute-start | bytes 208904 | tf_op jit(solution)/shard_map/ppermute | solution.py:291
  83.4 7.8 %collective-permute-start.8 = (f32[136,128]{1,0:T(8,128)S(1)}, f32[136,128]{1,0:T(8,128)S(1)}, u32[]{:S(2)}, u32[]{:S(2)}) collective-permute-start(f32[136,128]{1,0:T(8,128)S(1)} %row_total.3), channel_id=1, source_target_pairs={{64,0},{128,64},{192,128},{65,1},{129,65},{193,129},{66,2},{130,66... | collective-permute-start | bytes 208904 | tf_op jit(solution)/shard_map/ppermute | solution.py:291
  102.9 13.3 %collective-permute-start.11 = (f32[8,128,128]{2,1,0:T(8,128)S(1)}, f32[8,128,128]{2,1,0:T(8,128)S(1)}, u32[]{:S(2)}, u32[]{:S(2)}) collective-permute-start(f32[8,128,128]{2,1,0:T(8,128)S(1)} %get-tuple-element.61), channel_id=1, source_target_pairs={{0,4},{4,0},{1,5},{5,1},{2,6},{6,2},{3,7},{7,3},{8,12},{12,8},{9,1... | collective-permute-start | bytes 1572872 | tf_op jit(solution)/shard_map/ppermute | solution.py:287

commit v2 on v1

--- a/solution.py
+++ b/solution.py
@@ -18,16 +18,19 @@
 PLANE = ("z0", "y")
 VMEM = pl.BlockSpec(memory_space=pltpu.VMEM)
 SMEM = pl.BlockSpec(memory_space=pltpu.SMEM)
-
-
-def call(kernel, out, *args, flops=0, smem=1, limit=12, name=None):
+HBM = pl.BlockSpec(memory_space=pltpu.HBM)
+
+
+def call(kernel, out, *args, flops=0, smem=1, limit=12, name=None, specs=None, outs=None, scratch=(), aliases=None):
     moved = sum(a.size * a.dtype.itemsize for a in args)
     moved += sum(o.size * o.dtype.itemsize for o in jax.tree.leaves(out))
     return pl.pallas_call(
         kernel,
         out_shape=out,
-        in_specs=[SMEM] * smem + [VMEM] * (len(args) - smem),
-        out_specs=jax.tree.map(lambda _: VMEM, out),
+        in_specs=specs or [SMEM] * smem + [VMEM] * (len(args) - smem),
+        out_specs=outs or jax.tree.map(lambda _: VMEM, out),
+        scratch_shapes=scratch,
+        input_output_aliases=aliases or {},
         compiler_params=pltpu.CompilerParams(vmem_limit_bytes=limit << 20),
         cost_estimate=pl.CostEstimate(flops=flops, bytes_accessed=moved, transcendentals=0),
         name=name,
@@ -58,8 +61,8 @@
     rows = lax.broadcasted_iota(jnp.int32, (GROUP, GROUP), 0)
     cols = lax.broadcasted_iota(jnp.int32, (GROUP, GROUP), 1)
     tri = (rows >= cols).astype(F32)
-    down = dot(tri, decays, 1, 0, lax.Precision.HIGHEST)
-    across = dot(decays, tri, 0, 1, lax.Precision.HIGHEST)
+    down = dot(tri, decays, 1, 1, lax.Precision.HIGHEST)
+    across = dot(decays, tri, 1, 1, lax.Precision.HIGHEST)
     swapped = jnp.concatenate([down[:, HALF:], down[:, :HALF]], axis=1)
     down = jnp.where(core == 0, down, swapped)
     across = jnp.where(core == 0, across, jnp.concatenate([across[HALF:], across[:HALF]], axis=0))
@@ -72,17 +75,31 @@
     return dot(keyed, value_ref[:, at], 0, 0)
 
 
-def first_kernel(core_ref, keys_ref, value_ref, decay_ref, tab_ref, across_ref, send_ref):
-    core = core_ref[0]
+def first_kernel(
+    core_ref, keys_hbm, value_hbm, decay_hbm, tab_ref, across_ref, send_ref, keys_ref, value_ref, decay_ref, sems
+):
+    core = core_ref[0]
+    copies = [pltpu.make_async_copy(decay_hbm, decay_ref, sems.at[0])]
+    for role in (1, 0):
+        at = pl.ds(pl.multiple_of((core if role == 0 else 1 - core) * WIDE, WIDE), WIDE)
+        for source, target in ((keys_hbm, keys_ref), (value_hbm, value_ref)):
+            copies.append(pltpu.make_async_copy(source.at[:, at], target.at[:, at], sems.at[len(copies)]))
+    for copy in copies:
+        copy.start()
+    copies[0].wait()
     down, across = tables(core, decay_ref[...])
     last = down[GROUP - 1 :, :]
     blank = jnp.zeros((GROUP, 128 - 48), F32)
     tab = jnp.concatenate([down, jnp.exp(down), jnp.exp(last - down), blank], axis=1)
     tab_ref[...] = tab
     across_ref[...] = across
+    send_ref[WIDE:, :] = jnp.broadcast_to(tab[GROUP - 1 :, :], (8, 128))
+    copies[1].wait()
+    copies[2].wait()
     for i in range(HALF):
         send_ref[i * DH : (i + 1) * DH, :] = state_term(core, 1, i, keys_ref, value_ref, tab)
-    send_ref[WIDE:, :] = jnp.broadcast_to(tab[GROUP - 1 :, :], (8, 128))
+    copies[3].wait()
+    copies[4].wait()
 
 
 def second_kernel(core_ref, keys_ref, value_ref, tab_ref, keep_ref):
@@ -265,22 +282,32 @@
 
 
 def last_kernel(
-    core_ref, keys_ref, value_ref, own_state, other_state, own_keys, other_keys, own_value, other_value, tab_ref,
-    keys_out, value_out,
+    role, core_ref, keys_ref, value_ref, state_ref, part_keys, part_value, tab_ref, *refs
 ):
-    core = core_ref[0]
-    tab = tab_ref[...]
-    parts = ((0, own_state, own_keys, own_value), (1, other_state, other_keys, other_value))
-    for role, state_ref, part_keys, part_value in parts:
-        for i in range(HALF):
-            at = columns(role, core, i)
-            to = slice(i * DH, (i + 1) * DH)
-            state = state_ref[i].astype(BF16)
-            toward_end = lanes(tab, 2, role, i)
-            grad_keys = part_keys[:, to] + dot(value_ref[:, at], state, 1, 1) * toward_end
-            grad_value = part_value[:, to] + dot(keys_ref[:, at], state, 1, 0) * toward_end
-            keys_out[:, at] = grad_keys.astype(BF16)
-            value_out[:, at] = grad_value.astype(BF16)
+    keys_out, value_out, keys_buf, value_buf, sems = refs[-5:]
+    core = core_ref[0]
+    tab = tab_ref[...]
+    copies = []
+    for i in range(HALF):
+        at = columns(role, core, i)
+        to = slice(i * DH, (i + 1) * DH)
+        state = state_ref[i].astype(BF16)
+        toward_end = lanes(tab, 2, role, i)
+        grad_keys = part_keys[:, to] + dot(value_ref[:, at], state, 1, 1) * toward_end
+        grad_value = part_value[:, to] + dot(keys_ref[:, at], state, 1, 0) * toward_end
+        keys_buf[:, to] = grad_keys.astype(BF16)
+        value_buf[:, to] = grad_value.astype(BF16)
+        if i % 2 == 1:
+            width = 2 * DH
+            start = (i - 1) * DH
+            side = core if role == 0 else 1 - core
+            away = pl.ds(pl.multiple_of(side * WIDE + start, width), width)
+            for buf, out in ((keys_buf, keys_out), (value_buf, value_out)):
+                copy = pltpu.make_async_copy(buf.at[:, start : start + width], out.at[:, away], sems.at[len(copies)])
+                copy.start()
+                copies.append(copy)
+    for copy in copies:
+        copy.wait()
 
 
 def swap(array):
@@ -301,7 +328,7 @@
     return array
 
 
-def scan(core, own, other, tab, dec, decays, reverse):
+def scan(core, own, other, tab, dec, decays, reverse, beside):
     if reverse:
         totals = call(merge_backward, shape(HALF, DH, DH), core, own, other, dec, name="merge_b")
     else:
@@ -314,7 +341,8 @@
         functools.partial(total_kernel, reverse), shape(DH + 8, DH), parts, decays, smem=0, name="row_total"
     )
     step = -1 if reverse else 1
-    near, mid, far = (shifted(row, step * by) for by in (1, 2, 3))
+    moved = [shifted(row, step * by) for by in (1, 2, 3)]
+    (near, mid, far), beside = lax.optimization_barrier((moved, beside(row)))
     entering = call(
         functools.partial(enter_kernel, reverse), shape(8, DH, DH), parts, decays, near, mid, far, smem=0, name="enter"
     )
@@ -324,7 +352,7 @@
         (shape(HALF, DH, DH), shape(HALF, DH, DH)),
         core, entering, own, other, dec, name="leave",
     )
-    return keep, swap(send), dec, decays
+    return keep, swap(send), dec, decays, beside
 
 
 def on_device(query, keys, value, gate, decay, gain, upstream):
@@ -333,24 +361,32 @@
     big = 2 * GROUP * GROUP * DH * HALF
     small = big // 2
 
-    tab, across, send = call(
+    full = shape(GROUP, 2 * WIDE, dtype=BF16)
+    tab, across, send, keys, value = call(
         first_kernel,
-        (shape(GROUP, 128), shape(16, GROUP), shape(WIDE + 8, DH)),
-        core, keys, value, decay, flops=small, name="first",
+        (shape(GROUP, 128), shape(16, GROUP), shape(WIDE + 8, DH), full, full),
+        core, *(pltpu.with_memory_space_constraint(a, pltpu.HBM) for a in (keys, value, decay.T)),
+        flops=small, name="first",
+        specs=[SMEM, HBM, HBM, HBM], scratch=[pltpu.VMEM((16, GROUP), F32), pltpu.SemaphoreType.DMA((5,))],
     )
     other = swap(send)
     own = call(second_kernel, shape(WIDE, DH), core, keys, value, tab, flops=small, name="second")
 
     wide = shape(GROUP, WIDE)
-    intra = [
-        call(
-            functools.partial(intra_kernel, role), (wide, wide),
-            core, query, keys, value, gate, gain, upstream, tab, across, flops=2 * big, name=f"intra{role}",
-        )
-        for role in (0, 1)
-    ]
-
-    state_own, state_other, dec, decays = scan(core, own, other, tab, None, None, False)
+
+    def intra_parts(after):
+        held, _ = lax.optimization_barrier((query, after))
+        return [
+            call(
+                functools.partial(intra_kernel, role), (wide, wide),
+                core, held, keys, value, gate, gain, upstream, tab, across, flops=2 * big, name=f"intra{role}",
+            )
+            for role in (0, 1)
+        ]
+
+    state_own, state_other, dec, decays, intra = scan(
+        core, own, other, tab, None, None, False, intra_parts
+    )
 
     def attend_first(core_ref, query_ref, state_ref, intra_ref, normed_ref, tab_ref, out_ref, add_ref):
         attend_kernel(0, core_ref, query_ref, state_ref, intra_ref, normed_ref, tab_ref, None, out_ref, add_ref)
@@ -376,25 +412,34 @@
         flops=small, name="grad0",
     )
 
-    inner = [
-        call(
-            functools.partial(inner_kernel, role), (shape(GROUP, WIDE, dtype=BF16), wide, wide),
-            core, query, keys, value, state, grad, tab, across, flops=6 * big, name=f"inner{role}",
+    def inner_parts(after):
+        held, _ = lax.optimization_barrier((query, after))
+        inner = [
+            call(
+                functools.partial(inner_kernel, role), (shape(GROUP, WIDE, dtype=BF16), wide, wide),
+                core, held, keys, value, state, grad, tab, across, flops=6 * big, name=f"inner{role}",
+            )
+            for role, state, grad in ((0, state_own, grad_own), (1, state_other, grad_other))
+        ]
+
+        return inner, call(
+            gate_kernel, (full, full, full),
+            core, gate, gain, upstream, att_own, att_other, inner[0][0], inner[1][0], sums, name="gates", limit=20,
         )
-        for role, state, grad in ((0, state_own, grad_own), (1, state_other, grad_other))
-    ]
-    full = shape(GROUP, 2 * WIDE, dtype=BF16)
-    mixed, grad_gate, grad_query = call(
-        gate_kernel, (full, full, full),
-        core, gate, gain, upstream, att_own, att_other, inner[0][0], inner[1][0], sums, name="gates", limit=20,
-    )
-
-    after_own, after_other, _, _ = scan(core, term_own, term_other, tab, dec, decays, True)
-    grad_keys, grad_value = call(
-        last_kernel, (full, full),
-        core, keys, value, after_own, after_other, inner[0][1], inner[1][1], inner[0][2], inner[1][2], tab,
-        flops=4 * small, name="last", limit=20,
-    )
+
+    after_own, after_other, _, _, (inner, (mixed, grad_gate, grad_query)) = scan(
+        core, term_own, term_other, tab, dec, decays, True, inner_parts
+    )
+    half = pltpu.VMEM((GROUP, WIDE), BF16)
+    ends = ()
+    for role, state in ((0, after_own), (1, after_other)):
+        ends = call(
+            functools.partial(last_kernel, role), (full, full),
+            core, keys, value, state, *inner[role][1:], tab, *ends, flops=2 * small, name=f"last{role}",
+            specs=[SMEM] + [VMEM] * 6 + [HBM] * len(ends), outs=(HBM, HBM),
+            scratch=[half, half, pltpu.SemaphoreType.DMA((8,))], aliases={7: 0, 8: 1} if ends else None,
+        )
+    grad_keys, grad_value = ends
     return mixed, grad_query, grad_keys, grad_value, grad_gate
 
 

time: 120 us -> 110 us (0.917)
  waiting for transfers between devices: 11.3 us -> 5.99 us
  starting transfers between devices: 34.8 us -> 31.1 us
  local copies, waits for them, and re-layouts: 3.29 us -> 0.02 us
  blocking collectives: 47.3 us -> 48.5 us
    ppermute x6, waiting for transfers between devices: 7.85 us -> 1.75 us  [shifted(): lax.ppermute(array, 'z1', [(i, i + by) for i in range(4) if 0 <= i + by <...]
    ppermute x4, starting transfers between devices: 14.7 us -> 11 us  [swap(): return lax.ppermute(array, 'core', [(0, 1), (1, 0)])]
    unnamed x17 -> x8, local copies, waits for them, and re-layouts: 3.29 us -> 0.02 us
    pallas_call x20 -> x21, Pallas kernels: 21.3 us -> 22.5 us  [call(): pl.pallas_call(kernel, out_shape=out, in_specs=specs or [SMEM] * smem + [...]
  transfers between devices with their start and end apart: 12 -> 12, of which waited for: 7 -> 7; matrix products, arithmetic and copies ran while one was open for 0% -> 0% of each run, Pallas kernels for 12% -> 15%
where the time goes in v2:
time: 110 us; the launch traced here: 109 us
  blocking collectives  48.5 us (44%)
  starting transfers between devices  31.1 us (28%)
  Pallas kernels  22.5 us (20%)
  waiting for transfers between devices  5.99 us (5%)
    all_to_all x4, blocking collectives, spread(): return lax.all_to_all(array, PLANE, 0, 0, tiled=True)  48.5 us
    pallas_call x21, Pallas kernels, call(): pl.pallas_call(kernel, out_shape=out, in_specs=specs or [SMEM] * smem + [...  22.5 us
    ppermute x6, starting transfers between devices, shifted(): lax.ppermute(array, 'z1', [(i, i + by) for i in range(4) if 0 <= i + by <...  16.4 us
    ppermute x4, starting transfers between devices, swap(): return lax.ppermute(array, 'core', [(0, 1), (1, 0)])  11 us
    ppermute x2, starting transfers between devices, across_heads(): lax.ppermute(array, 'head', [(i, i ^ flip) for i in range(4)])  3.72 us
    ppermute x2, waiting for transfers between devices, across_heads(): lax.ppermute(array, 'head', [(i, i ^ flip) for i in range(4)])  2.53 us
  transfers between devices with their start and end apart: 12, of which 7 were waited for; matrix products, arithmetic and copies ran while one was open for 0% of the time, Pallas kernels for 15%

profile of v2, /device:TPU:1, one launch (start us, length us, event | category | flops | bytes accessed | tf_op | source)
XLA Modules:
  0.0 109.2 jit_solution(3372911474828168390)
XLA Ops:
  0.6 2.4 %first.1 = (f32[256,128]{1,0:T(8,128)S(1)}, f32[16,256]{1,0:T(8,128)S(1)}, f32[1032,128]{1,0:T(8,128)S(1)}, bf16[256,2048]{1,0:T(8,128)(2,1)S(1)}, bf16[256,2048]{1,0:T(8,128)(2,1)S(1)}) custom-call(s32[1]{0:T(128)} %bitcast.core_ref, bf16[256,2048]{1,0:T(8,128)(2,1)} %keys_hbm.1, bf16[256,2048]{1,0:T(8,128)(2,1)} %value_hbm.1, f32[16,256]{1,0:T(8,128)} %bitcast.6), custom_call_target="tpu_custom_call" | custom-call | flops 67108864 | bytes 4886532 | tf_op jit(solution)/shard_map/first/pallas_call | solution.py:27
  3.0 3.3 %collective-permute-start = (f32[1032,128]{1,0:T(8,128)S(1)}, f32[1032,128]{1,0:T(8,128)S(1)}, u32[]{:S(2)}, u32[]{:S(2)}) collective-permute-start(f32[1032,128]{1,0:T(8,128)S(1)} %get-tuple-element.63), channel_id=1, source_target_pairs={{0,4},{4,0},{1,5},{5,1},{2,6},{6,2},{3,7},{7,3},{8,12},{12,8},{9,1... | collective-permute-start | bytes 1585160 | tf_op jit(solution)/shard_map/ppermute | solution.py:314
  6.4 0.9 second.1.own_ref
  7.3 0.6 collective-permute-done.other_ref
  7.9 0.2 merge_f.1
  8.1 0.0 copy-start
  8.1 0.0 copy-start.1
  8.2 13.7 %all_to_all.20.parts_ref.decays_ref = f32[8,136,128]{2,1,0:T(8,128)S(1)} all-to-all(f32[8,136,128]{2,1,0:T(8,128)S(1)} %get-tuple-element.64), channel_id=1, replica_groups=mesh['z1'=4,'z0'=2,'y'=4,'core'=2,'head'=4] {'z0','y'}, dimensions={0} | all-to-all | bytes 1114112 | tf_op jit(solution)/shard_map/all_to_all | solution.py:322
  21.9 4.9 %collective-permute-start.1 = (f32[136,128]{1,0:T(8,128)S(1)}, f32[136,128]{1,0:T(8,128)S(1)}, u32[]{:S(2)}, u32[]{:S(2)}) collective-permute-start(f32[136,128]{1,0:T(8,128)S(1)} %row_total.2), channel_id=1, source_target_pairs={{0,64},{64,128},{128,192},{1,65},{65,129},{129,193},{2,66},{66,130... | collective-permute-start | bytes 208904 | tf_op jit(solution)/shard_map/ppermute | solution.py:318
  26.8 6.1 %collective-permute-start.2 = (f32[136,128]{1,0:T(8,128)S(1)}, f32[136,128]{1,0:T(8,128)S(1)}, u32[]{:S(2)}, u32[]{:S(2)}) collective-permute-start(f32[136,128]{1,0:T(8,128)S(1)} %row_total.2), channel_id=1, source_target_pairs={{0,128},{64,192},{1,129},{65,193},{2,130},{66,194},{3,131},{67,195... | collective-permute-start | bytes 208904 | tf_op jit(solution)/shard_map/ppermute | solution.py:318
  33.0 1.3 %collective-permute-start.3 = (f32[136,128]{1,0:T(8,128)S(1)}, f32[136,128]{1,0:T(8,128)S(1)}, u32[]{:S(2)}, u32[]{:S(2)}) collective-permute-start(f32[136,128]{1,0:T(8,128)S(1)} %row_total.2), channel_id=1, source_target_pairs={{0,192},{1,193},{2,194},{3,195},{4,196},{5,197},{6,198},{7,199},{8... | collective-permute-start | bytes 208904 | tf_op jit(solution)/shard_map/ppermute | solution.py:318
  34.3 1.3 %intra1.1 = (f32[256,1024]{1,0:T(8,128)S(1)}, f32[256,1024]{1,0:T(8,128)S(1)}) custom-call(s32[1]{0:T(128)} %bitcast.core_ref, bf16[256,2048]{1,0:T(8,128)(2,1)S(1)} %copy-done, bf16[256,2048]{1,0:T(8,128)(2,1)S(1)} %get-tuple-element.60.keys_ref, bf16[256,2048]{1,0:T(8,128)(2,1)S(1)} %get-tuple-element.61.value_ref, bf16[256,2048]{1,0:T(8,128)(2,1)S(1)} %copy-done.1, ...), custom_call_target="tpu_custom_call" | custom-call | flops 268435456 | bytes 7495684 | tf_op jit(solution)/shard_map/intra1/pallas_call | solution.py:27
  35.6 1.3 %intra0.1 = (f32[256,1024]{1,0:T(8,128)S(1)}, f32[256,1024]{1,0:T(8,128)S(1)}) custom-call(s32[1]{0:T(128)} %bitcast.core_ref, bf16[256,2048]{1,0:T(8,128)(2,1)S(1)} %copy-done, bf16[256,2048]{1,0:T(8,128)(2,1)S(1)} %get-tuple-element.60.keys_ref, bf16[256,2048]{1,0:T(8,128)(2,1)S(1)} %get-tuple-element.61.value_ref, bf16[256,2048]{1,0:T(8,128)(2,1)S(1)} %copy-done.1, ...), custom_call_target="tpu_custom_call" | custom-call | flops 268435456 | bytes 7495684 | tf_op jit(solution)/shard_map/intra0/pallas_call | solution.py:27
  36.9 0.0 collective-permute-done.1.near_ref
  37.0 0.0 collective-permute-done.2.mid_ref
  37.0 1.7 %collective-permute-done.3.far_ref = f32[136,128]{1,0:T(8,128)S(1)} collective-permute-done((f32[136,128]{1,0:T(8,128)S(1)}, f32[136,128]{1,0:T(8,128)S(1)}, u32[]{:S(2)}, u32[]{:S(2)}) %collective-permute-start.3) | collective-permute-done | bytes 69664 | tf_op jit(solution)/shard_map/ppermute | solution.py:318
  38.7 0.1 enter.2
  38.8 11.1 %all_to_all.21.enter_ref = f32[8,128,128]{2,1,0:T(8,128)S(1)} all-to-all(f32[8,128,128]{2,1,0:T(8,128)S(1)} %enter.2), channel_id=1, replica_groups=mesh['z1'=4,'z0'=2,'y'=4,'core'=2,'head'=4] {'z0','y'}, dimensions={0} | all-to-all | bytes 1048576 | tf_op jit(solution)/shard_map/all_to_all | solution.py:322
  49.9 0.1 leave.2
  50.1 2.4 %collective-permute-start.4 = (f32[8,128,128]{2,1,0:T(8,128)S(1)}, f32[8,128,128]{2,1,0:T(8,128)S(1)}, u32[]{:S(2)}, u32[]{:S(2)}) collective-permute-start(f32[8,128,128]{2,1,0:T(8,128)S(1)} %get-tuple-element.79), channel_id=1, source_target_pairs={{0,4},{4,0},{1,5},{5,1},{2,6},{6,2},{3,7},{7,3},{8,12},{12,8},{9,1... | collective-permute-start | bytes 1572872 | tf_op jit(solution)/shard_map/ppermute | solution.py:314
  52.5 0.8 attend0.1
  53.3 0.7 collective-permute-done.4.state_ref
  54.0 0.8 attend1.1
  54.9 1.2 %collective-permute-start.5 = (f32[8,256]{1,0:T(8,128)S(1)}, f32[8,256]{1,0:T(8,128)S(1)}, u32[]{:S(2)}, u32[]{:S(2)}) collective-permute-start(f32[8,256]{1,0:T(8,128)S(1)} %get-tuple-element.83), channel_id=1, source_target_pairs={{0,1},{1,0},{2,3},{3,2},{4,5},{5,4},{6,7},{7,6},{8,9},{9,8},{10,11... | collective-permute-start | bytes 24584 | tf_op jit(solution)/shard_map/ppermute | solution.py:327
  56.1 1.3 %collective-permute-done.5 = f32[8,256]{1,0:T(8,128)S(1)} collective-permute-done((f32[8,256]{1,0:T(8,128)S(1)}, f32[8,256]{1,0:T(8,128)S(1)}, u32[]{:S(2)}, u32[]{:S(2)}) %collective-permute-start.5) | collective-permute-done | bytes 8224 | tf_op jit(solution)/shard_map/ppermute | solution.py:327
  57.4 2.5 %collective-permute-start.6 = (f32[8,256]{1,0:T(8,128)S(1)}, f32[8,256]{1,0:T(8,128)S(1)}, u32[]{:S(2)}, u32[]{:S(2)}) collective-permute-start(f32[8,256]{1,0:T(8,128)S(1)} %add.6), channel_id=1, source_target_pairs={{0,3},{1,2},{2,1},{3,0},{4,7},{5,6},{6,5},{7,4},{8,11},{9,10},{10,... | collective-permute-start | bytes 24584 | tf_op jit(solution)/shard_map/ppermute | solution.py:327
  59.9 1.2 %collective-permute-done.6 = f32[8,256]{1,0:T(8,128)S(1)} collective-permute-done((f32[8,256]{1,0:T(8,128)S(1)}, f32[8,256]{1,0:T(8,128)S(1)}, u32[]{:S(2)}, u32[]{:S(2)}) %collective-permute-start.6) | collective-permute-done | bytes 8224 | tf_op jit(solution)/shard_map/ppermute | solution.py:327
  61.1 1.3 %grad1.1 = (bf16[256,1024]{1,0:T(8,128)(2,1)S(1)}, f32[1024,128]{1,0:T(8,128)S(1)}) custom-call(s32[1]{0:T(128)} %bitcast.core_ref, bf16[256,2048]{1,0:T(8,128)(2,1)S(1)} %copy-done, f32[256,1024]{1,0:T(8,128)S(1)} %get-tuple-element.85.attention_ref.other_ref, f32[256,1024]{1,0:T(8,128)S(1)} %get-tuple-element.81.normed_ref, ...), custom_call_target="tpu_custom_call" | custom-call | flops 67108864 | bytes 4333572 | tf_op jit(solution)/shard_map/grad1/pallas_call | solution.py:27
  62.4 2.8 %collective-permute-start.7 = (f32[1024,128]{1,0:T(8,128)S(1)}, f32[1024,128]{1,0:T(8,128)S(1)}, u32[]{:S(2)}, u32[]{:S(2)}) collective-permute-start(f32[1024,128]{1,0:T(8,128)S(1)} %get-tuple-element.86), channel_id=1, source_target_pairs={{0,4},{4,0},{1,5},{5,1},{2,6},{6,2},{3,7},{7,3},{8,12},{12,8},{9,1... | collective-permute-start | bytes 1572872 | tf_op jit(solution)/shard_map/ppermute | solution.py:314
  65.1 1.3 %grad0.1 = (bf16[256,1024]{1,0:T(8,128)(2,1)S(1)}, f32[1024,128]{1,0:T(8,128)S(1)}) custom-call(s32[1]{0:T(128)} %bitcast.core_ref, bf16[256,2048]{1,0:T(8,128)(2,1)S(1)} %copy-done, f32[256,1024]{1,0:T(8,128)S(1)} %get-tuple-element.78.attention_ref.own_ref, f32[256,1024]{1,0:T(8,128)S(1)} %get-tuple-element.77.normed_ref, ...), custom_call_target="tpu_custom_call" | custom-call | flops 67108864 | bytes 4333572 | tf_op jit(solution)/shard_map/grad0/pallas_call | solution.py:27
  66.4 0.3 collective-permute-done.7.other_ref
  66.7 0.1 merge_b.1
  66.8 11.1 %all_to_all.22.parts_ref = f32[8,128,128]{2,1,0:T(8,128)S(1)} all-to-all(f32[8,128,128]{2,1,0:T(8,128)S(1)} %merge_b.1), channel_id=1, replica_groups=mesh['z1'=4,'z0'=2,'y'=4,'core'=2,'head'=4] {'z0','y'}, dimensions={0} | all-to-all | bytes 1048576 | tf_op jit(solution)/shard_map/all_to_all | solution.py:322
  77.9 1.3 %collective-permute-start.10 = (f32[136,128]{1,0:T(8,128)S(1)}, f32[136,128]{1,0:T(8,128)S(1)}, u32[]{:S(2)}, u32[]{:S(2)}) collective-permute-start(f32[136,128]{1,0:T(8,128)S(1)} %row_total.3), channel_id=1, source_target_pairs={{192,0},{193,1},{194,2},{195,3},{196,4},{197,5},{198,6},{199,7},{2... | collective-permute-start | bytes 208904 | tf_op jit(solution)/shard_map/ppermute | solution.py:318
  79.2 1.3 %collective-permute-start.8 = (f32[136,128]{1,0:T(8,128)S(1)}, f32[136,128]{1,0:T(8,128)S(1)}, u32[]{:S(2)}, u32[]{:S(2)}) collective-permute-start(f32[136,128]{1,0:T(8,128)S(1)} %row_total.3), channel_id=1, source_target_pairs={{64,0},{128,64},{192,128},{65,1},{129,65},{193,129},{66,2},{130,66... | collective-permute-start | bytes 208904 | tf_op jit(solution)/shard_map/ppermute | solution.py:318
  80.5 1.5 %collective-permute-start.9 = (f32[136,128]{1,0:T(8,128)S(1)}, f32[136,128]{1,0:T(8,128)S(1)}, u32[]{:S(2)}, u32[]{:S(2)}) collective-permute-start(f32[136,128]{1,0:T(8,128)S(1)} %row_total.3), channel_id=1, source_target_pairs={{128,0},{192,64},{129,1},{193,65},{130,2},{194,66},{131,3},{195,67... | collective-permute-start | bytes 208904 | tf_op jit(solution)/shard_map/ppermute | solution.py:318
  82.0 2.8 %inner0.1 = (bf16[256,1024]{1,0:T(8,128)(2,1)S(1)}, f32[256,1024]{1,0:T(8,128)S(1)}, f32[256,1024]{1,0:T(8,128)S(1)}) custom-call(s32[1]{0:T(128)} %bitcast.core_ref, bf16[256,2048]{1,0:T(8,128)(2,1)S(1)} %copy-done, bf16[256,2048]{1,0:T(8,128)(2,1)S(1)} %get-tuple-element.60.keys_ref, bf16[256,2048]{1,0:T(8,128)(2,1)S(1)} %get-tuple-element.61.value_ref, ...), custom_call_target="tpu_custom_call" | custom-call | flops 805306368 | bytes 6963204 | tf_op jit(solution)/shard_map/inner0/pallas_call | solution.py:27
  84.8 2.8 %inner1.1 = (bf16[256,1024]{1,0:T(8,128)(2,1)S(1)}, f32[256,1024]{1,0:T(8,128)S(1)}, f32[256,1024]{1,0:T(8,128)S(1)}) custom-call(s32[1]{0:T(128)} %bitcast.core_ref, bf16[256,2048]{1,0:T(8,128)(2,1)S(1)} %copy-done, bf16[256,2048]{1,0:T(8,128)(2,1)S(1)} %get-tuple-element.60.keys_ref, bf16[256,2048]{1,0:T(8,128)(2,1)S(1)} %get-tuple-element.61.value_ref, ...), custom_call_target="tpu_custom_call" | custom-call | flops 805306368 | bytes 6963204 | tf_op jit(solution)/shard_map/inner1/pallas_call | solution.py:27
  87.6 3.2 %gates.1 = (bf16[256,2048]{1,0:T(8,128)(2,1)}, bf16[256,2048]{1,0:T(8,128)(2,1)}, bf16[256,2048]{1,0:T(8,128)(2,1)}) custom-call(s32[1]{0:T(128)} %bitcast.core_ref, bf16[256,2048]{1,0:T(8,128)(2,1)S(1)} %copy-done.1, f32[1,2048]{1,0:T(1,128)S(1)} %bitcast.5, bf16[256,2048]{1,0:T(8,128)(2,1)S(1)} %copy-done.2, ...), custom_call_target="tpu_custom_call" | custom-call | bytes 8404996 | tf_op jit(solution)/shard_map/gates/pallas_call | solution.py:27
  90.8 0.0 collective-permute-done.10.far_ref
  90.8 0.0 collective-permute-done.8.near_ref
  90.8 0.1 enter.3
  90.9 12.5 %all_to_all.23.enter_ref = f32[8,128,128]{2,1,0:T(8,128)S(1)} all-to-all(f32[8,128,128]{2,1,0:T(8,128)S(1)} %enter.3), channel_id=1, replica_groups=mesh['z1'=4,'z0'=2,'y'=4,'core'=2,'head'=4] {'z0','y'}, dimensions={0} | all-to-all | bytes 1048576 | tf_op jit(solution)/shard_map/all_to_all | solution.py:322
  103.4 0.1 leave.3
  103.6 2.5 %collective-permute-start.11 = (f32[8,128,128]{2,1,0:T(8,128)S(1)}, f32[8,128,128]{2,1,0:T(8,128)S(1)}, u32[]{:S(2)}, u32[]{:S(2)}) collective-permute-start(f32[8,128,128]{2,1,0:T(8,128)S(1)} %get-tuple-element.104), channel_id=1, source_target_pairs={{0,4},{4,0},{1,5},{5,1},{2,6},{6,2},{3,7},{7,3},{8,12},{12,8},{9,1... | collective-permute-start | bytes 1572872 | tf_op jit(solution)/shard_map/ppermute | solution.py:314
  106.1 1.4 %last0.1 = (bf16[256,2048]{1,0:T(8,128)(2,1)}, bf16[256,2048]{1,0:T(8,128)(2,1)}) custom-call(s32[1]{0:T(128)} %bitcast.core_ref, bf16[256,2048]{1,0:T(8,128)(2,1)S(1)} %get-tuple-element.60.keys_ref, bf16[256,2048]{1,0:T(8,128)(2,1)S(1)} %get-tuple-element.61.value_ref, f32[8,128,128]{2,1,0:T(8,128)S(1)} %get-tuple-element.107.state_ref, ...), custom_call_target="tpu_custom_call" | custom-call | flops 134217728 | bytes 6946820 | tf_op jit(solution)/shard_map/last0/pallas_call | solution.py:27
  107.5 0.1 collective-permute-done.11.state_ref
  107.6 1.4 %last1.1 = (bf16[256,2048]{1,0:T(8,128)(2,1)}, bf16[256,2048]{1,0:T(8,128)(2,1)}) custom-call(s32[1]{0:T(128)} %bitcast.core_ref, bf16[256,2048]{1,0:T(8,128)(2,1)S(1)} %get-tuple-element.60.keys_ref, bf16[256,2048]{1,0:T(8,128)(2,1)S(1)} %get-tuple-element.61.value_ref, ...), custom_call_target="tpu_custom_call", output_to_operand_aliasing={{0}: (7, {}), {1}: (8, {})} | custom-call | flops 134217728 | bytes 9043972 | tf_op jit(solution)/shard_map/last1/pallas_call | solution.py:27
  (11 shorter events, 0.1 us)
Async XLA Ops:
  3.0 4.9 %collective-permute-start = (f32[1032,128]{1,0:T(8,128)S(1)}, f32[1032,128]{1,0:T(8,128)S(1)}, u32[]{:S(2)}, u32[]{:S(2)}) collective-permute-start(f32[1032,128]{1,0:T(8,128)S(1)} %get-tuple-element.63), channel_id=1, source_target_pairs={{0,4},{4,0},{1,5},{5,1},{2,6},{6,2},{3,7},{7,3},{8,12},{12,8},{9,1... | collective-permute-start | bytes 1585160 | tf_op jit(solution)/shard_map/ppermute | solution.py:314
  7.9 26.4 %copy-start.2 = (bf16[256,2048]{1,0:T(8,128)(2,1)S(1)}, bf16[256,2048]{1,0:T(8,128)(2,1)}, u32[]{:S(2)}) copy-start(bf16[256,2048]{1,0:T(8,128)(2,1)} %upstream_ref.1) | copy-start | bytes 3145732
  8.1 26.1 %copy-start = (bf16[256,2048]{1,0:T(8,128)(2,1)S(1)}, bf16[256,2048]{1,0:T(8,128)(2,1)}, u32[]{:S(2)}) copy-start(bf16[256,2048]{1,0:T(8,128)(2,1)} %query_ref.11) | copy-start | bytes 3145732
  8.1 26.1 %copy-start.1 = (bf16[256,2048]{1,0:T(8,128)(2,1)S(1)}, bf16[256,2048]{1,0:T(8,128)(2,1)}, u32[]{:S(2)}) copy-start(bf16[256,2048]{1,0:T(8,128)(2,1)} %gate_ref.5) | copy-start | bytes 3145732
  21.9 12.4 %copy-start.3 = (f32[2048]{0:T(1024)S(1)}, f32[2048]{0:T(1024)}, u32[]{:S(2)}) copy-start(f32[2048]{0:T(1024)} %param.12) | copy-start | bytes 24580
  21.9 15.0 %collective-permute-start.1 = (f32[136,128]{1,0:T(8,128)S(1)}, f32[136,128]{1,0:T(8,128)S(1)}, u32[]{:S(2)}, u32[]{:S(2)}) collective-permute-start(f32[136,128]{1,0:T(8,128)S(1)} %row_total.2), channel_id=1, source_target_pairs={{0,64},{64,128},{128,192},{1,65},{65,129},{129,193},{2,66},{66,130... | collective-permute-start | bytes 208904 | tf_op jit(solution)/shard_map/ppermute | solution.py:318
  26.8 10.1 %collective-permute-start.2 = (f32[136,128]{1,0:T(8,128)S(1)}, f32[136,128]{1,0:T(8,128)S(1)}, u32[]{:S(2)}, u32[]{:S(2)}) collective-permute-start(f32[136,128]{1,0:T(8,128)S(1)} %row_total.2), channel_id=1, source_target_pairs={{0,128},{64,192},{1,129},{65,193},{2,130},{66,194},{3,131},{67,195... | collective-permute-start | bytes 208904 | tf_op jit(solution)/shard_map/ppermute | solution.py:318
  33.0 5.7 %collective-permute-start.3 = (f32[136,128]{1,0:T(8,128)S(1)}, f32[136,128]{1,0:T(8,128)S(1)}, u32[]{:S(2)}, u32[]{:S(2)}) collective-permute-start(f32[136,128]{1,0:T(8,128)S(1)} %row_total.2), channel_id=1, source_target_pairs={{0,192},{1,193},{2,194},{3,195},{4,196},{5,197},{6,198},{7,199},{8... | collective-permute-start | bytes 208904 | tf_op jit(solution)/shard_map/ppermute | solution.py:318
  50.1 4.0 %collective-permute-start.4 = (f32[8,128,128]{2,1,0:T(8,128)S(1)}, f32[8,128,128]{2,1,0:T(8,128)S(1)}, u32[]{:S(2)}, u32[]{:S(2)}) collective-permute-start(f32[8,128,128]{2,1,0:T(8,128)S(1)} %get-tuple-element.79), channel_id=1, source_target_pairs={{0,4},{4,0},{1,5},{5,1},{2,6},{6,2},{3,7},{7,3},{8,12},{12,8},{9,1... | collective-permute-start | bytes 1572872 | tf_op jit(solution)/shard_map/ppermute | solution.py:314
  54.9 2.5 %collective-permute-start.5 = (f32[8,256]{1,0:T(8,128)S(1)}, f32[8,256]{1,0:T(8,128)S(1)}, u32[]{:S(2)}, u32[]{:S(2)}) collective-permute-start(f32[8,256]{1,0:T(8,128)S(1)} %get-tuple-element.83), channel_id=1, source_target_pairs={{0,1},{1,0},{2,3},{3,2},{4,5},{5,4},{6,7},{7,6},{8,9},{9,8},{10,11... | collective-permute-start | bytes 24584 | tf_op jit(solution)/shard_map/ppermute | solution.py:327
  57.4 3.7 %collective-permute-start.6 = (f32[8,256]{1,0:T(8,128)S(1)}, f32[8,256]{1,0:T(8,128)S(1)}, u32[]{:S(2)}, u32[]{:S(2)}) collective-permute-start(f32[8,256]{1,0:T(8,128)S(1)} %add.6), channel_id=1, source_target_pairs={{0,3},{1,2},{2,1},{3,0},{4,7},{5,6},{6,5},{7,4},{8,11},{9,10},{10,... | collective-permute-start | bytes 24584 | tf_op jit(solution)/shard_map/ppermute | solution.py:327
  62.4 4.3 %collective-permute-start.7 = (f32[1024,128]{1,0:T(8,128)S(1)}, f32[1024,128]{1,0:T(8,128)S(1)}, u32[]{:S(2)}, u32[]{:S(2)}) collective-permute-start(f32[1024,128]{1,0:T(8,128)S(1)} %get-tuple-element.86), channel_id=1, source_target_pairs={{0,4},{4,0},{1,5},{5,1},{2,6},{6,2},{3,7},{7,3},{8,12},{12,8},{9,1... | collective-permute-start | bytes 1572872 | tf_op jit(solution)/shard_map/ppermute | solution.py:314
  77.9 12.9 %collective-permute-start.10 = (f32[136,128]{1,0:T(8,128)S(1)}, f32[136,128]{1,0:T(8,128)S(1)}, u32[]{:S(2)}, u32[]{:S(2)}) collective-permute-start(f32[136,128]{1,0:T(8,128)S(1)} %row_total.3), channel_id=1, source_target_pairs={{192,0},{193,1},{194,2},{195,3},{196,4},{197,5},{198,6},{199,7},{2... | collective-permute-start | bytes 208904 | tf_op jit(solution)/shard_map/ppermute | solution.py:318
  79.2 11.6 %collective-permute-start.8 = (f32[136,128]{1,0:T(8,128)S(1)}, f32[136,128]{1,0:T(8,128)S(1)}, u32[]{:S(2)}, u32[]{:S(2)}) collective-permute-start(f32[136,128]{1,0:T(8,128)S(1)} %row_total.3), channel_id=1, source_target_pairs={{64,0},{128,64},{192,128},{65,1},{129,65},{193,129},{66,2},{130,66... | collective-permute-start | bytes 208904 | tf_op jit(solution)/shard_map/ppermute | solution.py:318
  80.5 10.3 %collective-permute-start.9 = (f32[136,128]{1,0:T(8,128)S(1)}, f32[136,128]{1,0:T(8,128)S(1)}, u32[]{:S(2)}, u32[]{:S(2)}) collective-permute-start(f32[136,128]{1,0:T(8,128)S(1)} %row_total.3), channel_id=1, source_target_pairs={{128,0},{192,64},{129,1},{193,65},{130,2},{194,66},{131,3},{195,67... | collective-permute-start | bytes 208904 | tf_op jit(solution)/shard_map/ppermute | solution.py:318
  103.6 4.1 %collective-permute-start.11 = (f32[8,128,128]{2,1,0:T(8,128)S(1)}, f32[8,128,128]{2,1,0:T(8,128)S(1)}, u32[]{:S(2)}, u32[]{:S(2)}) collective-permute-start(f32[8,128,128]{2,1,0:T(8,128)S(1)} %get-tuple-element.104), channel_id=1, source_target_pairs={{0,4},{4,0},{1,5},{5,1},{2,6},{6,2},{3,7},{7,3},{8,12},{12,8},{9,1... | collective-permute-start | bytes 1572872 | tf_op jit(solution)/shard_map/ppermute | solution.py:314

commit v3 on v2

--- a/solution.py
+++ b/solution.py
@@ -1,4 +1,5 @@
 import functools
+import math
 
 import jax
 import jax.numpy as jnp
@@ -21,9 +22,9 @@
 HBM = pl.BlockSpec(memory_space=pltpu.HBM)
 
 
-def call(kernel, out, *args, flops=0, smem=1, limit=12, name=None, specs=None, outs=None, scratch=(), aliases=None):
+def call(kernel, out, *args, flops=0, smem=1, limit=6, name=None, specs=None, outs=None, scratch=(), aliases=None):
     moved = sum(a.size * a.dtype.itemsize for a in args)
-    moved += sum(o.size * o.dtype.itemsize for o in jax.tree.leaves(out))
+    moved += sum(math.prod(o.shape) * 4 for o in jax.tree.leaves(out))
     return pl.pallas_call(
         kernel,
         out_shape=out,
@@ -148,10 +149,15 @@
     out_ref[DH:, :] = decay
 
 
-def enter_kernel(reverse, parts_ref, decays_ref, near_ref, mid_ref, far_ref, out_ref):
-    state = far_ref[:DH, :]
-    for ref in (mid_ref, near_ref):
-        state = jnp.exp(ref[DH : DH + 1, :]) * state + ref[:DH, :]
+def enter_kernel(reverse, place_ref, parts_ref, decays_ref, one_ref, two_ref, three_ref, out_ref):
+    place = 3 - place_ref[0] if reverse else place_ref[0]
+    one, two, three = one_ref[...], two_ref[...], three_ref[...]
+    far = jnp.where(place >= 2, jnp.where(place == 2, two, three), 0.0)
+    mid = jnp.where(place >= 2, jnp.where(place == 2, three, two), 0.0)
+    near = jnp.where((place == 1) | (place == 3), one, 0.0)
+    state = far[:DH, :]
+    for part in (mid, near):
+        state = jnp.exp(part[DH : DH + 1, :]) * state + part[:DH, :]
     order = list(range(8))[:: -1 if reverse else 1]
     for at in order:
         out_ref[at] = state
@@ -172,25 +178,40 @@
         send_ref[i] = jnp.where(first, y, x)
 
 
-def weights_of(tab, across_ref, role, i):
-    rows = lax.broadcasted_iota(jnp.int32, (GROUP, GROUP), 0)
-    cols = lax.broadcasted_iota(jnp.int32, (GROUP, GROUP), 1)
-    at = role * HALF + i
-    gaps = lanes(tab, 0, role, i) - across_ref[at : at + 1, :]
-    return jnp.exp(jnp.where(rows >= cols, gaps, -jnp.inf))
+LOW, HIGH = slice(0, DH), slice(DH, GROUP)
+
+
+def causal(low, first, second):
+    return jnp.concatenate(
+        [jnp.concatenate([low, jnp.zeros_like(low)], axis=1), jnp.concatenate([first, second], axis=1)], axis=0
+    )
 
 
 def intra_kernel(
     role, core_ref, query_ref, keys_ref, value_ref, gate_ref, gain_ref, mixed_ref, tab_ref, across_ref,
-    intra_ref, normed_ref,
+    intra_ref, normed_ref, probs_ref, weights_ref,
 ):
     core = core_ref[0]
     tab = tab_ref[...]
+    rows = lax.broadcasted_iota(jnp.int32, (DH, DH), 0)
+    cols = lax.broadcasted_iota(jnp.int32, (DH, DH), 1)
+    lower = rows >= cols
     for i in range(HALF):
         at = columns(role, core, i)
         to = slice(i * DH, (i + 1) * DH)
-        scores = dot(query_ref[:, at], keys_ref[:, at], 1, 1)
-        probs = (scores * weights_of(tab, across_ref, role, i)).astype(BF16)
+        query, keys = query_ref[:, at], keys_ref[:, at]
+        down = lanes(tab, 0, role, i)
+        across = across_ref[role * HALF + i : role * HALF + i + 1, :]
+        first = jnp.exp(jnp.where(lower, down[LOW] - across[:, LOW], -jnp.inf))
+        second = jnp.exp(down[HIGH] - across[:, LOW])
+        third = jnp.exp(jnp.where(lower, down[HIGH] - across[:, HIGH], -jnp.inf))
+        weights_ref[i, 0], weights_ref[i, 1], weights_ref[i, 2] = first, second, third
+        above = dot(query[LOW], keys[LOW], 1, 1)
+        below = dot(query[HIGH], keys, 1, 1)
+        probs = causal(
+            (above * first).astype(BF16), (below[:, LOW] * second).astype(BF16), (below[:, HIGH] * third).astype(BF16)
+        )
+        probs_ref[i] = probs
         intra_ref[:, to] = dot(probs, value_ref[:, at], 1, 0)
         opening = jax.nn.sigmoid(gate_ref[:, at].astype(F32))
         normed_ref[:, to] = mixed_ref[:, at].astype(F32) * opening * gain_ref[:, at]
@@ -217,68 +238,117 @@
     add_ref[...] = both if sums_ref is None else sums_ref[...] + both
 
 
-def upright(row):
-    rows = lax.broadcasted_iota(jnp.int32, (GROUP, GROUP), 0)
-    cols = lax.broadcasted_iota(jnp.int32, (GROUP, GROUP), 1)
-    return jnp.sum(jnp.where(rows == cols, row, 0.0), axis=1, keepdims=True)
-
-
-def norm_terms(sums_ref):
-    scale = lax.rsqrt(sums_ref[0:1, :] / FEATURES + EPSILON)
-    projection = scale * sums_ref[1:2, :] / FEATURES
-    return upright(scale), upright(projection)
-
-
-def grad_kernel(role, core_ref, query_ref, attention_ref, normed_ref, tab_ref, sums_ref, grad_ref, term_ref):
+def norm_terms(sums, terms_ref):
+    scale = lax.rsqrt(sums[0:1, :] / FEATURES + EPSILON)
+    projection = scale * sums[1:2, :] / FEATURES
+    both = jnp.concatenate([scale, scale * projection, jnp.zeros((6, GROUP), F32)], axis=0)
+    terms_ref[...] = jnp.concatenate([both.T, jnp.zeros((GROUP, DH - 8), F32)], axis=1)
+
+
+def grad_kernel(role, core_ref, query_ref, attention_ref, normed_ref, tab_ref, terms_ref, grad_ref, term_ref):
     core = core_ref[0]
     tab = tab_ref[...]
-    scale, projection = norm_terms(sums_ref)
+    scale, shift = terms_ref[:, 0:1], terms_ref[:, 1:2]
     for i in range(HALF):
         at = columns(role, core, i)
         to = slice(i * DH, (i + 1) * DH)
-        normed = attention_ref[:, to] * scale
-        grad = (scale * (normed_ref[:, to] - normed * projection)).astype(BF16)
+        grad = (scale * (normed_ref[:, to] - attention_ref[:, to] * shift)).astype(BF16)
         grad_ref[:, to] = grad
         weighted = (query_ref[:, at].astype(F32) * lanes(tab, 1, role, i)).astype(BF16)
         term_ref[i * DH : (i + 1) * DH, :] = dot(weighted, grad, 0, 0)
 
 
+def grad_first(
+    core_ref, query_ref, attention_ref, normed_ref, tab_ref, sum_a, sum_b, sum_c, sum_d, grad_ref, term_ref, terms_ref
+):
+    norm_terms((sum_a[...] + sum_b[...]) + (sum_c[...] + sum_d[...]), terms_ref)
+    grad_kernel(1, core_ref, query_ref, attention_ref, normed_ref, tab_ref, terms_ref, grad_ref, term_ref)
+
+
+class Sender:
+    def __init__(self, role, core, sems):
+        self.side = core if role == 0 else 1 - core
+        self.sems = sems
+        self.copies = []
+
+    def send(self, buf, out, start, width):
+        away = pl.ds(pl.multiple_of(self.side * WIDE + start, width), width)
+        copy = pltpu.make_async_copy(
+            buf.at[:, start : start + width], out.at[:, away], self.sems.at[len(self.copies)]
+        )
+        copy.start()
+        self.copies.append(copy)
+
+    def wait(self):
+        for copy in self.copies:
+            copy.wait()
+
+
 def inner_kernel(
-    role, core_ref, query_ref, keys_ref, value_ref, state_ref, grad_ref, tab_ref, across_ref,
-    query_out, keys_out, value_out,
+    role, core_ref, query_ref, keys_ref, value_ref, state_ref, grad_ref, probs_ref, weights_ref, tab_ref, *refs
 ):
+    query_out, keys_out, value_out, query_buf, sems = refs[-5:]
     core = core_ref[0]
     tab = tab_ref[...]
+    sender = Sender(role, core, sems)
     for i in range(HALF):
         at = columns(role, core, i)
         to = slice(i * DH, (i + 1) * DH)
         query, keys, value, grad = query_ref[:, at], keys_ref[:, at], value_ref[:, at], grad_ref[:, to]
-        weights = weights_of(tab, across_ref, role, i)
-        probs = (dot(query, keys, 1, 1) * weights).astype(BF16)
-        grad_scores = (dot(grad, value, 1, 1) * weights).astype(BF16)
+        above = dot(grad[LOW], value[LOW], 1, 1)
+        below = dot(grad[HIGH], value, 1, 1)
+        grad_scores = causal(
+            (above * weights_ref[i, 0]).astype(BF16),
+            (below[:, LOW] * weights_ref[i, 1]).astype(BF16),
+            (below[:, HIGH] * weights_ref[i, 2]).astype(BF16),
+        )
         grad_query = dot(grad_scores, keys, 1, 0)
         grad_query = grad_query + dot(grad, state_ref[i].astype(BF16), 1, 1) * lanes(tab, 1, role, i)
-        query_out[:, to] = grad_query.astype(BF16)
+        query_buf[:, to] = grad_query.astype(BF16)
         keys_out[:, to] = dot(grad_scores, query, 0, 0)
-        value_out[:, to] = dot(probs, grad, 0, 0)
-
-
-def gate_kernel(
-    core_ref, gate_ref, gain_ref, upstream_ref, own_ref, other_ref, own_query, other_query, sums_ref,
-    mixed_out, gate_out, query_out,
+        value_out[:, to] = dot(probs_ref[i], grad, 0, 0)
+        if i % 2 == 1:
+            sender.send(query_buf, query_out, (i - 1) * DH, 2 * DH)
+    sender.wait()
+
+
+def opened_kernel(
+    core_ref, gate_ref, gain_ref, upstream_ref, own_ref, other_ref, own_normed, other_normed, mixed_ref, gate_out
 ):
     core = core_ref[0]
-    scale, _ = norm_terms(sums_ref)
-    for role, ref, grad_query in ((0, own_ref, own_query), (1, other_ref, other_query)):
+    for role, ref, normed_ref in ((0, own_ref, own_normed), (1, other_ref, other_normed)):
         for i in range(HALF):
             at = columns(role, core, i)
             to = slice(i * DH, (i + 1) * DH)
-            shaped = ref[:, to] * scale * gain_ref[:, at]
+            into = slice(role * WIDE + i * DH, role * WIDE + (i + 1) * DH)
             opening = jax.nn.sigmoid(gate_ref[:, at].astype(F32))
-            mixed_out[:, at] = (shaped * opening).astype(BF16)
-            upstream = upstream_ref[:, at].astype(F32)
-            gate_out[:, at] = (upstream * shaped * opening * (1.0 - opening)).astype(BF16)
-            query_out[:, at] = grad_query[:, to]
+            attention = ref[:, to]
+            mixed_ref[:, into] = attention * (gain_ref[:, at] * opening)
+            gate_out[:, into] = normed_ref[:, to] * (attention * (1.0 - opening))
+
+
+def gate_kernel(core_ref, mixed_ref, gate_ref, terms_ref, mixed_out, gate_out, mixed_buf, gate_buf, sems):
+    core = core_ref[0]
+    scale = terms_ref[:, 0:1]
+    for role in (0, 1):
+        sender = Sender(role, core, sems.at[role])
+        for i in range(HALF):
+            into = slice(role * WIDE + i * DH, role * WIDE + (i + 1) * DH)
+            mixed_buf[:, into] = (mixed_ref[:, into] * scale).astype(BF16)
+            gate_buf[:, into] = (gate_ref[:, into] * scale).astype(BF16)
+            if i % 4 == 3:
+                start = role * WIDE + (i - 3) * DH
+                for buf, out in ((mixed_buf, mixed_out), (gate_buf, gate_out)):
+                    part = pl.ds(pl.multiple_of(sender.side * WIDE + (i - 3) * DH, 4 * DH), 4 * DH)
+                    copy = pltpu.make_async_copy(
+                        buf.at[:, start : start + 4 * DH], out.at[:, part], sems.at[role, len(sender.copies)]
+                    )
+                    copy.start()
+                    sender.copies.append(copy)
+        if role == 0:
+            held = sender
+    held.wait()
+    sender.wait()
 
 
 def last_kernel(
@@ -287,7 +357,7 @@
     keys_out, value_out, keys_buf, value_buf, sems = refs[-5:]
     core = core_ref[0]
     tab = tab_ref[...]
-    copies = []
+    sender = Sender(role, core, sems)
     for i in range(HALF):
         at = columns(role, core, i)
         to = slice(i * DH, (i + 1) * DH)
@@ -298,37 +368,24 @@
         keys_buf[:, to] = grad_keys.astype(BF16)
         value_buf[:, to] = grad_value.astype(BF16)
         if i % 2 == 1:
-            width = 2 * DH
-            start = (i - 1) * DH
-            side = core if role == 0 else 1 - core
-            away = pl.ds(pl.multiple_of(side * WIDE + start, width), width)
             for buf, out in ((keys_buf, keys_out), (value_buf, value_out)):
-                copy = pltpu.make_async_copy(buf.at[:, start : start + width], out.at[:, away], sems.at[len(copies)])
-                copy.start()
-                copies.append(copy)
-    for copy in copies:
-        copy.wait()
+                sender.send(buf, out, (i - 1) * DH, 2 * DH)
+    sender.wait()
 
 
 def swap(array):
     return lax.ppermute(array, "core", [(0, 1), (1, 0)])
 
 
-def shifted(array, by):
-    return lax.ppermute(array, "z1", [(i, i + by) for i in range(4) if 0 <= i + by < 4])
+def flipped(array, axis, flip):
+    return lax.ppermute(array, axis, [(i, i ^ flip) for i in range(4)])
 
 
 def spread(array):
     return lax.all_to_all(array, PLANE, 0, 0, tiled=True)
 
 
-def across_heads(array):
-    for flip in (1, 3):
-        array = array + lax.ppermute(array, "head", [(i, i ^ flip) for i in range(4)])
-    return array
-
-
-def scan(core, own, other, tab, dec, decays, reverse, beside):
+def scan(core, place, own, other, tab, dec, decays, reverse, beside):
     if reverse:
         totals = call(merge_backward, shape(HALF, DH, DH), core, own, other, dec, name="merge_b")
     else:
@@ -340,11 +397,10 @@
     row = call(
         functools.partial(total_kernel, reverse), shape(DH + 8, DH), parts, decays, smem=0, name="row_total"
     )
-    step = -1 if reverse else 1
-    moved = [shifted(row, step * by) for by in (1, 2, 3)]
-    (near, mid, far), beside = lax.optimization_barrier((moved, beside(row)))
+    moved = [flipped(row, "z1", flip) for flip in (1, 2, 3)]
+    moved, beside = lax.optimization_barrier((moved, beside(row)))
     entering = call(
-        functools.partial(enter_kernel, reverse), shape(8, DH, DH), parts, decays, near, mid, far, smem=0, name="enter"
+        functools.partial(enter_kernel, reverse), shape(8, DH, DH), place, parts, decays, *moved, name="enter"
     )
     entering = spread(entering)
     keep, send = call(
@@ -356,7 +412,9 @@
 
 
 def on_device(query, keys, value, gate, decay, gain, upstream):
-    core = lax.axis_index("core").astype(jnp.int32).reshape(1)
+    core, place = lax.optimization_barrier(
+        [lax.axis_index(axis).astype(jnp.int32).reshape(1) for axis in ("core", "z1")]
+    )
     gain = gain.reshape(1, -1)
     big = 2 * GROUP * GROUP * DH * HALF
     small = big // 2
@@ -373,19 +431,21 @@
     own = call(second_kernel, shape(WIDE, DH), core, keys, value, tab, flops=small, name="second")
 
     wide = shape(GROUP, WIDE)
+    probs_shape = shape(HALF, GROUP, GROUP, dtype=BF16)
+    weights_shape = shape(HALF, 3, DH, DH)
 
     def intra_parts(after):
         held, _ = lax.optimization_barrier((query, after))
         return [
             call(
-                functools.partial(intra_kernel, role), (wide, wide),
+                functools.partial(intra_kernel, role), (wide, wide, probs_shape, weights_shape),
                 core, held, keys, value, gate, gain, upstream, tab, across, flops=2 * big, name=f"intra{role}",
             )
             for role in (0, 1)
         ]
 
     state_own, state_other, dec, decays, intra = scan(
-        core, own, other, tab, None, None, False, intra_parts
+        core, place, own, other, tab, None, None, False, intra_parts
     )
 
     def attend_first(core_ref, query_ref, state_ref, intra_ref, normed_ref, tab_ref, out_ref, add_ref):
@@ -393,49 +453,59 @@
 
     sums_shape = shape(8, GROUP)
     att_own, sums = call(
-        attend_first, (wide, sums_shape), core, query, state_own, *intra[0], tab, flops=small, name="attend0"
+        attend_first, (wide, sums_shape), core, query, state_own, *intra[0][:2], tab, flops=small, name="attend0"
     )
     att_other, sums = call(
         functools.partial(attend_kernel, 1), (wide, sums_shape),
-        core, query, state_other, *intra[1], tab, sums, flops=small, name="attend1",
-    )
-    sums = across_heads(sums)
+        core, query, state_other, *intra[1][:2], tab, sums, flops=small, name="attend1",
+    )
+    opened = call(
+        opened_kernel, (shape(GROUP, 2 * WIDE), shape(GROUP, 2 * WIDE)),
+        core, gate, gain, upstream, att_own, att_other, intra[0][1], intra[1][1], name="opened",
+    )
+    moved = [flipped(sums, "head", flip) for flip in (1, 2, 3)]
+    moved, opened = lax.optimization_barrier((moved, opened))
 
     grads_shape = (shape(GROUP, WIDE, dtype=BF16), shape(WIDE, DH))
-    grad_other, term_send = call(
-        functools.partial(grad_kernel, 1), grads_shape, core, query, att_other, intra[1][1], tab, sums,
-        flops=small, name="grad1",
+    grad_other, term_send, terms = call(
+        grad_first, (*grads_shape, shape(GROUP, DH)),
+        core, query, att_other, intra[1][1], tab, sums, *moved, flops=small, name="grad1",
     )
     term_other = swap(term_send)
     grad_own, term_own = call(
-        functools.partial(grad_kernel, 0), grads_shape, core, query, att_own, intra[0][1], tab, sums,
+        functools.partial(grad_kernel, 0), grads_shape, core, query, att_own, intra[0][1], tab, terms,
         flops=small, name="grad0",
     )
 
     def inner_parts(after):
-        held, _ = lax.optimization_barrier((query, after))
-        inner = [
-            call(
-                functools.partial(inner_kernel, role), (shape(GROUP, WIDE, dtype=BF16), wide, wide),
-                core, held, keys, value, state, grad, tab, across, flops=6 * big, name=f"inner{role}",
+        held, factors, _ = lax.optimization_barrier((query, terms, after))
+        inner, queries = [], ()
+        for role, state, grad in ((0, state_own, grad_own), (1, state_other, grad_other)):
+            results = call(
+                functools.partial(inner_kernel, role), (pltpu.HBM((GROUP, 2 * WIDE), BF16), wide, wide),
+                core, held, keys, value, state, grad, *intra[role][2:], tab, *queries,
+                flops=5 * big, name=f"inner{role}",
+                specs=[SMEM] + [VMEM] * 8 + [HBM] * len(queries), outs=(HBM, VMEM, VMEM),
+                scratch=[pltpu.VMEM((GROUP, WIDE), BF16), pltpu.SemaphoreType.DMA((4,))],
+                aliases={9: 0} if queries else None,
             )
-            for role, state, grad in ((0, state_own, grad_own), (1, state_other, grad_other))
-        ]
-
-        return inner, call(
-            gate_kernel, (full, full, full),
-            core, gate, gain, upstream, att_own, att_other, inner[0][0], inner[1][0], sums, name="gates", limit=20,
+            queries = results[:1]
+            inner.append(results[1:])
+        whole = pltpu.VMEM((GROUP, 2 * WIDE), BF16)
+        return inner, queries[0], call(
+            gate_kernel, (full, full), core, *opened, factors, name="gates", outs=(HBM, HBM),
+            scratch=[whole, whole, pltpu.SemaphoreType.DMA((2, 4))],
         )
 
-    after_own, after_other, _, _, (inner, (mixed, grad_gate, grad_query)) = scan(
-        core, term_own, term_other, tab, dec, decays, True, inner_parts
+    after_own, after_other, _, _, (inner, grad_query, (mixed, grad_gate)) = scan(
+        core, place, term_own, term_other, tab, dec, decays, True, inner_parts
     )
     half = pltpu.VMEM((GROUP, WIDE), BF16)
     ends = ()
     for role, state in ((0, after_own), (1, after_other)):
         ends = call(
             functools.partial(last_kernel, role), (full, full),
-            core, keys, value, state, *inner[role][1:], tab, *ends, flops=2 * small, name=f"last{role}",
+            core, keys, value, state, *inner[role], tab, *ends, flops=2 * small, name=f"last{role}",
             specs=[SMEM] + [VMEM] * 6 + [HBM] * len(ends), outs=(HBM, HBM),
             scratch=[half, half, pltpu.SemaphoreType.DMA((8,))], aliases={7: 0, 8: 1} if ends else None,
         )

time: 110 us -> 111 us (level)
  starting transfers between devices: 31.1 us -> 28.5 us
  waiting for transfers between devices: 5.99 us -> 7.68 us
  blocking collectives: 48.5 us -> 49.8 us
    ppermute x8 -> x9, starting transfers between devices: 20.1 us -> 16.9 us  [flipped(): return lax.ppermute(array, axis, [(i, i ^ flip) for i in range(4)])]
    ppermute x8 -> x9, waiting for transfers between devices: 4.28 us -> 5.9 us  [flipped(): return lax.ppermute(array, axis, [(i, i ^ flip) for i in range(4)])]
    all_to_all x4, blocking collectives: 48.5 us -> 49.8 us  [spread(): return lax.all_to_all(array, PLANE, 0, 0, tiled=True)]
    pallas_call x21 -> x22, Pallas kernels: 22.5 us -> 23.2 us  [call(): pl.pallas_call(kernel, out_shape=out, in_specs=specs or [SMEM] * smem + [...]
  transfers between devices with their start and end apart: 12 -> 13, of which waited for: 7 -> 8; matrix products, arithmetic and copies ran while one was open for 0% -> 0% of each run, Pallas kernels for 15% -> 15%
where the time goes in v3:
time: 111 us; the launch traced here: 110 us
  blocking collectives  49.8 us (45%)
  starting transfers between devices  28.5 us (26%)
  Pallas kernels  23.2 us (21%)
  waiting for transfers between devices  7.68 us (7%)
    all_to_all x4, blocking collectives, spread(): return lax.all_to_all(array, PLANE, 0, 0, tiled=True)  49.8 us
    pallas_call x22, Pallas kernels, call(): pl.pallas_call(kernel, out_shape=out, in_specs=specs or [SMEM] * smem + [...  23.2 us
    ppermute x9, starting transfers between devices, flipped(): return lax.ppermute(array, axis, [(i, i ^ flip) for i in range(4)])  16.9 us
    ppermute x4, starting transfers between devices, swap(): return lax.ppermute(array, 'core', [(0, 1), (1, 0)])  11.5 us
    ppermute x9, waiting for transfers between devices, flipped(): return lax.ppermute(array, axis, [(i, i ^ flip) for i in range(4)])  5.9 us
  transfers between devices with their start and end apart: 13, of which 8 were waited for; matrix products, arithmetic and copies ran while one was open for 0% of the time, Pallas kernels for 15%

profile of v3, /device:TPU:1, one launch (start us, length us, event | category | flops | bytes accessed | tf_op | source)
XLA Modules:
  0.0 110.2 jit_solution(11355752150595641443)
XLA Ops:
  0.6 2.4 %first.1 = (f32[256,128]{1,0:T(8,128)S(1)}, f32[16,256]{1,0:T(8,128)S(1)}, f32[1032,128]{1,0:T(8,128)S(1)}, bf16[256,2048]{1,0:T(8,128)(2,1)S(1)}, bf16[256,2048]{1,0:T(8,128)(2,1)S(1)}) custom-call(s32[1]{0:T(128)} %bitcast.core_ref, bf16[256,2048]{1,0:T(8,128)(2,1)} %keys_hbm.1, bf16[256,2048]{1,0:T(8,128)(2,1)} %value_hbm.1, f32[16,256]{1,0:T(8,128)} %bitcast.7), custom_call_target="tpu_custom_call" | custom-call | flops 67108864 | bytes 6983684 | tf_op jit(solution)/shard_map/first/pallas_call | solution.py:28
  3.0 3.3 %collective-permute-start = (f32[1032,128]{1,0:T(8,128)S(1)}, f32[1032,128]{1,0:T(8,128)S(1)}, u32[]{:S(2)}, u32[]{:S(2)}) collective-permute-start(f32[1032,128]{1,0:T(8,128)S(1)} %get-tuple-element.83), channel_id=1, source_target_pairs={{0,4},{4,0},{1,5},{5,1},{2,6},{6,2},{3,7},{7,3},{8,12},{12,8},{9,1... | collective-permute-start | bytes 1585160 | tf_op jit(solution)/shard_map/ppermute | solution.py:377
  6.4 0.9 second.1.own_ref
  7.3 0.0 copy-start
  7.3 0.0 copy-start.1
  7.3 0.0 copy-start.2
  7.3 0.0 copy-start.3
  7.3 0.6 collective-permute-done.other_ref
  7.9 0.2 merge_f.1
  8.1 13.9 %all_to_all.20.parts_ref.decays_ref = f32[8,136,128]{2,1,0:T(8,128)S(1)} all-to-all(f32[8,136,128]{2,1,0:T(8,128)S(1)} %get-tuple-element.84), channel_id=1, replica_groups=mesh['z1'=4,'z0'=2,'y'=4,'core'=2,'head'=4] {'z0','y'}, dimensions={0} | all-to-all | bytes 1114112 | tf_op jit(solution)/shard_map/all_to_all | solution.py:385
  22.0 3.1 %collective-permute-start.1 = (f32[136,128]{1,0:T(8,128)S(1)}, f32[136,128]{1,0:T(8,128)S(1)}, u32[]{:S(2)}, u32[]{:S(2)}) collective-permute-start(f32[136,128]{1,0:T(8,128)S(1)} %row_total.2), channel_id=1, source_target_pairs={{0,64},{64,0},{128,192},{192,128},{1,65},{65,1},{129,193},{193,129... | collective-permute-start | bytes 208904 | tf_op jit(solution)/shard_map/ppermute | solution.py:381
  25.1 4.2 %collective-permute-start.2 = (f32[136,128]{1,0:T(8,128)S(1)}, f32[136,128]{1,0:T(8,128)S(1)}, u32[]{:S(2)}, u32[]{:S(2)}) collective-permute-start(f32[136,128]{1,0:T(8,128)S(1)} %row_total.2), channel_id=1, source_target_pairs={{0,128},{64,192},{128,0},{192,64},{1,129},{65,193},{129,1},{193,65... | collective-permute-start | bytes 208904 | tf_op jit(solution)/shard_map/ppermute | solution.py:381
  29.4 1.3 %intra1.1 = (f32[256,1024]{1,0:T(8,128)S(1)}, f32[256,1024]{1,0:T(8,128)S(1)}, bf16[8,256,256]{2,1,0:T(8,128)(2,1)S(1)}, f32[8,3,128,128]{3,2,1,0:T(8,128)S(1)}) custom-call(s32[1]{0:T(128)} %bitcast.core_ref, bf16[256,2048]{1,0:T(8,128)(2,1)S(1)} %copy-done, bf16[256,2048]{1,0:T(8,128)(2,1)S(1)} %get-tuple-element.80.keys_ref, ...), custom_call_target="tpu_custom_call" | custom-call | flops 268435456 | bytes 11165700 | tf_op jit(solution)/shard_map/intra1/pallas_call | solution.py:28
  30.7 1.3 %intra0.1 = (f32[256,1024]{1,0:T(8,128)S(1)}, f32[256,1024]{1,0:T(8,128)S(1)}, bf16[8,256,256]{2,1,0:T(8,128)(2,1)S(1)}, f32[8,3,128,128]{3,2,1,0:T(8,128)S(1)}) custom-call(s32[1]{0:T(128)} %bitcast.core_ref, bf16[256,2048]{1,0:T(8,128)(2,1)S(1)} %copy-done, bf16[256,2048]{1,0:T(8,128)(2,1)S(1)} %get-tuple-element.80.keys_ref, ...), custom_call_target="tpu_custom_call" | custom-call | flops 268435456 | bytes 11165700 | tf_op jit(solution)/shard_map/intra0/pallas_call | solution.py:28
  32.1 0.0 collective-permute-done.1.one_ref
  32.1 0.3 collective-permute-done.2.two_ref
  32.4 3.2 %collective-permute-done.3.three_ref = f32[136,128]{1,0:T(8,128)S(1)} collective-permute-done((f32[136,128]{1,0:T(8,128)S(1)}, f32[136,128]{1,0:T(8,128)S(1)}, u32[]{:S(2)}, u32[]{:S(2)}) %collective-permute-start.3) | collective-permute-done | bytes 69664 | tf_op jit(solution)/shard_map/ppermute | solution.py:381
  35.6 0.1 enter.2
  35.6 13.3 %all_to_all.21.enter_ref = f32[8,128,128]{2,1,0:T(8,128)S(1)} all-to-all(f32[8,128,128]{2,1,0:T(8,128)S(1)} %enter.2), channel_id=1, replica_groups=mesh['z1'=4,'z0'=2,'y'=4,'core'=2,'head'=4] {'z0','y'}, dimensions={0} | all-to-all | bytes 1048576 | tf_op jit(solution)/shard_map/all_to_all | solution.py:385
  49.0 0.1 leave.2
  49.1 2.5 %collective-permute-start.4 = (f32[8,128,128]{2,1,0:T(8,128)S(1)}, f32[8,128,128]{2,1,0:T(8,128)S(1)}, u32[]{:S(2)}, u32[]{:S(2)}) collective-permute-start(f32[8,128,128]{2,1,0:T(8,128)S(1)} %get-tuple-element.103), channel_id=1, source_target_pairs={{0,4},{4,0},{1,5},{5,1},{2,6},{6,2},{3,7},{7,3},{8,12},{12,8},{9,1... | collective-permute-start | bytes 1572872 | tf_op jit(solution)/shard_map/ppermute | solution.py:377
  51.6 0.8 attend0.1
  52.4 0.7 collective-permute-done.4.state_ref
  53.2 0.8 attend1.1
  54.0 1.2 %collective-permute-start.5 = (f32[8,256]{1,0:T(8,128)S(1)}, f32[8,256]{1,0:T(8,128)S(1)}, u32[]{:S(2)}, u32[]{:S(2)}) collective-permute-start(f32[8,256]{1,0:T(8,128)S(1)} %get-tuple-element.108.sum_a), channel_id=1, source_target_pairs={{0,1},{1,0},{2,3},{3,2},{4,5},{5,4},{6,7},{7,6},{8,9},{9,8},{10,11... | collective-permute-start | bytes 24584 | tf_op jit(solution)/shard_map/ppermute | solution.py:381
  55.3 2.5 %collective-permute-start.6 = (f32[8,256]{1,0:T(8,128)S(1)}, f32[8,256]{1,0:T(8,128)S(1)}, u32[]{:S(2)}, u32[]{:S(2)}) collective-permute-start(f32[8,256]{1,0:T(8,128)S(1)} %get-tuple-element.108.sum_a), channel_id=1, source_target_pairs={{0,2},{1,3},{2,0},{3,1},{4,6},{5,7},{6,4},{7,5},{8,10},{9,11},{10,... | collective-permute-start | bytes 24584 | tf_op jit(solution)/shard_map/ppermute | solution.py:381
  57.7 0.2 collective-permute-start.7
  57.9 1.1 %opened.1 = (f32[256,2048]{1,0:T(8,128)S(1)}, f32[256,2048]{1,0:T(8,128)S(1)}) custom-call(s32[1]{0:T(128)} %bitcast.core_ref, bf16[256,2048]{1,0:T(8,128)(2,1)S(1)} %copy-done.1, f32[1,2048]{1,0:T(1,128)S(1)} %bitcast.6, bf16[256,2048]{1,0:T(8,128)(2,1)S(1)} %copy-done.2, f32[256,1024]{1,0:T(8,128)S(1)} %get-tuple-element.102.own_ref.attention_ref, ...), custom_call_target="tpu_custom_call" | custom-call | bytes 10493956 | tf_op jit(solution)/shard_map/opened/pallas_call | solution.py:28
  59.0 0.2 collective-permute-done.6.sum_c
  59.3 2.2 %collective-permute-done.7.sum_d = f32[8,256]{1,0:T(8,128)S(1)} collective-permute-done((f32[8,256]{1,0:T(8,128)S(1)}, f32[8,256]{1,0:T(8,128)S(1)}, u32[]{:S(2)}, u32[]{:S(2)}) %collective-permute-start.7) | collective-permute-done | bytes 8224 | tf_op jit(solution)/shard_map/ppermute | solution.py:381
  61.4 1.3 %grad1.1 = (bf16[256,1024]{1,0:T(8,128)(2,1)S(1)}, f32[1024,128]{1,0:T(8,128)S(1)}, f32[256,128]{1,0:T(8,128)S(1)}) custom-call(s32[1]{0:T(128)} %bitcast.core_ref, bf16[256,2048]{1,0:T(8,128)(2,1)S(1)} %copy-done, f32[256,1024]{1,0:T(8,128)S(1)} %get-tuple-element.107.other_ref.attention_ref, f32[256,1024]{1,0:T(8,128)S(1)} %get-tuple-element.105.normed_ref.other_normed, ...), custom_call_target="tpu_custom_call" | custom-call | flops 67108864 | bytes 5013508 | tf_op jit(solution)/shard_map/grad1/pallas_call | solution.py:28
  62.8 2.2 %collective-permute-start.8 = (f32[1024,128]{1,0:T(8,128)S(1)}, f32[1024,128]{1,0:T(8,128)S(1)}, u32[]{:S(2)}, u32[]{:S(2)}) collective-permute-start(f32[1024,128]{1,0:T(8,128)S(1)} %get-tuple-element.116), channel_id=1, source_target_pairs={{0,4},{4,0},{1,5},{5,1},{2,6},{6,2},{3,7},{7,3},{8,12},{12,8},{9,1... | collective-permute-start | bytes 1572872 | tf_op jit(solution)/shard_map/ppermute | solution.py:377
  64.9 1.2 %grad0.1 = (bf16[256,1024]{1,0:T(8,128)(2,1)S(1)}, f32[1024,128]{1,0:T(8,128)S(1)}) custom-call(s32[1]{0:T(128)} %bitcast.core_ref, bf16[256,2048]{1,0:T(8,128)(2,1)S(1)} %copy-done, f32[256,1024]{1,0:T(8,128)S(1)} %get-tuple-element.102.own_ref.attention_ref, f32[256,1024]{1,0:T(8,128)S(1)} %get-tuple-element.101.normed_ref.own_normed, ...), custom_call_target="tpu_custom_call" | custom-call | flops 67108864 | bytes 4980740 | tf_op jit(solution)/shard_map/grad0/pallas_call | solution.py:28
  66.1 0.4 collective-permute-done.8.other_ref
  66.5 0.1 merge_b.1
  66.6 11.1 %all_to_all.22.parts_ref = f32[8,128,128]{2,1,0:T(8,128)S(1)} all-to-all(f32[8,128,128]{2,1,0:T(8,128)S(1)} %merge_b.1), channel_id=1, replica_groups=mesh['z1'=4,'z0'=2,'y'=4,'core'=2,'head'=4] {'z0','y'}, dimensions={0} | all-to-all | bytes 1048576 | tf_op jit(solution)/shard_map/all_to_all | solution.py:385
  77.7 3.6 %collective-permute-start.10 = (f32[136,128]{1,0:T(8,128)S(1)}, f32[136,128]{1,0:T(8,128)S(1)}, u32[]{:S(2)}, u32[]{:S(2)}) collective-permute-start(f32[136,128]{1,0:T(8,128)S(1)} %row_total.3), channel_id=1, source_target_pairs={{0,128},{64,192},{128,0},{192,64},{1,129},{65,193},{129,1},{193,65... | collective-permute-start | bytes 208904 | tf_op jit(solution)/shard_map/ppermute | solution.py:381
  81.3 2.2 %collective-permute-start.9 = (f32[136,128]{1,0:T(8,128)S(1)}, f32[136,128]{1,0:T(8,128)S(1)}, u32[]{:S(2)}, u32[]{:S(2)}) collective-permute-start(f32[136,128]{1,0:T(8,128)S(1)} %row_total.3), channel_id=1, source_target_pairs={{0,64},{64,0},{128,192},{192,128},{1,65},{65,1},{129,193},{193,129... | collective-permute-start | bytes 208904 | tf_op jit(solution)/shard_map/ppermute | solution.py:381
  83.5 3.3 %inner0.1 = (bf16[256,2048]{1,0:T(8,128)(2,1)}, f32[256,1024]{1,0:T(8,128)S(1)}, f32[256,1024]{1,0:T(8,128)S(1)}) custom-call(s32[1]{0:T(128)} %bitcast.core_ref, bf16[256,2048]{1,0:T(8,128)(2,1)S(1)} %copy-done, bf16[256,2048]{1,0:T(8,128)(2,1)S(1)} %get-tuple-element.80.keys_ref, bf16[256,2048]{1,0:T(8,128)(2,1)S(1)} %get-tuple-element.81.value_ref, ...), custom_call_target="tpu_custom_call" | custom-call | flops 671088640 | bytes 11141124 | tf_op jit(solution)/shard_map/inner0/pallas_call | solution.py:28
  86.8 1.7 %gates.1 = (bf16[256,2048]{1,0:T(8,128)(2,1)}, bf16[256,2048]{1,0:T(8,128)(2,1)}) custom-call(s32[1]{0:T(128)} %bitcast.core_ref, f32[256,2048]{1,0:T(8,128)S(1)} %get-tuple-element.130.mixed_ref, f32[256,2048]{1,0:T(8,128)S(1)} %get-tuple-element.131.gate_ref, f32[256,128]{1,0:T(8,128)S(1)} %get-tuple-element.132.terms_ref), custom_call_target="tpu_custom_call" | custom-call | bytes 8519684 | tf_op jit(solution)/shard_map/gates/pallas_call | solution.py:28
  88.5 3.3 %inner1.1 = (bf16[256,2048]{1,0:T(8,128)(2,1)}, f32[256,1024]{1,0:T(8,128)S(1)}, f32[256,1024]{1,0:T(8,128)S(1)}) custom-call(s32[1]{0:T(128)} %bitcast.core_ref, bf16[256,2048]{1,0:T(8,128)(2,1)S(1)} %copy-done, bf16[256,2048]{1,0:T(8,128)(2,1)S(1)} %get-tuple-element.80.keys_ref, ...), custom_call_target="tpu_custom_call", output_to_operand_aliasing={{0}: (9, {})} | custom-call | flops 671088640 | bytes 12189700 | tf_op jit(solution)/shard_map/inner1/pallas_call | solution.py:28
  91.9 0.1 enter.3
  91.9 11.5 %all_to_all.23.enter_ref = f32[8,128,128]{2,1,0:T(8,128)S(1)} all-to-all(f32[8,128,128]{2,1,0:T(8,128)S(1)} %enter.3), channel_id=1, replica_groups=mesh['z1'=4,'z0'=2,'y'=4,'core'=2,'head'=4] {'z0','y'}, dimensions={0} | all-to-all | bytes 1048576 | tf_op jit(solution)/shard_map/all_to_all | solution.py:385
  103.4 0.1 leave.3
  103.5 3.5 %collective-permute-start.12 = (f32[8,128,128]{2,1,0:T(8,128)S(1)}, f32[8,128,128]{2,1,0:T(8,128)S(1)}, u32[]{:S(2)}, u32[]{:S(2)}) collective-permute-start(f32[8,128,128]{2,1,0:T(8,128)S(1)} %get-tuple-element.140), channel_id=1, source_target_pairs={{0,4},{4,0},{1,5},{5,1},{2,6},{6,2},{3,7},{7,3},{8,12},{12,8},{9,1... | collective-permute-start | bytes 1572872 | tf_op jit(solution)/shard_map/ppermute | solution.py:377
  107.1 1.4 %last0.1 = (bf16[256,2048]{1,0:T(8,128)(2,1)}, bf16[256,2048]{1,0:T(8,128)(2,1)}) custom-call(s32[1]{0:T(128)} %bitcast.core_ref, bf16[256,2048]{1,0:T(8,128)(2,1)S(1)} %get-tuple-element.80.keys_ref, bf16[256,2048]{1,0:T(8,128)(2,1)S(1)} %get-tuple-element.81.value_ref, f32[8,128,128]{2,1,0:T(8,128)S(1)} %get-tuple-element.143.state_ref, ...), custom_call_target="tpu_custom_call" | custom-call | flops 134217728 | bytes 9043972 | tf_op jit(solution)/shard_map/last0/pallas_call | solution.py:28
  108.5 0.1 collective-permute-done.12.state_ref
  108.6 1.4 %last1.1 = (bf16[256,2048]{1,0:T(8,128)(2,1)}, bf16[256,2048]{1,0:T(8,128)(2,1)}) custom-call(s32[1]{0:T(128)} %bitcast.core_ref, bf16[256,2048]{1,0:T(8,128)(2,1)S(1)} %get-tuple-element.80.keys_ref, bf16[256,2048]{1,0:T(8,128)(2,1)S(1)} %get-tuple-element.81.value_ref, ...), custom_call_target="tpu_custom_call", output_to_operand_aliasing={{0}: (7, {}), {1}: (8, {})} | custom-call | flops 134217728 | bytes 11141124 | tf_op jit(solution)/shard_map/last1/pallas_call | solution.py:28
  (12 shorter events, 0.1 us)
Async XLA Ops:
  3.0 4.9 %collective-permute-start = (f32[1032,128]{1,0:T(8,128)S(1)}, f32[1032,128]{1,0:T(8,128)S(1)}, u32[]{:S(2)}, u32[]{:S(2)}) collective-permute-start(f32[1032,128]{1,0:T(8,128)S(1)} %get-tuple-element.83), channel_id=1, source_target_pairs={{0,4},{4,0},{1,5},{5,1},{2,6},{6,2},{3,7},{7,3},{8,12},{12,8},{9,1... | collective-permute-start | bytes 1585160 | tf_op jit(solution)/shard_map/ppermute | solution.py:377
  7.3 22.0 %copy-start = (bf16[256,2048]{1,0:T(8,128)(2,1)S(1)}, bf16[256,2048]{1,0:T(8,128)(2,1)}, u32[]{:S(2)}) copy-start(bf16[256,2048]{1,0:T(8,128)(2,1)} %query_ref.11) | copy-start | bytes 3145732
  7.3 22.0 %copy-start.1 = (bf16[256,2048]{1,0:T(8,128)(2,1)S(1)}, bf16[256,2048]{1,0:T(8,128)(2,1)}, u32[]{:S(2)}) copy-start(bf16[256,2048]{1,0:T(8,128)(2,1)} %gate_ref.5) | copy-start | bytes 3145732
  7.3 22.0 %copy-start.2 = (bf16[256,2048]{1,0:T(8,128)(2,1)S(1)}, bf16[256,2048]{1,0:T(8,128)(2,1)}, u32[]{:S(2)}) copy-start(bf16[256,2048]{1,0:T(8,128)(2,1)} %upstream_ref.1) | copy-start | bytes 3145732
  7.3 22.0 %copy-start.3 = (f32[2048]{0:T(1024)S(1)}, f32[2048]{0:T(1024)}, u32[]{:S(2)}) copy-start(f32[2048]{0:T(1024)} %param.12) | copy-start | bytes 24580
  22.0 10.0 %collective-permute-start.1 = (f32[136,128]{1,0:T(8,128)S(1)}, f32[136,128]{1,0:T(8,128)S(1)}, u32[]{:S(2)}, u32[]{:S(2)}) collective-permute-start(f32[136,128]{1,0:T(8,128)S(1)} %row_total.2), channel_id=1, source_target_pairs={{0,64},{64,0},{128,192},{192,128},{1,65},{65,1},{129,193},{193,129... | collective-permute-start | bytes 208904 | tf_op jit(solution)/shard_map/ppermute | solution.py:381
  25.1 7.3 %collective-permute-start.2 = (f32[136,128]{1,0:T(8,128)S(1)}, f32[136,128]{1,0:T(8,128)S(1)}, u32[]{:S(2)}, u32[]{:S(2)}) collective-permute-start(f32[136,128]{1,0:T(8,128)S(1)} %row_total.2), channel_id=1, source_target_pairs={{0,128},{64,192},{128,0},{192,64},{1,129},{65,193},{129,1},{193,65... | collective-permute-start | bytes 208904 | tf_op jit(solution)/shard_map/ppermute | solution.py:381
  29.3 6.2 %collective-permute-start.3 = (f32[136,128]{1,0:T(8,128)S(1)}, f32[136,128]{1,0:T(8,128)S(1)}, u32[]{:S(2)}, u32[]{:S(2)}) collective-permute-start(f32[136,128]{1,0:T(8,128)S(1)} %row_total.2), channel_id=1, source_target_pairs={{0,192},{64,128},{128,64},{192,0},{1,193},{65,129},{129,65},{193,1... | collective-permute-start | bytes 208904 | tf_op jit(solution)/shard_map/ppermute | solution.py:381
  49.1 4.1 %collective-permute-start.4 = (f32[8,128,128]{2,1,0:T(8,128)S(1)}, f32[8,128,128]{2,1,0:T(8,128)S(1)}, u32[]{:S(2)}, u32[]{:S(2)}) collective-permute-start(f32[8,128,128]{2,1,0:T(8,128)S(1)} %get-tuple-element.103), channel_id=1, source_target_pairs={{0,4},{4,0},{1,5},{5,1},{2,6},{6,2},{3,7},{7,3},{8,12},{12,8},{9,1... | collective-permute-start | bytes 1572872 | tf_op jit(solution)/shard_map/ppermute | solution.py:377
  54.0 5.0 %collective-permute-start.5 = (f32[8,256]{1,0:T(8,128)S(1)}, f32[8,256]{1,0:T(8,128)S(1)}, u32[]{:S(2)}, u32[]{:S(2)}) collective-permute-start(f32[8,256]{1,0:T(8,128)S(1)} %get-tuple-element.108.sum_a), channel_id=1, source_target_pairs={{0,1},{1,0},{2,3},{3,2},{4,5},{5,4},{6,7},{7,6},{8,9},{9,8},{10,11... | collective-permute-start | bytes 24584 | tf_op jit(solution)/shard_map/ppermute | solution.py:381
  55.3 4.0 %collective-permute-start.6 = (f32[8,256]{1,0:T(8,128)S(1)}, f32[8,256]{1,0:T(8,128)S(1)}, u32[]{:S(2)}, u32[]{:S(2)}) collective-permute-start(f32[8,256]{1,0:T(8,128)S(1)} %get-tuple-element.108.sum_a), channel_id=1, source_target_pairs={{0,2},{1,3},{2,0},{3,1},{4,6},{5,7},{6,4},{7,5},{8,10},{9,11},{10,... | collective-permute-start | bytes 24584 | tf_op jit(solution)/shard_map/ppermute | solution.py:381
  57.7 3.7 %collective-permute-start.7 = (f32[8,256]{1,0:T(8,128)S(1)}, f32[8,256]{1,0:T(8,128)S(1)}, u32[]{:S(2)}, u32[]{:S(2)}) collective-permute-start(f32[8,256]{1,0:T(8,128)S(1)} %get-tuple-element.108.sum_a), channel_id=1, source_target_pairs={{0,3},{1,2},{2,1},{3,0},{4,7},{5,6},{6,5},{7,4},{8,11},{9,10},{10,... | collective-permute-start | bytes 24584 | tf_op jit(solution)/shard_map/ppermute | solution.py:381
  62.8 3.7 %collective-permute-start.8 = (f32[1024,128]{1,0:T(8,128)S(1)}, f32[1024,128]{1,0:T(8,128)S(1)}, u32[]{:S(2)}, u32[]{:S(2)}) collective-permute-start(f32[1024,128]{1,0:T(8,128)S(1)} %get-tuple-element.116), channel_id=1, source_target_pairs={{0,4},{4,0},{1,5},{5,1},{2,6},{6,2},{3,7},{7,3},{8,12},{12,8},{9,1... | collective-permute-start | bytes 1572872 | tf_op jit(solution)/shard_map/ppermute | solution.py:377
  77.7 14.1 %collective-permute-start.10 = (f32[136,128]{1,0:T(8,128)S(1)}, f32[136,128]{1,0:T(8,128)S(1)}, u32[]{:S(2)}, u32[]{:S(2)}) collective-permute-start(f32[136,128]{1,0:T(8,128)S(1)} %row_total.3), channel_id=1, source_target_pairs={{0,128},{64,192},{128,0},{192,64},{1,129},{65,193},{129,1},{193,65... | collective-permute-start | bytes 208904 | tf_op jit(solution)/shard_map/ppermute | solution.py:381
  81.3 10.5 %collective-permute-start.11 = (f32[136,128]{1,0:T(8,128)S(1)}, f32[136,128]{1,0:T(8,128)S(1)}, u32[]{:S(2)}, u32[]{:S(2)}) collective-permute-start(f32[136,128]{1,0:T(8,128)S(1)} %row_total.3), channel_id=1, source_target_pairs={{0,192},{64,128},{128,64},{192,0},{1,193},{65,129},{129,65},{193,1... | collective-permute-start | bytes 208904 | tf_op jit(solution)/shard_map/ppermute | solution.py:381
  81.3 10.5 %collective-permute-start.9 = (f32[136,128]{1,0:T(8,128)S(1)}, f32[136,128]{1,0:T(8,128)S(1)}, u32[]{:S(2)}, u32[]{:S(2)}) collective-permute-start(f32[136,128]{1,0:T(8,128)S(1)} %row_total.3), channel_id=1, source_target_pairs={{0,64},{64,0},{128,192},{192,128},{1,65},{65,1},{129,193},{193,129... | collective-permute-start | bytes 208904 | tf_op jit(solution)/shard_map/ppermute | solution.py:381
  103.5 5.1 %collective-permute-start.12 = (f32[8,128,128]{2,1,0:T(8,128)S(1)}, f32[8,128,128]{2,1,0:T(8,128)S(1)}, u32[]{:S(2)}, u32[]{:S(2)}) collective-permute-start(f32[8,128,128]{2,1,0:T(8,128)S(1)} %get-tuple-element.140), channel_id=1, source_target_pairs={{0,4},{4,0},{1,5},{5,1},{2,6},{6,2},{3,7},{7,3},{8,12},{12,8},{9,1... | collective-permute-start | bytes 1572872 | tf_op jit(solution)/shard_map/ppermute | solution.py:377

commit v4 on v3

--- a/solution.py
+++ b/solution.py
@@ -48,6 +48,13 @@
     )
 
 
+def turned(x):
+    n = x.shape[1]
+    rows = lax.broadcasted_iota(jnp.int32, (n, n), 0)
+    cols = lax.broadcasted_iota(jnp.int32, (n, n), 1)
+    return dot((rows == cols).astype(BF16), x, 1, 1).astype(BF16)
+
+
 def columns(role, core, i):
     side = core if role == 0 else 1 - core
     return pl.ds(pl.multiple_of(side * WIDE + i * DH, DH), DH)
@@ -61,19 +68,21 @@
 def tables(core, decays):
     rows = lax.broadcasted_iota(jnp.int32, (GROUP, GROUP), 0)
     cols = lax.broadcasted_iota(jnp.int32, (GROUP, GROUP), 1)
-    tri = (rows >= cols).astype(F32)
-    down = dot(tri, decays, 1, 1, lax.Precision.HIGHEST)
-    across = dot(decays, tri, 1, 1, lax.Precision.HIGHEST)
-    swapped = jnp.concatenate([down[:, HALF:], down[:, :HALF]], axis=1)
-    down = jnp.where(core == 0, down, swapped)
+    tri = (rows >= cols).astype(BF16)
+    high = decays.astype(BF16)
+    rest = decays - high.astype(F32)
+    middle = rest.astype(BF16)
+    low = (rest - middle.astype(F32)).astype(BF16)
+    across = dot(jnp.concatenate([high, middle, low], axis=0), tri, 1, 1)
+    across = across[:16] + (across[16:32] + across[32:])
     across = jnp.where(core == 0, across, jnp.concatenate([across[HALF:], across[:HALF]], axis=0))
-    return down, across
+    return across.T, across
 
 
 def state_term(core, role, i, keys_ref, value_ref, tab):
     at = columns(role, core, i)
     keyed = (keys_ref[:, at].astype(F32) * lanes(tab, 2, role, i)).astype(BF16)
-    return dot(keyed, value_ref[:, at], 0, 0)
+    return dot(turned(keyed), value_ref[:, at], 1, 0)
 
 
 def first_kernel(
@@ -181,47 +190,59 @@
 LOW, HIGH = slice(0, DH), slice(DH, GROUP)
 
 
-def causal(low, first, second):
-    return jnp.concatenate(
-        [jnp.concatenate([low, jnp.zeros_like(low)], axis=1), jnp.concatenate([first, second], axis=1)], axis=0
-    )
+def causal(first, middle, last, upper=False):
+    blank = jnp.zeros_like(first)
+    top, bottom = ([first, middle], [blank, last]) if upper else ([first, blank], [middle, last])
+    return jnp.concatenate([jnp.concatenate(top, axis=1), jnp.concatenate(bottom, axis=1)], axis=0)
+
+
+def masked(array, weights, upper=False):
+    middle = array[LOW, HIGH] if upper else array[HIGH, LOW]
+    parts = (array[LOW, LOW], middle, array[HIGH, HIGH])
+    return causal(*((part * weights[at]).astype(BF16) for at, part in enumerate(parts)), upper=upper)
 
 
 def intra_kernel(
     role, core_ref, query_ref, keys_ref, value_ref, gate_ref, gain_ref, mixed_ref, tab_ref, across_ref,
-    intra_ref, normed_ref, probs_ref, weights_ref,
+    intra_ref, normed_ref, turned_ref, weights_ref,
 ):
     core = core_ref[0]
     tab = tab_ref[...]
     rows = lax.broadcasted_iota(jnp.int32, (DH, DH), 0)
     cols = lax.broadcasted_iota(jnp.int32, (DH, DH), 1)
-    lower = rows >= cols
+    lower, upper = rows >= cols, rows <= cols
     for i in range(HALF):
         at = columns(role, core, i)
         to = slice(i * DH, (i + 1) * DH)
         query, keys = query_ref[:, at], keys_ref[:, at]
         down = lanes(tab, 0, role, i)
         across = across_ref[role * HALF + i : role * HALF + i + 1, :]
-        first = jnp.exp(jnp.where(lower, down[LOW] - across[:, LOW], -jnp.inf))
-        second = jnp.exp(down[HIGH] - across[:, LOW])
-        third = jnp.exp(jnp.where(lower, down[HIGH] - across[:, HIGH], -jnp.inf))
-        weights_ref[i, 0], weights_ref[i, 1], weights_ref[i, 2] = first, second, third
-        above = dot(query[LOW], keys[LOW], 1, 1)
-        below = dot(query[HIGH], keys, 1, 1)
-        probs = causal(
-            (above * first).astype(BF16), (below[:, LOW] * second).astype(BF16), (below[:, HIGH] * third).astype(BF16)
+        weights = (
+            jnp.exp(jnp.where(lower, down[LOW] - across[:, LOW], -jnp.inf)),
+            jnp.exp(down[HIGH] - across[:, LOW]),
+            jnp.exp(jnp.where(lower, down[HIGH] - across[:, HIGH], -jnp.inf)),
+            jnp.exp(jnp.where(upper, across[:, LOW] - down[LOW], -jnp.inf)),
+            jnp.exp(across[:, HIGH] - down[LOW]),
+            jnp.exp(jnp.where(upper, across[:, HIGH] - down[HIGH], -jnp.inf)),
         )
-        probs_ref[i] = probs
+        for part, array in enumerate(weights):
+            weights_ref[i, part] = array
+        probs = masked(dot(query, keys, 1, 1), weights[:3])
+        turned_ref[i] = masked(dot(keys, query, 1, 1), weights[3:], upper=True)
         intra_ref[:, to] = dot(probs, value_ref[:, at], 1, 0)
         opening = jax.nn.sigmoid(gate_ref[:, at].astype(F32))
         normed_ref[:, to] = mixed_ref[:, at].astype(F32) * opening * gain_ref[:, at]
 
 
-def attend_kernel(role, core_ref, query_ref, state_ref, intra_ref, normed_ref, tab_ref, sums_ref, out_ref, add_ref):
+def attend_kernel(role, core_ref, query_ref, state_ref, intra_ref, normed_ref, tab_ref, *refs):
+    if role == 0:
+        out_ref, squares_ref, products_ref = refs
+        squares, products = jnp.zeros((GROUP, DH), F32), jnp.zeros((GROUP, DH), F32)
+    else:
+        squares_in, products_in, out_ref, sums_ref = refs
+        squares, products = squares_in[...], products_in[...]
     core = core_ref[0]
     tab = tab_ref[...]
-    squares = jnp.zeros((GROUP, DH), F32)
-    products = jnp.zeros((GROUP, DH), F32)
     for i in range(HALF):
         at = columns(role, core, i)
         to = slice(i * DH, (i + 1) * DH)
@@ -230,12 +251,12 @@
         out_ref[:, to] = attention
         squares = squares + attention * attention
         products = products + normed_ref[:, to] * attention
-    ones = jnp.ones((8, DH), F32)
-    squares = dot(ones, squares, 1, 1, lax.Precision.HIGHEST)
-    products = dot(ones, products, 1, 1, lax.Precision.HIGHEST)
-    row = lax.broadcasted_iota(jnp.int32, (8, GROUP), 0)
-    both = jnp.where(row == 0, squares, products)
-    add_ref[...] = both if sums_ref is None else sums_ref[...] + both
+    if role == 0:
+        squares_ref[...] = squares
+        products_ref[...] = products
+    else:
+        both = [jnp.sum(array.T, axis=0, keepdims=True) for array in (squares, products)]
+        sums_ref[...] = jnp.concatenate(both + [jnp.zeros((6, GROUP), F32)], axis=0)
 
 
 def norm_terms(sums, terms_ref):
@@ -255,7 +276,7 @@
         grad = (scale * (normed_ref[:, to] - attention_ref[:, to] * shift)).astype(BF16)
         grad_ref[:, to] = grad
         weighted = (query_ref[:, at].astype(F32) * lanes(tab, 1, role, i)).astype(BF16)
-        term_ref[i * DH : (i + 1) * DH, :] = dot(weighted, grad, 0, 0)
+        term_ref[i * DH : (i + 1) * DH, :] = dot(turned(weighted), grad, 1, 0)
 
 
 def grad_first(
@@ -284,32 +305,59 @@
             copy.wait()
 
 
-def inner_kernel(
-    role, core_ref, query_ref, keys_ref, value_ref, state_ref, grad_ref, probs_ref, weights_ref, tab_ref, *refs
-):
-    query_out, keys_out, value_out, query_buf, sems = refs[-5:]
-    core = core_ref[0]
-    tab = tab_ref[...]
-    sender = Sender(role, core, sems)
+def inner_part(
+    role, core, query_ref, keys_ref, value_ref, state_ref, grad_ref, turned_ref, weights_ref, tab, keys_out, value_out,
+    query_buf, sender, query_out,
+):
     for i in range(HALF):
         at = columns(role, core, i)
         to = slice(i * DH, (i + 1) * DH)
         query, keys, value, grad = query_ref[:, at], keys_ref[:, at], value_ref[:, at], grad_ref[:, to]
-        above = dot(grad[LOW], value[LOW], 1, 1)
-        below = dot(grad[HIGH], value, 1, 1)
-        grad_scores = causal(
-            (above * weights_ref[i, 0]).astype(BF16),
-            (below[:, LOW] * weights_ref[i, 1]).astype(BF16),
-            (below[:, HIGH] * weights_ref[i, 2]).astype(BF16),
-        )
-        grad_query = dot(grad_scores, keys, 1, 0)
+        weights = [weights_ref[i, part] for part in range(6)]
+        scores = masked(dot(grad, value, 1, 1), weights[:3])
+        flipped_scores = masked(dot(value, grad, 1, 1), weights[3:], upper=True)
+        grad_query = dot(scores, keys, 1, 0)
         grad_query = grad_query + dot(grad, state_ref[i].astype(BF16), 1, 1) * lanes(tab, 1, role, i)
         query_buf[:, to] = grad_query.astype(BF16)
-        keys_out[:, to] = dot(grad_scores, query, 0, 0)
-        value_out[:, to] = dot(probs_ref[i], grad, 0, 0)
+        keys_out[:, to] = dot(flipped_scores, query, 1, 0)
+        value_out[:, to] = dot(turned_ref[i], grad, 1, 0)
         if i % 2 == 1:
             sender.send(query_buf, query_out, (i - 1) * DH, 2 * DH)
-    sender.wait()
+
+
+def local_kernel(
+    core_ref, query_ref, keys_ref, value_ref, own_state, other_state, own_grad, other_grad, own_turned, own_weights,
+    other_turned, other_weights, tab_ref, mixed_ref, gate_ref, terms_ref,
+    query_out, mixed_out, gate_out, own_keys, own_value, other_keys, other_value,
+    query_own, query_other, mixed_own, mixed_other, gate_own, gate_other, sems,
+):
+    core = core_ref[0]
+    tab = tab_ref[...]
+    scale = terms_ref[:, 0:1]
+    senders = [Sender(role, core, sems.at[role]) for role in (0, 1)]
+
+    def gates(role, mixed_buf, gate_buf):
+        for i in range(HALF):
+            to = slice(i * DH, (i + 1) * DH)
+            into = slice(role * WIDE + i * DH, role * WIDE + (i + 1) * DH)
+            mixed_buf[:, to] = (mixed_ref[:, into] * scale).astype(BF16)
+            gate_buf[:, to] = (gate_ref[:, into] * scale).astype(BF16)
+            if i % 4 == 3:
+                senders[role].send(mixed_buf, mixed_out, (i - 3) * DH, 4 * DH)
+                senders[role].send(gate_buf, gate_out, (i - 3) * DH, 4 * DH)
+
+    gates(0, mixed_own, gate_own)
+    gates(1, mixed_other, gate_other)
+    inner_part(
+        0, core, query_ref, keys_ref, value_ref, own_state, own_grad, own_turned, own_weights, tab, own_keys, own_value,
+        query_own, senders[0], query_out,
+    )
+    inner_part(
+        1, core, query_ref, keys_ref, value_ref, other_state, other_grad, other_turned, other_weights, tab, other_keys,
+        other_value, query_other, senders[1], query_out,
+    )
+    for sender in senders:
+        sender.wait()
 
 
 def opened_kernel(
@@ -325,30 +373,6 @@
             attention = ref[:, to]
             mixed_ref[:, into] = attention * (gain_ref[:, at] * opening)
             gate_out[:, into] = normed_ref[:, to] * (attention * (1.0 - opening))
-
-
-def gate_kernel(core_ref, mixed_ref, gate_ref, terms_ref, mixed_out, gate_out, mixed_buf, gate_buf, sems):
-    core = core_ref[0]
-    scale = terms_ref[:, 0:1]
-    for role in (0, 1):
-        sender = Sender(role, core, sems.at[role])
-        for i in range(HALF):
-            into = slice(role * WIDE + i * DH, role * WIDE + (i + 1) * DH)
-            mixed_buf[:, into] = (mixed_ref[:, into] * scale).astype(BF16)
-            gate_buf[:, into] = (gate_ref[:, into] * scale).astype(BF16)
-            if i % 4 == 3:
-                start = role * WIDE + (i - 3) * DH
-                for buf, out in ((mixed_buf, mixed_out), (gate_buf, gate_out)):
-                    part = pl.ds(pl.multiple_of(sender.side * WIDE + (i - 3) * DH, 4 * DH), 4 * DH)
-                    copy = pltpu.make_async_copy(
-                        buf.at[:, start : start + 4 * DH], out.at[:, part], sems.at[role, len(sender.copies)]
-                    )
-                    copy.start()
-                    sender.copies.append(copy)
-        if role == 0:
-            held = sender
-    held.wait()
-    sender.wait()
 
 
 def last_kernel(
@@ -432,7 +456,7 @@
 
     wide = shape(GROUP, WIDE)
     probs_shape = shape(HALF, GROUP, GROUP, dtype=BF16)
-    weights_shape = shape(HALF, 3, DH, DH)
+    weights_shape = shape(HALF, 6, DH, DH)
 
     def intra_parts(after):
         held, _ = lax.optimization_barrier((query, after))
@@ -448,16 +472,14 @@
         core, place, own, other, tab, None, None, False, intra_parts
     )
 
-    def attend_first(core_ref, query_ref, state_ref, intra_ref, normed_ref, tab_ref, out_ref, add_ref):
-        attend_kernel(0, core_ref, query_ref, state_ref, intra_ref, normed_ref, tab_ref, None, out_ref, add_ref)
-
-    sums_shape = shape(8, GROUP)
-    att_own, sums = call(
-        attend_first, (wide, sums_shape), core, query, state_own, *intra[0][:2], tab, flops=small, name="attend0"
+    narrow = shape(GROUP, DH)
+    att_own, *partial = call(
+        functools.partial(attend_kernel, 0), (wide, narrow, narrow),
+        core, query, state_own, *intra[0][:2], tab, flops=small, name="attend0",
     )
     att_other, sums = call(
-        functools.partial(attend_kernel, 1), (wide, sums_shape),
-        core, query, state_other, *intra[1][:2], tab, sums, flops=small, name="attend1",
+        functools.partial(attend_kernel, 1), (wide, shape(8, GROUP)),
+        core, query, state_other, *intra[1][:2], tab, *partial, flops=small, name="attend1",
     )
     opened = call(
         opened_kernel, (shape(GROUP, 2 * WIDE), shape(GROUP, 2 * WIDE)),
@@ -477,35 +499,25 @@
         flops=small, name="grad0",
     )
 
-    def inner_parts(after):
+    half = pltpu.VMEM((GROUP, WIDE), BF16)
+
+    def local(after):
         held, factors, _ = lax.optimization_barrier((query, terms, after))
-        inner, queries = [], ()
-        for role, state, grad in ((0, state_own, grad_own), (1, state_other, grad_other)):
-            results = call(
-                functools.partial(inner_kernel, role), (pltpu.HBM((GROUP, 2 * WIDE), BF16), wide, wide),
-                core, held, keys, value, state, grad, *intra[role][2:], tab, *queries,
-                flops=5 * big, name=f"inner{role}",
-                specs=[SMEM] + [VMEM] * 8 + [HBM] * len(queries), outs=(HBM, VMEM, VMEM),
-                scratch=[pltpu.VMEM((GROUP, WIDE), BF16), pltpu.SemaphoreType.DMA((4,))],
-                aliases={9: 0} if queries else None,
-            )
-            queries = results[:1]
-            inner.append(results[1:])
-        whole = pltpu.VMEM((GROUP, 2 * WIDE), BF16)
-        return inner, queries[0], call(
-            gate_kernel, (full, full), core, *opened, factors, name="gates", outs=(HBM, HBM),
-            scratch=[whole, whole, pltpu.SemaphoreType.DMA((2, 4))],
+        return call(
+            local_kernel, (full, full, full, wide, wide, wide, wide),
+            core, held, keys, value, state_own, state_other, grad_own, grad_other, *intra[0][2:], *intra[1][2:], tab,
+            *opened, factors, flops=10 * big, name="local", limit=14,
+            outs=(HBM, HBM, HBM, VMEM, VMEM, VMEM, VMEM), scratch=[half] * 6 + [pltpu.SemaphoreType.DMA((2, 8))],
         )
 
-    after_own, after_other, _, _, (inner, grad_query, (mixed, grad_gate)) = scan(
-        core, place, term_own, term_other, tab, dec, decays, True, inner_parts
-    )
-    half = pltpu.VMEM((GROUP, WIDE), BF16)
+    after_own, after_other, _, _, (grad_query, mixed, grad_gate, *inner) = scan(
+        core, place, term_own, term_other, tab, dec, decays, True, local
+    )
     ends = ()
     for role, state in ((0, after_own), (1, after_other)):
         ends = call(
             functools.partial(last_kernel, role), (full, full),
-            core, keys, value, state, *inner[role], tab, *ends, flops=2 * small, name=f"last{role}",
+            core, keys, value, state, *inner[2 * role : 2 * role + 2], tab, *ends, flops=2 * small, name=f"last{role}",
             specs=[SMEM] + [VMEM] * 6 + [HBM] * len(ends), outs=(HBM, HBM),
             scratch=[half, half, pltpu.SemaphoreType.DMA((8,))], aliases={7: 0, 8: 1} if ends else None,
         )

time: 111 us -> 107 us (0.964)
  Pallas kernels: 23.2 us -> 18.7 us
    pallas_call x22 -> x20, Pallas kernels: 23.2 us -> 18.7 us  [call(): pl.pallas_call(kernel, out_shape=out, in_specs=specs or [SMEM] * smem + [...]
  transfers between devices with their start and end apart: 13 -> 13, of which waited for: 8 -> 7; matrix products, arithmetic and copies ran while one was open for 0% -> 0% of each run, Pallas kernels for 15% -> 12%
where the time goes in v4:
time: 107 us; the launch traced here: 106 us
  blocking collectives  49.2 us (46%)
  starting transfers between devices  29.4 us (27%)
  Pallas kernels  18.7 us (17%)
  waiting for transfers between devices  7.95 us (7%)
    all_to_all x4, blocking collectives, spread(): return lax.all_to_all(array, PLANE, 0, 0, tiled=True)  49.2 us
    pallas_call x20, Pallas kernels, call(): pl.pallas_call(kernel, out_shape=out, in_specs=specs or [SMEM] * smem + [...  18.7 us
    ppermute x9, starting transfers between devices, flipped(): return lax.ppermute(array, axis, [(i, i ^ flip) for i in range(4)])  17.1 us
    ppermute x4, starting transfers between devices, swap(): return lax.ppermute(array, 'core', [(0, 1), (1, 0)])  12.2 us
    ppermute x9, waiting for transfers between devices, flipped(): return lax.ppermute(array, axis, [(i, i ^ flip) for i in range(4)])  5.37 us
    ppermute x4, waiting for transfers between devices, swap(): return lax.ppermute(array, 'core', [(0, 1), (1, 0)])  2.58 us
  transfers between devices with their start and end apart: 13, of which 7 were waited for; matrix products, arithmetic and copies ran while one was open for 0% of the time, Pallas kernels for 12%

profile of v4, /device:TPU:1, one launch (start us, length us, event | category | flops | bytes accessed | tf_op | source)
XLA Modules:
  0.0 106.2 jit_solution(12043637827908948628)
XLA Ops:
  0.6 1.9 %first.1 = (f32[256,128]{1,0:T(8,128)S(1)}, f32[16,256]{1,0:T(8,128)S(1)}, f32[1032,128]{1,0:T(8,128)S(1)}, bf16[256,2048]{1,0:T(8,128)(2,1)S(1)}, bf16[256,2048]{1,0:T(8,128)(2,1)S(1)}) custom-call(s32[1]{0:T(128)} %bitcast.core_ref, bf16[256,2048]{1,0:T(8,128)(2,1)} %keys_hbm.1, bf16[256,2048]{1,0:T(8,128)(2,1)} %value_hbm.1, f32[16,256]{1,0:T(8,128)} %bitcast.7), custom_call_target="tpu_custom_call" | custom-call | flops 67108864 | bytes 6983684 | tf_op jit(solution)/shard_map/first/pallas_call | solution.py:28
  2.5 0.0 copy-start
  2.5 0.0 copy-start.1
  2.6 0.0 copy-start.2
  2.6 0.0 copy-start.3
  2.6 3.3 %collective-permute-start = (f32[1032,128]{1,0:T(8,128)S(1)}, f32[1032,128]{1,0:T(8,128)S(1)}, u32[]{:S(2)}, u32[]{:S(2)}) collective-permute-start(f32[1032,128]{1,0:T(8,128)S(1)} %get-tuple-element.83), channel_id=1, source_target_pairs={{0,4},{4,0},{1,5},{5,1},{2,6},{6,2},{3,7},{7,3},{8,12},{12,8},{9,1... | collective-permute-start | bytes 1585160 | tf_op jit(solution)/shard_map/ppermute | solution.py:401
  5.9 0.7 second.1.own_ref
  6.7 0.8 collective-permute-done.other_ref
  7.5 0.2 merge_f.1
  7.7 13.6 %all_to_all.20.parts_ref.decays_ref = f32[8,136,128]{2,1,0:T(8,128)S(1)} all-to-all(f32[8,136,128]{2,1,0:T(8,128)S(1)} %get-tuple-element.84), channel_id=1, replica_groups=mesh['z1'=4,'z0'=2,'y'=4,'core'=2,'head'=4] {'z0','y'}, dimensions={0} | all-to-all | bytes 1114112 | tf_op jit(solution)/shard_map/all_to_all | solution.py:409
  21.3 5.2 %collective-permute-start.3 = (f32[136,128]{1,0:T(8,128)S(1)}, f32[136,128]{1,0:T(8,128)S(1)}, u32[]{:S(2)}, u32[]{:S(2)}) collective-permute-start(f32[136,128]{1,0:T(8,128)S(1)} %row_total.2), channel_id=1, source_target_pairs={{0,192},{64,128},{128,64},{192,0},{1,193},{65,129},{129,65},{193,1... | collective-permute-start | bytes 208904 | tf_op jit(solution)/shard_map/ppermute | solution.py:405
  26.5 1.2 %collective-permute-start.2 = (f32[136,128]{1,0:T(8,128)S(1)}, f32[136,128]{1,0:T(8,128)S(1)}, u32[]{:S(2)}, u32[]{:S(2)}) collective-permute-start(f32[136,128]{1,0:T(8,128)S(1)} %row_total.2), channel_id=1, source_target_pairs={{0,128},{64,192},{128,0},{192,64},{1,129},{65,193},{129,1},{193,65... | collective-permute-start | bytes 208904 | tf_op jit(solution)/shard_map/ppermute | solution.py:405
  27.7 1.0 collective-permute-start.1
  28.7 1.7 %intra1.1 = (f32[256,1024]{1,0:T(8,128)S(1)}, f32[256,1024]{1,0:T(8,128)S(1)}, bf16[8,256,256]{2,1,0:T(8,128)(2,1)S(1)}, f32[8,6,128,128]{3,2,1,0:T(8,128)S(1)}) custom-call(s32[1]{0:T(128)} %bitcast.core_ref, bf16[256,2048]{1,0:T(8,128)(2,1)S(1)} %copy-done, bf16[256,2048]{1,0:T(8,128)(2,1)S(1)} %get-tuple-element.80.keys_ref, ...), custom_call_target="tpu_custom_call" | custom-call | flops 268435456 | bytes 12738564 | tf_op jit(solution)/shard_map/intra1/pallas_call | solution.py:28
  30.4 1.7 %intra0.1 = (f32[256,1024]{1,0:T(8,128)S(1)}, f32[256,1024]{1,0:T(8,128)S(1)}, bf16[8,256,256]{2,1,0:T(8,128)(2,1)S(1)}, f32[8,6,128,128]{3,2,1,0:T(8,128)S(1)}) custom-call(s32[1]{0:T(128)} %bitcast.core_ref, bf16[256,2048]{1,0:T(8,128)(2,1)S(1)} %copy-done, bf16[256,2048]{1,0:T(8,128)(2,1)S(1)} %get-tuple-element.80.keys_ref, ...), custom_call_target="tpu_custom_call" | custom-call | flops 268435456 | bytes 12738564 | tf_op jit(solution)/shard_map/intra0/pallas_call | solution.py:28
  32.1 0.0 collective-permute-done.3.three_ref
  32.1 2.6 %collective-permute-done.2.two_ref = f32[136,128]{1,0:T(8,128)S(1)} collective-permute-done((f32[136,128]{1,0:T(8,128)S(1)}, f32[136,128]{1,0:T(8,128)S(1)}, u32[]{:S(2)}, u32[]{:S(2)}) %collective-permute-start.2) | collective-permute-done | bytes 69664 | tf_op jit(solution)/shard_map/ppermute | solution.py:405
  34.7 0.0 collective-permute-done.1.one_ref
  34.7 0.1 enter.2
  34.8 9.9 %all_to_all.21.enter_ref = f32[8,128,128]{2,1,0:T(8,128)S(1)} all-to-all(f32[8,128,128]{2,1,0:T(8,128)S(1)} %enter.2), channel_id=1, replica_groups=mesh['z1'=4,'z0'=2,'y'=4,'core'=2,'head'=4] {'z0','y'}, dimensions={0} | all-to-all | bytes 1048576 | tf_op jit(solution)/shard_map/all_to_all | solution.py:409
  44.7 0.1 leave.2
  44.8 4.4 %collective-permute-start.4 = (f32[8,128,128]{2,1,0:T(8,128)S(1)}, f32[8,128,128]{2,1,0:T(8,128)S(1)}, u32[]{:S(2)}, u32[]{:S(2)}) collective-permute-start(f32[8,128,128]{2,1,0:T(8,128)S(1)} %get-tuple-element.103), channel_id=1, source_target_pairs={{0,4},{4,0},{1,5},{5,1},{2,6},{6,2},{3,7},{7,3},{8,12},{12,8},{9,1... | collective-permute-start | bytes 1572872 | tf_op jit(solution)/shard_map/ppermute | solution.py:401
  49.3 0.5 attend0.1
  49.8 1.0 collective-permute-done.4.state_ref.other_state
  50.8 0.7 attend1.1
  51.5 2.6 %collective-permute-start.7 = (f32[8,256]{1,0:T(8,128)S(1)}, f32[8,256]{1,0:T(8,128)S(1)}, u32[]{:S(2)}, u32[]{:S(2)}) collective-permute-start(f32[8,256]{1,0:T(8,128)S(1)} %get-tuple-element.109.sum_a), channel_id=1, source_target_pairs={{0,3},{1,2},{2,1},{3,0},{4,7},{5,6},{6,5},{7,4},{8,11},{9,10},{10,... | collective-permute-start | bytes 24584 | tf_op jit(solution)/shard_map/ppermute | solution.py:405
  54.0 0.5 collective-permute-start.6
  54.6 0.3 collective-permute-start.5
  54.8 0.9 opened.1
  55.8 2.3 %collective-permute-done.6.sum_c = f32[8,256]{1,0:T(8,128)S(1)} collective-permute-done((f32[8,256]{1,0:T(8,128)S(1)}, f32[8,256]{1,0:T(8,128)S(1)}, u32[]{:S(2)}, u32[]{:S(2)}) %collective-permute-start.6) | collective-permute-done | bytes 8224 | tf_op jit(solution)/shard_map/ppermute | solution.py:405
  58.1 1.0 grad1.1
  59.0 1.9 %collective-permute-start.8 = (f32[1024,128]{1,0:T(8,128)S(1)}, f32[1024,128]{1,0:T(8,128)S(1)}, u32[]{:S(2)}, u32[]{:S(2)}) collective-permute-start(f32[1024,128]{1,0:T(8,128)S(1)} %get-tuple-element.117), channel_id=1, source_target_pairs={{0,4},{4,0},{1,5},{5,1},{2,6},{6,2},{3,7},{7,3},{8,12},{12,8},{9,1... | collective-permute-start | bytes 1572872 | tf_op jit(solution)/shard_map/ppermute | solution.py:401
  60.9 0.9 grad0.1
  61.8 0.7 collective-permute-done.8.other_ref
  62.5 0.1 merge_b.1
  62.6 11.1 %all_to_all.22.parts_ref = f32[8,128,128]{2,1,0:T(8,128)S(1)} all-to-all(f32[8,128,128]{2,1,0:T(8,128)S(1)} %merge_b.1), channel_id=1, replica_groups=mesh['z1'=4,'z0'=2,'y'=4,'core'=2,'head'=4] {'z0','y'}, dimensions={0} | all-to-all | bytes 1048576 | tf_op jit(solution)/shard_map/all_to_all | solution.py:409
  73.7 4.2 %collective-permute-start.11 = (f32[136,128]{1,0:T(8,128)S(1)}, f32[136,128]{1,0:T(8,128)S(1)}, u32[]{:S(2)}, u32[]{:S(2)}) collective-permute-start(f32[136,128]{1,0:T(8,128)S(1)} %row_total.3), channel_id=1, source_target_pairs={{0,192},{64,128},{128,64},{192,0},{1,193},{65,129},{129,65},{193,1... | collective-permute-start | bytes 208904 | tf_op jit(solution)/shard_map/ppermute | solution.py:405
  77.9 0.6 collective-permute-start.10
  78.5 1.6 %collective-permute-start.9 = (f32[136,128]{1,0:T(8,128)S(1)}, f32[136,128]{1,0:T(8,128)S(1)}, u32[]{:S(2)}, u32[]{:S(2)}) collective-permute-start(f32[136,128]{1,0:T(8,128)S(1)} %row_total.3), channel_id=1, source_target_pairs={{0,64},{64,0},{128,192},{192,128},{1,65},{65,1},{129,193},{193,129... | collective-permute-start | bytes 208904 | tf_op jit(solution)/shard_map/ppermute | solution.py:405
  80.1 5.0 %local.1 = (bf16[256,2048]{1,0:T(8,128)(2,1)}, bf16[256,2048]{1,0:T(8,128)(2,1)}, bf16[256,2048]{1,0:T(8,128)(2,1)}, f32[256,1024]{1,0:T(8,128)S(1)}, f32[256,10...) custom-call(s32[1]{0:T(128)} %bitcast.core_ref, bf16[256,2048]{1,0:T(8,128)(2,1)S(1)} %copy-done, ...), custom_call_target="tpu_custom_call" | custom-call | flops 1342177280 | bytes 28573700 | tf_op jit(solution)/shard_map/local/pallas_call | solution.py:28
  85.2 0.5 collective-permute-done.10.two_ref
  85.7 0.1 enter.3
  85.7 14.6 %all_to_all.23.enter_ref = f32[8,128,128]{2,1,0:T(8,128)S(1)} all-to-all(f32[8,128,128]{2,1,0:T(8,128)S(1)} %enter.3), channel_id=1, replica_groups=mesh['z1'=4,'z0'=2,'y'=4,'core'=2,'head'=4] {'z0','y'}, dimensions={0} | all-to-all | bytes 1048576 | tf_op jit(solution)/shard_map/all_to_all | solution.py:409
  100.4 0.1 leave.3
  100.5 2.6 %collective-permute-start.12 = (f32[8,128,128]{2,1,0:T(8,128)S(1)}, f32[8,128,128]{2,1,0:T(8,128)S(1)}, u32[]{:S(2)}, u32[]{:S(2)}) collective-permute-start(f32[8,128,128]{2,1,0:T(8,128)S(1)} %get-tuple-element.140), channel_id=1, source_target_pairs={{0,4},{4,0},{1,5},{5,1},{2,6},{6,2},{3,7},{7,3},{8,12},{12,8},{9,1... | collective-permute-start | bytes 1572872 | tf_op jit(solution)/shard_map/ppermute | solution.py:401
  103.1 1.4 %last0.1 = (bf16[256,2048]{1,0:T(8,128)(2,1)}, bf16[256,2048]{1,0:T(8,128)(2,1)}) custom-call(s32[1]{0:T(128)} %bitcast.core_ref, bf16[256,2048]{1,0:T(8,128)(2,1)S(1)} %get-tuple-element.80.keys_ref, bf16[256,2048]{1,0:T(8,128)(2,1)S(1)} %get-tuple-element.81.value_ref, f32[8,128,128]{2,1,0:T(8,128)S(1)} %get-tuple-element.143.state_ref, ...), custom_call_target="tpu_custom_call" | custom-call | flops 134217728 | bytes 9043972 | tf_op jit(solution)/shard_map/last0/pallas_call | solution.py:28
  104.5 0.1 collective-permute-done.12.state_ref
  104.6 1.4 %last1.1 = (bf16[256,2048]{1,0:T(8,128)(2,1)}, bf16[256,2048]{1,0:T(8,128)(2,1)}) custom-call(s32[1]{0:T(128)} %bitcast.core_ref, bf16[256,2048]{1,0:T(8,128)(2,1)S(1)} %get-tuple-element.80.keys_ref, bf16[256,2048]{1,0:T(8,128)(2,1)S(1)} %get-tuple-element.81.value_ref, ...), custom_call_target="tpu_custom_call", output_to_operand_aliasing={{0}: (7, {}), {1}: (8, {})} | custom-call | flops 134217728 | bytes 11141124 | tf_op jit(solution)/shard_map/last1/pallas_call | solution.py:28
  (10 shorter events, 0.1 us)
Async XLA Ops:
  2.5 26.2 %copy-start = (bf16[256,2048]{1,0:T(8,128)(2,1)S(1)}, bf16[256,2048]{1,0:T(8,128)(2,1)}, u32[]{:S(2)}) copy-start(bf16[256,2048]{1,0:T(8,128)(2,1)} %query_ref.10) | copy-start | bytes 3145732
  2.5 26.2 %copy-start.1 = (bf16[256,2048]{1,0:T(8,128)(2,1)S(1)}, bf16[256,2048]{1,0:T(8,128)(2,1)}, u32[]{:S(2)}) copy-start(bf16[256,2048]{1,0:T(8,128)(2,1)} %gate_ref.5) | copy-start | bytes 3145732
  2.6 26.2 %copy-start.2 = (bf16[256,2048]{1,0:T(8,128)(2,1)S(1)}, bf16[256,2048]{1,0:T(8,128)(2,1)}, u32[]{:S(2)}) copy-start(bf16[256,2048]{1,0:T(8,128)(2,1)} %upstream_ref.1) | copy-start | bytes 3145732
  2.6 26.2 %copy-start.3 = (f32[2048]{0:T(1024)S(1)}, f32[2048]{0:T(1024)}, u32[]{:S(2)}) copy-start(f32[2048]{0:T(1024)} %param.12) | copy-start | bytes 24580
  2.6 4.9 %collective-permute-start = (f32[1032,128]{1,0:T(8,128)S(1)}, f32[1032,128]{1,0:T(8,128)S(1)}, u32[]{:S(2)}, u32[]{:S(2)}) collective-permute-start(f32[1032,128]{1,0:T(8,128)S(1)} %get-tuple-element.83), channel_id=1, source_target_pairs={{0,4},{4,0},{1,5},{5,1},{2,6},{6,2},{3,7},{7,3},{8,12},{12,8},{9,1... | collective-permute-start | bytes 1585160 | tf_op jit(solution)/shard_map/ppermute | solution.py:401
  21.3 10.8 %collective-permute-start.3 = (f32[136,128]{1,0:T(8,128)S(1)}, f32[136,128]{1,0:T(8,128)S(1)}, u32[]{:S(2)}, u32[]{:S(2)}) collective-permute-start(f32[136,128]{1,0:T(8,128)S(1)} %row_total.2), channel_id=1, source_target_pairs={{0,192},{64,128},{128,64},{192,0},{1,193},{65,129},{129,65},{193,1... | collective-permute-start | bytes 208904 | tf_op jit(solution)/shard_map/ppermute | solution.py:405
  26.5 8.2 %collective-permute-start.2 = (f32[136,128]{1,0:T(8,128)S(1)}, f32[136,128]{1,0:T(8,128)S(1)}, u32[]{:S(2)}, u32[]{:S(2)}) collective-permute-start(f32[136,128]{1,0:T(8,128)S(1)} %row_total.2), channel_id=1, source_target_pairs={{0,128},{64,192},{128,0},{192,64},{1,129},{65,193},{129,1},{193,65... | collective-permute-start | bytes 208904 | tf_op jit(solution)/shard_map/ppermute | solution.py:405
  27.7 7.0 %collective-permute-start.1 = (f32[136,128]{1,0:T(8,128)S(1)}, f32[136,128]{1,0:T(8,128)S(1)}, u32[]{:S(2)}, u32[]{:S(2)}) collective-permute-start(f32[136,128]{1,0:T(8,128)S(1)} %row_total.2), channel_id=1, source_target_pairs={{0,64},{64,0},{128,192},{192,128},{1,65},{65,1},{129,193},{193,129... | collective-permute-start | bytes 208904 | tf_op jit(solution)/shard_map/ppermute | solution.py:405
  44.8 6.0 %collective-permute-start.4 = (f32[8,128,128]{2,1,0:T(8,128)S(1)}, f32[8,128,128]{2,1,0:T(8,128)S(1)}, u32[]{:S(2)}, u32[]{:S(2)}) collective-permute-start(f32[8,128,128]{2,1,0:T(8,128)S(1)} %get-tuple-element.103), channel_id=1, source_target_pairs={{0,4},{4,0},{1,5},{5,1},{2,6},{6,2},{3,7},{7,3},{8,12},{12,8},{9,1... | collective-permute-start | bytes 1572872 | tf_op jit(solution)/shard_map/ppermute | solution.py:401
  51.5 4.3 %collective-permute-start.7 = (f32[8,256]{1,0:T(8,128)S(1)}, f32[8,256]{1,0:T(8,128)S(1)}, u32[]{:S(2)}, u32[]{:S(2)}) collective-permute-start(f32[8,256]{1,0:T(8,128)S(1)} %get-tuple-element.109.sum_a), channel_id=1, source_target_pairs={{0,3},{1,2},{2,1},{3,0},{4,7},{5,6},{6,5},{7,4},{8,11},{9,10},{10,... | collective-permute-start | bytes 24584 | tf_op jit(solution)/shard_map/ppermute | solution.py:405
  54.0 4.0 %collective-permute-start.6 = (f32[8,256]{1,0:T(8,128)S(1)}, f32[8,256]{1,0:T(8,128)S(1)}, u32[]{:S(2)}, u32[]{:S(2)}) collective-permute-start(f32[8,256]{1,0:T(8,128)S(1)} %get-tuple-element.109.sum_a), channel_id=1, source_target_pairs={{0,2},{1,3},{2,0},{3,1},{4,6},{5,7},{6,4},{7,5},{8,10},{9,11},{10,... | collective-permute-start | bytes 24584 | tf_op jit(solution)/shard_map/ppermute | solution.py:405
  54.6 3.5 %collective-permute-start.5 = (f32[8,256]{1,0:T(8,128)S(1)}, f32[8,256]{1,0:T(8,128)S(1)}, u32[]{:S(2)}, u32[]{:S(2)}) collective-permute-start(f32[8,256]{1,0:T(8,128)S(1)} %get-tuple-element.109.sum_a), channel_id=1, source_target_pairs={{0,1},{1,0},{2,3},{3,2},{4,5},{5,4},{6,7},{7,6},{8,9},{9,8},{10,11... | collective-permute-start | bytes 24584 | tf_op jit(solution)/shard_map/ppermute | solution.py:405
  59.0 3.4 %collective-permute-start.8 = (f32[1024,128]{1,0:T(8,128)S(1)}, f32[1024,128]{1,0:T(8,128)S(1)}, u32[]{:S(2)}, u32[]{:S(2)}) collective-permute-start(f32[1024,128]{1,0:T(8,128)S(1)} %get-tuple-element.117), channel_id=1, source_target_pairs={{0,4},{4,0},{1,5},{5,1},{2,6},{6,2},{3,7},{7,3},{8,12},{12,8},{9,1... | collective-permute-start | bytes 1572872 | tf_op jit(solution)/shard_map/ppermute | solution.py:401
  73.7 11.4 %collective-permute-start.11 = (f32[136,128]{1,0:T(8,128)S(1)}, f32[136,128]{1,0:T(8,128)S(1)}, u32[]{:S(2)}, u32[]{:S(2)}) collective-permute-start(f32[136,128]{1,0:T(8,128)S(1)} %row_total.3), channel_id=1, source_target_pairs={{0,192},{64,128},{128,64},{192,0},{1,193},{65,129},{129,65},{193,1... | collective-permute-start | bytes 208904 | tf_op jit(solution)/shard_map/ppermute | solution.py:405
  77.9 7.7 %collective-permute-start.10 = (f32[136,128]{1,0:T(8,128)S(1)}, f32[136,128]{1,0:T(8,128)S(1)}, u32[]{:S(2)}, u32[]{:S(2)}) collective-permute-start(f32[136,128]{1,0:T(8,128)S(1)} %row_total.3), channel_id=1, source_target_pairs={{0,128},{64,192},{128,0},{192,64},{1,129},{65,193},{129,1},{193,65... | collective-permute-start | bytes 208904 | tf_op jit(solution)/shard_map/ppermute | solution.py:405
  78.5 7.2 %collective-permute-start.9 = (f32[136,128]{1,0:T(8,128)S(1)}, f32[136,128]{1,0:T(8,128)S(1)}, u32[]{:S(2)}, u32[]{:S(2)}) collective-permute-start(f32[136,128]{1,0:T(8,128)S(1)} %row_total.3), channel_id=1, source_target_pairs={{0,64},{64,0},{128,192},{192,128},{1,65},{65,1},{129,193},{193,129... | collective-permute-start | bytes 208904 | tf_op jit(solution)/shard_map/ppermute | solution.py:405
  100.5 4.1 %collective-permute-start.12 = (f32[8,128,128]{2,1,0:T(8,128)S(1)}, f32[8,128,128]{2,1,0:T(8,128)S(1)}, u32[]{:S(2)}, u32[]{:S(2)}) collective-permute-start(f32[8,128,128]{2,1,0:T(8,128)S(1)} %get-tuple-element.140), channel_id=1, source_target_pairs={{0,4},{4,0},{1,5},{5,1},{2,6},{6,2},{3,7},{7,3},{8,12},{12,8},{9,1... | collective-permute-start | bytes 1572872 | tf_op jit(solution)/shard_map/ppermute | solution.py:401

commit v5 on v4

--- a/solution.py
+++ b/solution.py
@@ -158,15 +158,19 @@
     out_ref[DH:, :] = decay
 
 
-def enter_kernel(reverse, place_ref, parts_ref, decays_ref, one_ref, two_ref, three_ref, out_ref):
+def pair_kernel(reverse, place_ref, own_ref, near_ref, out_ref):
     place = 3 - place_ref[0] if reverse else place_ref[0]
-    one, two, three = one_ref[...], two_ref[...], three_ref[...]
-    far = jnp.where(place >= 2, jnp.where(place == 2, two, three), 0.0)
-    mid = jnp.where(place >= 2, jnp.where(place == 2, three, two), 0.0)
-    near = jnp.where((place == 1) | (place == 3), one, 0.0)
-    state = far[:DH, :]
-    for part in (mid, near):
-        state = jnp.exp(part[DH : DH + 1, :]) * state + part[:DH, :]
+    even = (place == 0) | (place == 2)
+    own, near = own_ref[...], near_ref[...]
+    first, second = jnp.where(even, own, near), jnp.where(even, near, own)
+    out_ref[...] = jnp.exp(second[DH : DH + 1, :]) * first[:DH, :] + second[:DH, :]
+
+
+def enter_kernel(reverse, place_ref, parts_ref, decays_ref, near_ref, far_ref, out_ref):
+    place = 3 - place_ref[0] if reverse else place_ref[0]
+    near = jnp.where((place == 1) | (place == 3), near_ref[...], 0.0)
+    state = jnp.where(place >= 2, far_ref[...], 0.0)
+    state = jnp.exp(near[DH : DH + 1, :]) * state + near[:DH, :]
     order = list(range(8))[:: -1 if reverse else 1]
     for at in order:
         out_ref[at] = state
@@ -326,38 +330,27 @@
 
 
 def local_kernel(
-    core_ref, query_ref, keys_ref, value_ref, own_state, other_state, own_grad, other_grad, own_turned, own_weights,
-    other_turned, other_weights, tab_ref, mixed_ref, gate_ref, terms_ref,
-    query_out, mixed_out, gate_out, own_keys, own_value, other_keys, other_value,
-    query_own, query_other, mixed_own, mixed_other, gate_own, gate_other, sems,
-):
+    role, core_ref, query_ref, keys_ref, value_ref, state_ref, grad_ref, turned_ref, weights_ref, tab_ref, mixed_ref,
+    gate_ref, terms_ref, *refs
+):
+    query_out, mixed_out, gate_out, keys_out, value_out, query_buf, mixed_buf, gate_buf, sems = refs[-9:]
     core = core_ref[0]
     tab = tab_ref[...]
     scale = terms_ref[:, 0:1]
-    senders = [Sender(role, core, sems.at[role]) for role in (0, 1)]
-
-    def gates(role, mixed_buf, gate_buf):
-        for i in range(HALF):
-            to = slice(i * DH, (i + 1) * DH)
-            into = slice(role * WIDE + i * DH, role * WIDE + (i + 1) * DH)
-            mixed_buf[:, to] = (mixed_ref[:, into] * scale).astype(BF16)
-            gate_buf[:, to] = (gate_ref[:, into] * scale).astype(BF16)
-            if i % 4 == 3:
-                senders[role].send(mixed_buf, mixed_out, (i - 3) * DH, 4 * DH)
-                senders[role].send(gate_buf, gate_out, (i - 3) * DH, 4 * DH)
-
-    gates(0, mixed_own, gate_own)
-    gates(1, mixed_other, gate_other)
+    sender = Sender(role, core, sems)
+    for i in range(HALF):
+        to = slice(i * DH, (i + 1) * DH)
+        into = slice(role * WIDE + i * DH, role * WIDE + (i + 1) * DH)
+        mixed_buf[:, to] = (mixed_ref[:, into] * scale).astype(BF16)
+        gate_buf[:, to] = (gate_ref[:, into] * scale).astype(BF16)
+        if i % 4 == 3:
+            sender.send(mixed_buf, mixed_out, (i - 3) * DH, 4 * DH)
+            sender.send(gate_buf, gate_out, (i - 3) * DH, 4 * DH)
     inner_part(
-        0, core, query_ref, keys_ref, value_ref, own_state, own_grad, own_turned, own_weights, tab, own_keys, own_value,
-        query_own, senders[0], query_out,
-    )
-    inner_part(
-        1, core, query_ref, keys_ref, value_ref, other_state, other_grad, other_turned, other_weights, tab, other_keys,
-        other_value, query_other, senders[1], query_out,
-    )
-    for sender in senders:
-        sender.wait()
+        role, core, query_ref, keys_ref, value_ref, state_ref, grad_ref, turned_ref, weights_ref, tab, keys_out, value_out,
+        query_buf, sender, query_out,
+    )
+    sender.wait()
 
 
 def opened_kernel(
@@ -421,10 +414,11 @@
     row = call(
         functools.partial(total_kernel, reverse), shape(DH + 8, DH), parts, decays, smem=0, name="row_total"
     )
-    moved = [flipped(row, "z1", flip) for flip in (1, 2, 3)]
-    moved, beside = lax.optimization_barrier((moved, beside(row)))
+    near, done = lax.optimization_barrier((flipped(row, "z1", 1), beside(row, 0, ())))
+    pair = call(functools.partial(pair_kernel, reverse), shape(DH, DH), place, row, near, name="pair")
+    far, done = lax.optimization_barrier((flipped(pair, "z1", 3), beside(pair, 1, done)))
     entering = call(
-        functools.partial(enter_kernel, reverse), shape(8, DH, DH), place, parts, decays, *moved, name="enter"
+        functools.partial(enter_kernel, reverse), shape(8, DH, DH), place, parts, decays, near, far, name="enter"
     )
     entering = spread(entering)
     keep, send = call(
@@ -432,7 +426,7 @@
         (shape(HALF, DH, DH), shape(HALF, DH, DH)),
         core, entering, own, other, dec, name="leave",
     )
-    return keep, swap(send), dec, decays, beside
+    return keep, swap(send), dec, decays, done
 
 
 def on_device(query, keys, value, gate, decay, gain, upstream):
@@ -458,18 +452,16 @@
     probs_shape = shape(HALF, GROUP, GROUP, dtype=BF16)
     weights_shape = shape(HALF, 6, DH, DH)
 
-    def intra_parts(after):
+    def intra_part(after, role, done):
         held, _ = lax.optimization_barrier((query, after))
-        return [
-            call(
-                functools.partial(intra_kernel, role), (wide, wide, probs_shape, weights_shape),
-                core, held, keys, value, gate, gain, upstream, tab, across, flops=2 * big, name=f"intra{role}",
-            )
-            for role in (0, 1)
-        ]
+        results = call(
+            functools.partial(intra_kernel, role), (wide, wide, probs_shape, weights_shape),
+            core, held, keys, value, gate, gain, upstream, tab, across, flops=3 * big, name=f"intra{role}",
+        )
+        return (*done, results)
 
     state_own, state_other, dec, decays, intra = scan(
-        core, place, own, other, tab, None, None, False, intra_parts
+        core, place, own, other, tab, None, None, False, intra_part
     )
 
     narrow = shape(GROUP, DH)
@@ -501,14 +493,21 @@
 
     half = pltpu.VMEM((GROUP, WIDE), BF16)
 
-    def local(after):
+    whole = pltpu.HBM((GROUP, 2 * WIDE), BF16)
+
+    def local(after, role, done):
         held, factors, _ = lax.optimization_barrier((query, terms, after))
-        return call(
-            local_kernel, (full, full, full, wide, wide, wide, wide),
-            core, held, keys, value, state_own, state_other, grad_own, grad_other, *intra[0][2:], *intra[1][2:], tab,
-            *opened, factors, flops=10 * big, name="local", limit=14,
-            outs=(HBM, HBM, HBM, VMEM, VMEM, VMEM, VMEM), scratch=[half] * 6 + [pltpu.SemaphoreType.DMA((2, 8))],
+        state, grad = ((state_own, grad_own), (state_other, grad_other))[role]
+        sent = done[:3]
+        results = call(
+            functools.partial(local_kernel, role), (whole, whole, whole, wide, wide),
+            core, held, keys, value, state, grad, *intra[role][2:], tab, *opened, factors, *sent,
+            flops=5 * big, name=f"local{role}", limit=10,
+            specs=[SMEM] + [VMEM] * 11 + [HBM] * len(sent), outs=(HBM, HBM, HBM, VMEM, VMEM),
+            scratch=[half] * 3 + [pltpu.SemaphoreType.DMA((8,))],
+            aliases={12: 0, 13: 1, 14: 2} if sent else None,
         )
+        return (*results[:3], *done[3:], *results[3:])
 
     after_own, after_other, _, _, (grad_query, mixed, grad_gate, *inner) = scan(
         core, place, term_own, term_other, tab, dec, decays, True, local

time: 107 us -> 103 us (0.963)
  waiting for transfers between devices: 7.95 us -> 5.85 us
  blocking collectives: 49.2 us -> 48 us
    ppermute x9 -> x7, waiting for transfers between devices: 5.37 us -> 3.26 us  [flipped(): return lax.ppermute(array, axis, [(i, i ^ flip) for i in range(4)])]
    all_to_all x4, blocking collectives: 49.2 us -> 48 us  [spread(): return lax.all_to_all(array, PLANE, 0, 0, tiled=True)]
    ppermute x9 -> x7, starting transfers between devices: 17.1 us -> 16 us  [flipped(): return lax.ppermute(array, axis, [(i, i ^ flip) for i in range(4)])]
    pallas_call x20 -> x23, Pallas kernels: 18.7 us -> 19.5 us  [call(): pl.pallas_call(kernel, out_shape=out, in_specs=specs or [SMEM] * smem + [...]
  transfers between devices with their start and end apart: 13 -> 11, of which waited for: 7 -> 7; matrix products, arithmetic and copies ran while one was open for 0% -> 0% of each run, Pallas kernels for 12% -> 13%
where the time goes in v5:
time: 103 us
  blocking collectives  48 us (47%)
  starting transfers between devices  28.6 us (28%)
  Pallas kernels  19.5 us (19%)
  waiting for transfers between devices  5.85 us (6%)
    all_to_all x4, blocking collectives, spread(): return lax.all_to_all(array, PLANE, 0, 0, tiled=True)  48 us
    pallas_call x23, Pallas kernels, call(): pl.pallas_call(kernel, out_shape=out, in_specs=specs or [SMEM] * smem + [...  19.5 us
    ppermute x7, starting transfers between devices, flipped(): return lax.ppermute(array, axis, [(i, i ^ flip) for i in range(4)])  16 us
    ppermute x4, starting transfers between devices, swap(): return lax.ppermute(array, 'core', [(0, 1), (1, 0)])  12.6 us
    ppermute x7, waiting for transfers between devices, flipped(): return lax.ppermute(array, axis, [(i, i ^ flip) for i in range(4)])  3.26 us
    ppermute x4, waiting for transfers between devices, swap(): return lax.ppermute(array, 'core', [(0, 1), (1, 0)])  2.59 us
  transfers between devices with their start and end apart: 11, of which 7 were waited for; matrix products, arithmetic and copies ran while one was open for 0% of the time, Pallas kernels for 13%

profile of v5, /device:TPU:1, one launch (start us, length us, event | category | flops | bytes accessed | tf_op | source)
XLA Modules:
  0.0 103.0 jit_solution(13496034566954047224)
XLA Ops:
  0.6 1.9 %first.1 = (f32[256,128]{1,0:T(8,128)S(1)}, f32[16,256]{1,0:T(8,128)S(1)}, f32[1032,128]{1,0:T(8,128)S(1)}, bf16[256,2048]{1,0:T(8,128)(2,1)S(1)}, bf16[256,2048]{1,0:T(8,128)(2,1)S(1)}) custom-call(s32[1]{0:T(128)} %bitcast.core_ref, bf16[256,2048]{1,0:T(8,128)(2,1)} %keys_hbm.1, bf16[256,2048]{1,0:T(8,128)(2,1)} %value_hbm.1, f32[16,256]{1,0:T(8,128)} %bitcast.7), custom_call_target="tpu_custom_call" | custom-call | flops 67108864 | bytes 6983684 | tf_op jit(solution)/shard_map/first/pallas_call | solution.py:28
  2.5 0.0 copy-start
  2.5 0.0 copy-start.1
  2.6 0.0 copy-start.2
  2.6 0.0 copy-start.3
  2.6 3.3 %collective-permute-start = (f32[1032,128]{1,0:T(8,128)S(1)}, f32[1032,128]{1,0:T(8,128)S(1)}, u32[]{:S(2)}, u32[]{:S(2)}) collective-permute-start(f32[1032,128]{1,0:T(8,128)S(1)} %get-tuple-element.96), channel_id=1, source_target_pairs={{0,4},{4,0},{1,5},{5,1},{2,6},{6,2},{3,7},{7,3},{8,12},{12,8},{9,1... | collective-permute-start | bytes 1585160 | tf_op jit(solution)/shard_map/ppermute | solution.py:394
  5.9 0.7 second.1.own_ref
  6.7 0.8 collective-permute-done.other_ref
  7.5 0.2 merge_f.1
  7.7 13.6 %all_to_all.20.parts_ref.decays_ref = f32[8,136,128]{2,1,0:T(8,128)S(1)} all-to-all(f32[8,136,128]{2,1,0:T(8,128)S(1)} %get-tuple-element.97), channel_id=1, replica_groups=mesh['z1'=4,'z0'=2,'y'=4,'core'=2,'head'=4] {'z0','y'}, dimensions={0} | all-to-all | bytes 1114112 | tf_op jit(solution)/shard_map/all_to_all | solution.py:402
  21.3 3.1 %collective-permute-start.1 = (f32[136,128]{1,0:T(8,128)S(1)}, f32[136,128]{1,0:T(8,128)S(1)}, u32[]{:S(2)}, u32[]{:S(2)}) collective-permute-start(f32[136,128]{1,0:T(8,128)S(1)} %row_total.2.own_ref), channel_id=1, source_target_pairs={{0,64},{64,0},{128,192},{192,128},{1,65},{65,1},{129,193},{193,129... | collective-permute-start | bytes 208904 | tf_op jit(solution)/shard_map/ppermute | solution.py:398
  24.4 1.7 %intra0.1 = (f32[256,1024]{1,0:T(8,128)S(1)}, f32[256,1024]{1,0:T(8,128)S(1)}, bf16[8,256,256]{2,1,0:T(8,128)(2,1)S(1)}, f32[8,6,128,128]{3,2,1,0:T(8,128)S(1)}) custom-call(s32[1]{0:T(128)} %bitcast.core_ref, bf16[256,2048]{1,0:T(8,128)(2,1)S(1)} %copy-done, bf16[256,2048]{1,0:T(8,128)(2,1)S(1)} %get-tuple-element.93.keys_ref, ...), custom_call_target="tpu_custom_call" | custom-call | flops 402653184 | bytes 12738564 | tf_op jit(solution)/shard_map/intra0/pallas_call | solution.py:28
  26.1 0.7 collective-permute-done.1.near_ref
  26.9 3.8 %collective-permute-start.2 = (f32[128,128]{1,0:T(8,128)S(1)}, f32[128,128]{1,0:T(8,128)S(1)}, u32[]{:S(2)}, u32[]{:S(2)}) collective-permute-start(f32[128,128]{1,0:T(8,128)S(1)} %pair.2), channel_id=1, source_target_pairs={{0,192},{64,128},{128,64},{192,0},{1,193},{65,129},{129,65},{193,1... | collective-permute-start | bytes 196616 | tf_op jit(solution)/shard_map/ppermute | solution.py:398
  30.7 1.7 %intra1.1 = (f32[256,1024]{1,0:T(8,128)S(1)}, f32[256,1024]{1,0:T(8,128)S(1)}, bf16[8,256,256]{2,1,0:T(8,128)(2,1)S(1)}, f32[8,6,128,128]{3,2,1,0:T(8,128)S(1)}) custom-call(s32[1]{0:T(128)} %bitcast.core_ref, bf16[256,2048]{1,0:T(8,128)(2,1)S(1)} %copy-done, bf16[256,2048]{1,0:T(8,128)(2,1)S(1)} %get-tuple-element.93.keys_ref, ...), custom_call_target="tpu_custom_call" | custom-call | flops 402653184 | bytes 12738564 | tf_op jit(solution)/shard_map/intra1/pallas_call | solution.py:28
  32.4 0.2 collective-permute-done.2.far_ref
  32.6 0.1 enter.2
  32.7 11.2 %all_to_all.21.enter_ref = f32[8,128,128]{2,1,0:T(8,128)S(1)} all-to-all(f32[8,128,128]{2,1,0:T(8,128)S(1)} %enter.2), channel_id=1, replica_groups=mesh['z1'=4,'z0'=2,'y'=4,'core'=2,'head'=4] {'z0','y'}, dimensions={0} | all-to-all | bytes 1048576 | tf_op jit(solution)/shard_map/all_to_all | solution.py:402
  43.8 0.1 leave.2
  44.0 3.6 %collective-permute-start.3 = (f32[8,128,128]{2,1,0:T(8,128)S(1)}, f32[8,128,128]{2,1,0:T(8,128)S(1)}, u32[]{:S(2)}, u32[]{:S(2)}) collective-permute-start(f32[8,128,128]{2,1,0:T(8,128)S(1)} %get-tuple-element.120), channel_id=1, source_target_pairs={{0,4},{4,0},{1,5},{5,1},{2,6},{6,2},{3,7},{7,3},{8,12},{12,8},{9,1... | collective-permute-start | bytes 1572872 | tf_op jit(solution)/shard_map/ppermute | solution.py:394
  47.6 0.5 attend0.1
  48.1 1.0 collective-permute-done.3.state_ref
  49.1 0.7 attend1.1
  49.8 2.6 %collective-permute-start.6 = (f32[8,256]{1,0:T(8,128)S(1)}, f32[8,256]{1,0:T(8,128)S(1)}, u32[]{:S(2)}, u32[]{:S(2)}) collective-permute-start(f32[8,256]{1,0:T(8,128)S(1)} %get-tuple-element.126.sum_a), channel_id=1, source_target_pairs={{0,3},{1,2},{2,1},{3,0},{4,7},{5,6},{6,5},{7,4},{8,11},{9,10},{10,... | collective-permute-start | bytes 24584 | tf_op jit(solution)/shard_map/ppermute | solution.py:398
  52.4 0.5 collective-permute-start.5
  52.9 0.3 collective-permute-start.4
  53.2 0.9 opened.1
  54.1 0.0 collective-permute-done.6.sum_d
  54.1 2.3 %collective-permute-done.5.sum_c = f32[8,256]{1,0:T(8,128)S(1)} collective-permute-done((f32[8,256]{1,0:T(8,128)S(1)}, f32[8,256]{1,0:T(8,128)S(1)}, u32[]{:S(2)}, u32[]{:S(2)}) %collective-permute-start.5) | collective-permute-done | bytes 8224 | tf_op jit(solution)/shard_map/ppermute | solution.py:398
  56.4 0.0 collective-permute-done.4.sum_b
  56.4 1.0 grad1.1
  57.4 2.1 %collective-permute-start.7 = (f32[1024,128]{1,0:T(8,128)S(1)}, f32[1024,128]{1,0:T(8,128)S(1)}, u32[]{:S(2)}, u32[]{:S(2)}) collective-permute-start(f32[1024,128]{1,0:T(8,128)S(1)} %get-tuple-element.134), channel_id=1, source_target_pairs={{0,4},{4,0},{1,5},{5,1},{2,6},{6,2},{3,7},{7,3},{8,12},{12,8},{9,1... | collective-permute-start | bytes 1572872 | tf_op jit(solution)/shard_map/ppermute | solution.py:394
  59.5 0.9 grad0.1
  60.3 0.7 collective-permute-done.7.other_ref
  61.0 0.1 merge_b.1
  61.1 11.1 %all_to_all.22.parts_ref = f32[8,128,128]{2,1,0:T(8,128)S(1)} all-to-all(f32[8,128,128]{2,1,0:T(8,128)S(1)} %merge_b.1), channel_id=1, replica_groups=mesh['z1'=4,'z0'=2,'y'=4,'core'=2,'head'=4] {'z0','y'}, dimensions={0} | all-to-all | bytes 1048576 | tf_op jit(solution)/shard_map/all_to_all | solution.py:402
  72.3 2.3 %collective-permute-start.8 = (f32[136,128]{1,0:T(8,128)S(1)}, f32[136,128]{1,0:T(8,128)S(1)}, u32[]{:S(2)}, u32[]{:S(2)}) collective-permute-start(f32[136,128]{1,0:T(8,128)S(1)} %row_total.3.own_ref), channel_id=1, source_target_pairs={{0,64},{64,0},{128,192},{192,128},{1,65},{65,1},{129,193},{193,129... | collective-permute-start | bytes 208904 | tf_op jit(solution)/shard_map/ppermute | solution.py:398
  74.6 2.9 %local0.1 = (bf16[256,2048]{1,0:T(8,128)(2,1)}, bf16[256,2048]{1,0:T(8,128)(2,1)}, bf16[256,2048]{1,0:T(8,128)(2,1)}, f32[256,1024]{1,0:T(8,128)S(1)}, f32[256,1024]{1,0:T(8,128)S(1)}) custom-call(s32[1]{0:T(128)} %bitcast.core_ref, bf16[256,2048]{1,0:T(8,128)(2,1)S(1)} %copy-done, bf16[256,2048]{1,0:T(8,128)(2,1)S(1)} %get-tuple-element.93.keys_ref, ...), custom_call_target="tpu_custom_call" | custom-call | flops 671088640 | bytes 21233668 | tf_op jit(solution)/shard_map/local0/pallas_call | solution.py:28
  77.5 0.0 collective-permute-done.8.near_ref
  77.5 3.5 %collective-permute-start.9 = (f32[128,128]{1,0:T(8,128)S(1)}, f32[128,128]{1,0:T(8,128)S(1)}, u32[]{:S(2)}, u32[]{:S(2)}) collective-permute-start(f32[128,128]{1,0:T(8,128)S(1)} %pair.3), channel_id=1, source_target_pairs={{0,192},{64,128},{128,64},{192,0},{1,193},{65,129},{129,65},{193,1... | collective-permute-start | bytes 196616 | tf_op jit(solution)/shard_map/ppermute | solution.py:398
  81.0 2.9 %local1.1 = (bf16[256,2048]{1,0:T(8,128)(2,1)}, bf16[256,2048]{1,0:T(8,128)(2,1)}, bf16[256,2048]{1,0:T(8,128)(2,1)}, f32[256,1024]{1,0:T(8,128)S(1)}, f32[256,1024]{1,0:T(8,128)S(1)}) custom-call(s32[1]{0:T(128)} %bitcast.core_ref, bf16[256,2048]{1,0:T(8,128)(2,1)S(1)} %copy-done, ...), custom_call_target="tpu_custom_call", output_to_operand_aliasing={{0}: (12, {}), {1}: (13, {}), {2}: (14, {})} | custom-call | flops 671088640 | bytes 24379396 | tf_op jit(solution)/shard_map/local1/pallas_call | solution.py:28
  83.9 0.1 enter.3
  84.0 12.2 %all_to_all.23.enter_ref = f32[8,128,128]{2,1,0:T(8,128)S(1)} all-to-all(f32[8,128,128]{2,1,0:T(8,128)S(1)} %enter.3), channel_id=1, replica_groups=mesh['z1'=4,'z0'=2,'y'=4,'core'=2,'head'=4] {'z0','y'}, dimensions={0} | all-to-all | bytes 1048576 | tf_op jit(solution)/shard_map/all_to_all | solution.py:402
  96.2 0.1 leave.3
  96.3 3.5 %collective-permute-start.10 = (f32[8,128,128]{2,1,0:T(8,128)S(1)}, f32[8,128,128]{2,1,0:T(8,128)S(1)}, u32[]{:S(2)}, u32[]{:S(2)}) collective-permute-start(f32[8,128,128]{2,1,0:T(8,128)S(1)} %get-tuple-element.166), channel_id=1, source_target_pairs={{0,4},{4,0},{1,5},{5,1},{2,6},{6,2},{3,7},{7,3},{8,12},{12,8},{9,1... | collective-permute-start | bytes 1572872 | tf_op jit(solution)/shard_map/ppermute | solution.py:394
  99.8 1.4 %last0.1 = (bf16[256,2048]{1,0:T(8,128)(2,1)}, bf16[256,2048]{1,0:T(8,128)(2,1)}) custom-call(s32[1]{0:T(128)} %bitcast.core_ref, bf16[256,2048]{1,0:T(8,128)(2,1)S(1)} %get-tuple-element.93.keys_ref, bf16[256,2048]{1,0:T(8,128)(2,1)S(1)} %get-tuple-element.94.value_ref, f32[8,128,128]{2,1,0:T(8,128)S(1)} %get-tuple-element.169.state_ref, ...), custom_call_target="tpu_custom_call" | custom-call | flops 134217728 | bytes 9043972 | tf_op jit(solution)/shard_map/last0/pallas_call | solution.py:28
  101.3 0.1 collective-permute-done.10.state_ref
  101.4 1.4 %last1.1 = (bf16[256,2048]{1,0:T(8,128)(2,1)}, bf16[256,2048]{1,0:T(8,128)(2,1)}) custom-call(s32[1]{0:T(128)} %bitcast.core_ref, bf16[256,2048]{1,0:T(8,128)(2,1)S(1)} %get-tuple-element.93.keys_ref, bf16[256,2048]{1,0:T(8,128)(2,1)S(1)} %get-tuple-element.94.value_ref, ...), custom_call_target="tpu_custom_call", output_to_operand_aliasing={{0}: (7, {}), {1}: (8, {})} | custom-call | flops 134217728 | bytes 11141124 | tf_op jit(solution)/shard_map/last1/pallas_call | solution.py:28
  (9 shorter events, 0.1 us)
Async XLA Ops:
  2.5 21.9 %copy-start = (bf16[256,2048]{1,0:T(8,128)(2,1)S(1)}, bf16[256,2048]{1,0:T(8,128)(2,1)}, u32[]{:S(2)}) copy-start(bf16[256,2048]{1,0:T(8,128)(2,1)} %query_ref.11) | copy-start | bytes 3145732
  2.5 21.9 %copy-start.1 = (bf16[256,2048]{1,0:T(8,128)(2,1)S(1)}, bf16[256,2048]{1,0:T(8,128)(2,1)}, u32[]{:S(2)}) copy-start(bf16[256,2048]{1,0:T(8,128)(2,1)} %gate_ref.5) | copy-start | bytes 3145732
  2.6 21.8 %copy-start.2 = (bf16[256,2048]{1,0:T(8,128)(2,1)S(1)}, bf16[256,2048]{1,0:T(8,128)(2,1)}, u32[]{:S(2)}) copy-start(bf16[256,2048]{1,0:T(8,128)(2,1)} %upstream_ref.1) | copy-start | bytes 3145732
  2.6 21.8 %copy-start.3 = (f32[2048]{0:T(1024)S(1)}, f32[2048]{0:T(1024)}, u32[]{:S(2)}) copy-start(f32[2048]{0:T(1024)} %param.12) | copy-start | bytes 24580
  2.6 4.9 %collective-permute-start = (f32[1032,128]{1,0:T(8,128)S(1)}, f32[1032,128]{1,0:T(8,128)S(1)}, u32[]{:S(2)}, u32[]{:S(2)}) collective-permute-start(f32[1032,128]{1,0:T(8,128)S(1)} %get-tuple-element.96), channel_id=1, source_target_pairs={{0,4},{4,0},{1,5},{5,1},{2,6},{6,2},{3,7},{7,3},{8,12},{12,8},{9,1... | collective-permute-start | bytes 1585160 | tf_op jit(solution)/shard_map/ppermute | solution.py:394
  21.3 5.5 %collective-permute-start.1 = (f32[136,128]{1,0:T(8,128)S(1)}, f32[136,128]{1,0:T(8,128)S(1)}, u32[]{:S(2)}, u32[]{:S(2)}) collective-permute-start(f32[136,128]{1,0:T(8,128)S(1)} %row_total.2.own_ref), channel_id=1, source_target_pairs={{0,64},{64,0},{128,192},{192,128},{1,65},{65,1},{129,193},{193,129... | collective-permute-start | bytes 208904 | tf_op jit(solution)/shard_map/ppermute | solution.py:398
  26.9 5.7 %collective-permute-start.2 = (f32[128,128]{1,0:T(8,128)S(1)}, f32[128,128]{1,0:T(8,128)S(1)}, u32[]{:S(2)}, u32[]{:S(2)}) collective-permute-start(f32[128,128]{1,0:T(8,128)S(1)} %pair.2), channel_id=1, source_target_pairs={{0,192},{64,128},{128,64},{192,0},{1,193},{65,129},{129,65},{193,1... | collective-permute-start | bytes 196616 | tf_op jit(solution)/shard_map/ppermute | solution.py:398
  44.0 5.2 %collective-permute-start.3 = (f32[8,128,128]{2,1,0:T(8,128)S(1)}, f32[8,128,128]{2,1,0:T(8,128)S(1)}, u32[]{:S(2)}, u32[]{:S(2)}) collective-permute-start(f32[8,128,128]{2,1,0:T(8,128)S(1)} %get-tuple-element.120), channel_id=1, source_target_pairs={{0,4},{4,0},{1,5},{5,1},{2,6},{6,2},{3,7},{7,3},{8,12},{12,8},{9,1... | collective-permute-start | bytes 1572872 | tf_op jit(solution)/shard_map/ppermute | solution.py:394
  49.8 4.3 %collective-permute-start.6 = (f32[8,256]{1,0:T(8,128)S(1)}, f32[8,256]{1,0:T(8,128)S(1)}, u32[]{:S(2)}, u32[]{:S(2)}) collective-permute-start(f32[8,256]{1,0:T(8,128)S(1)} %get-tuple-element.126.sum_a), channel_id=1, source_target_pairs={{0,3},{1,2},{2,1},{3,0},{4,7},{5,6},{6,5},{7,4},{8,11},{9,10},{10,... | collective-permute-start | bytes 24584 | tf_op jit(solution)/shard_map/ppermute | solution.py:398
  52.4 4.0 %collective-permute-start.5 = (f32[8,256]{1,0:T(8,128)S(1)}, f32[8,256]{1,0:T(8,128)S(1)}, u32[]{:S(2)}, u32[]{:S(2)}) collective-permute-start(f32[8,256]{1,0:T(8,128)S(1)} %get-tuple-element.126.sum_a), channel_id=1, source_target_pairs={{0,2},{1,3},{2,0},{3,1},{4,6},{5,7},{6,4},{7,5},{8,10},{9,11},{10,... | collective-permute-start | bytes 24584 | tf_op jit(solution)/shard_map/ppermute | solution.py:398
  52.9 3.5 %collective-permute-start.4 = (f32[8,256]{1,0:T(8,128)S(1)}, f32[8,256]{1,0:T(8,128)S(1)}, u32[]{:S(2)}, u32[]{:S(2)}) collective-permute-start(f32[8,256]{1,0:T(8,128)S(1)} %get-tuple-element.126.sum_a), channel_id=1, source_target_pairs={{0,1},{1,0},{2,3},{3,2},{4,5},{5,4},{6,7},{7,6},{8,9},{9,8},{10,11... | collective-permute-start | bytes 24584 | tf_op jit(solution)/shard_map/ppermute | solution.py:398
  57.4 3.6 %collective-permute-start.7 = (f32[1024,128]{1,0:T(8,128)S(1)}, f32[1024,128]{1,0:T(8,128)S(1)}, u32[]{:S(2)}, u32[]{:S(2)}) collective-permute-start(f32[1024,128]{1,0:T(8,128)S(1)} %get-tuple-element.134), channel_id=1, source_target_pairs={{0,4},{4,0},{1,5},{5,1},{2,6},{6,2},{3,7},{7,3},{8,12},{12,8},{9,1... | collective-permute-start | bytes 1572872 | tf_op jit(solution)/shard_map/ppermute | solution.py:394
  72.3 5.2 %collective-permute-start.8 = (f32[136,128]{1,0:T(8,128)S(1)}, f32[136,128]{1,0:T(8,128)S(1)}, u32[]{:S(2)}, u32[]{:S(2)}) collective-permute-start(f32[136,128]{1,0:T(8,128)S(1)} %row_total.3.own_ref), channel_id=1, source_target_pairs={{0,64},{64,0},{128,192},{192,128},{1,65},{65,1},{129,193},{193,129... | collective-permute-start | bytes 208904 | tf_op jit(solution)/shard_map/ppermute | solution.py:398
  77.5 6.4 %collective-permute-start.9 = (f32[128,128]{1,0:T(8,128)S(1)}, f32[128,128]{1,0:T(8,128)S(1)}, u32[]{:S(2)}, u32[]{:S(2)}) collective-permute-start(f32[128,128]{1,0:T(8,128)S(1)} %pair.3), channel_id=1, source_target_pairs={{0,192},{64,128},{128,64},{192,0},{1,193},{65,129},{129,65},{193,1... | collective-permute-start | bytes 196616 | tf_op jit(solution)/shard_map/ppermute | solution.py:398
  96.3 5.1 %collective-permute-start.10 = (f32[8,128,128]{2,1,0:T(8,128)S(1)}, f32[8,128,128]{2,1,0:T(8,128)S(1)}, u32[]{:S(2)}, u32[]{:S(2)}) collective-permute-start(f32[8,128,128]{2,1,0:T(8,128)S(1)} %get-tuple-element.166), channel_id=1, source_target_pairs={{0,4},{4,0},{1,5},{5,1},{2,6},{6,2},{3,7},{7,3},{8,12},{12,8},{9,1... | collective-permute-start | bytes 1572872 | tf_op jit(solution)/shard_map/ppermute | solution.py:394

commit v6 on v5

--- a/solution.py
+++ b/solution.py
@@ -49,10 +49,9 @@
 
 
 def turned(x):
-    n = x.shape[1]
-    rows = lax.broadcasted_iota(jnp.int32, (n, n), 0)
-    cols = lax.broadcasted_iota(jnp.int32, (n, n), 1)
-    return dot((rows == cols).astype(BF16), x, 1, 1).astype(BF16)
+    rows = lax.broadcasted_iota(jnp.int32, (DH, DH), 0)
+    cols = lax.broadcasted_iota(jnp.int32, (DH, DH), 1)
+    return dot((rows == cols).astype(BF16), x, 1, 1)
 
 
 def columns(role, core, i):
@@ -75,18 +74,22 @@
     low = (rest - middle.astype(F32)).astype(BF16)
     across = dot(jnp.concatenate([high, middle, low], axis=0), tri, 1, 1)
     across = across[:16] + (across[16:32] + across[32:])
-    across = jnp.where(core == 0, across, jnp.concatenate([across[HALF:], across[:HALF]], axis=0))
-    return across.T, across
-
-
-def state_term(core, role, i, keys_ref, value_ref, tab):
+    return jnp.where(core == 0, across, jnp.concatenate([across[HALF:], across[:HALF]], axis=0))
+
+
+def state_term(core, role, i, keys_ref, value_ref, toward_end):
     at = columns(role, core, i)
-    keyed = (keys_ref[:, at].astype(F32) * lanes(tab, 2, role, i)).astype(BF16)
-    return dot(turned(keyed), value_ref[:, at], 1, 0)
+    row = toward_end[role * HALF + i : role * HALF + i + 1, :]
+    keyed = (turned(keys_ref[:, at]) * row).astype(BF16)
+    return dot(keyed, value_ref[:, at], 1, 0)
+
+
+def toward_last(across):
+    return jnp.exp(across[:, GROUP - 1 :] - across)
 
 
 def first_kernel(
-    core_ref, keys_hbm, value_hbm, decay_hbm, tab_ref, across_ref, send_ref, keys_ref, value_ref, decay_ref, sems
+    core_ref, keys_hbm, value_hbm, decay_hbm, across_ref, send_ref, keys_ref, value_ref, decay_ref, sems
 ):
     core = core_ref[0]
     copies = [pltpu.make_async_copy(decay_hbm, decay_ref, sems.at[0])]
@@ -97,44 +100,43 @@
     for copy in copies:
         copy.start()
     copies[0].wait()
-    down, across = tables(core, decay_ref[...])
+    across = tables(core, decay_ref[...])
+    across_ref[...] = across
+    send_ref[WIDE:, :] = jnp.broadcast_to(across[:, GROUP - 1 :], (16, DH))
+    toward_end = toward_last(across)
+    copies[1].wait()
+    copies[2].wait()
+    for i in range(HALF):
+        send_ref[i * DH : (i + 1) * DH, :] = state_term(core, 1, i, keys_ref, value_ref, toward_end)
+    copies[3].wait()
+    copies[4].wait()
+
+
+def second_kernel(core_ref, keys_ref, value_ref, across_ref, tab_ref, keep_ref):
+    core = core_ref[0]
+    across = across_ref[...]
+    down = across.T
     last = down[GROUP - 1 :, :]
     blank = jnp.zeros((GROUP, 128 - 48), F32)
-    tab = jnp.concatenate([down, jnp.exp(down), jnp.exp(last - down), blank], axis=1)
-    tab_ref[...] = tab
-    across_ref[...] = across
-    send_ref[WIDE:, :] = jnp.broadcast_to(tab[GROUP - 1 :, :], (8, 128))
-    copies[1].wait()
-    copies[2].wait()
-    for i in range(HALF):
-        send_ref[i * DH : (i + 1) * DH, :] = state_term(core, 1, i, keys_ref, value_ref, tab)
-    copies[3].wait()
-    copies[4].wait()
-
-
-def second_kernel(core_ref, keys_ref, value_ref, tab_ref, keep_ref):
-    core = core_ref[0]
-    tab = tab_ref[...]
-    for i in range(HALF):
-        keep_ref[i * DH : (i + 1) * DH, :] = state_term(core, 0, i, keys_ref, value_ref, tab)
-
-
-def merge_forward(core_ref, own_ref, other_ref, tab_ref, out_ref, dec_ref):
+    tab_ref[...] = jnp.concatenate([down, jnp.exp(down), jnp.exp(last - down), blank], axis=1)
+    toward_end = toward_last(across)
+    for i in range(HALF):
+        keep_ref[i * DH : (i + 1) * DH, :] = state_term(core, 0, i, keys_ref, value_ref, toward_end)
+
+
+def merge_forward(core_ref, own_ref, other_ref, across_ref, out_ref, dec_ref):
     zero = core_ref[0] == 0
-    mine = tab_ref[GROUP - 1 :, :HALF]
-    theirs = other_ref[WIDE : WIDE + 1, HALF : 2 * HALF]
-    last_a = jnp.where(zero, mine, theirs)
-    last_b = jnp.where(zero, theirs, mine)
-    for i in range(HALF):
-        own = own_ref[i * DH : (i + 1) * DH, :]
-        other = other_ref[i * DH : (i + 1) * DH, :]
-        a, b = jnp.where(zero, own, other), jnp.where(zero, other, own)
-        here_a = jnp.broadcast_to(last_a[:, i : i + 1], (1, 128))
-        here_b = jnp.broadcast_to(last_b[:, i : i + 1], (1, 128))
-        dec_ref[i : i + 1, :] = jnp.exp(here_a)
-        dec_ref[HALF + i : HALF + i + 1, :] = jnp.exp(here_b)
-        out_ref[i, :DH, :] = jnp.exp(here_b) * a + b
-        out_ref[i, DH:, :] = jnp.broadcast_to(here_a + here_b, (8, 128))
+    mine = jnp.broadcast_to(across_ref[:HALF, GROUP - 1 :], (HALF, DH))
+    theirs = other_ref[WIDE + HALF :, :]
+    decay = mine + theirs
+    factor = jnp.exp(jnp.where(zero, theirs, mine))
+    dec_ref[:HALF, :] = jnp.exp(jnp.where(zero, mine, theirs))
+    dec_ref[HALF:, :] = factor
+    own_factor, other_factor = jnp.where(zero, factor, 1.0), jnp.where(zero, 1.0, factor)
+    for i in range(HALF):
+        at = slice(i * DH, (i + 1) * DH)
+        out_ref[i, :DH, :] = own_factor[i : i + 1] * own_ref[at, :] + other_factor[i : i + 1] * other_ref[at, :]
+        out_ref[i, DH:, :] = jnp.broadcast_to(decay[i : i + 1], (8, DH))
 
 
 def merge_backward(core_ref, own_ref, other_ref, dec_ref, out_ref):
@@ -208,7 +210,7 @@
 
 def intra_kernel(
     role, core_ref, query_ref, keys_ref, value_ref, gate_ref, gain_ref, mixed_ref, tab_ref, across_ref,
-    intra_ref, normed_ref, turned_ref, weights_ref,
+    intra_ref, normed_ref, turned_ref, weights_ref, weighted_ref,
 ):
     core = core_ref[0]
     tab = tab_ref[...]
@@ -231,6 +233,7 @@
         )
         for part, array in enumerate(weights):
             weights_ref[i, part] = array
+        weighted_ref[i] = (turned(query) * jnp.exp(across)).astype(BF16)
         probs = masked(dot(query, keys, 1, 1), weights[:3])
         turned_ref[i] = masked(dot(keys, query, 1, 1), weights[3:], upper=True)
         intra_ref[:, to] = dot(probs, value_ref[:, at], 1, 0)
@@ -270,24 +273,20 @@
     terms_ref[...] = jnp.concatenate([both.T, jnp.zeros((GROUP, DH - 8), F32)], axis=1)
 
 
-def grad_kernel(role, core_ref, query_ref, attention_ref, normed_ref, tab_ref, terms_ref, grad_ref, term_ref):
-    core = core_ref[0]
-    tab = tab_ref[...]
+def grad_kernel(attention_ref, normed_ref, weighted_ref, terms_ref, grad_ref, term_ref):
     scale, shift = terms_ref[:, 0:1], terms_ref[:, 1:2]
     for i in range(HALF):
-        at = columns(role, core, i)
         to = slice(i * DH, (i + 1) * DH)
         grad = (scale * (normed_ref[:, to] - attention_ref[:, to] * shift)).astype(BF16)
         grad_ref[:, to] = grad
-        weighted = (query_ref[:, at].astype(F32) * lanes(tab, 1, role, i)).astype(BF16)
-        term_ref[i * DH : (i + 1) * DH, :] = dot(turned(weighted), grad, 1, 0)
+        term_ref[i * DH : (i + 1) * DH, :] = dot(weighted_ref[i], grad, 1, 0)
 
 
 def grad_first(
-    core_ref, query_ref, attention_ref, normed_ref, tab_ref, sum_a, sum_b, sum_c, sum_d, grad_ref, term_ref, terms_ref
+    attention_ref, normed_ref, weighted_ref, sum_a, sum_b, sum_c, sum_d, grad_ref, term_ref, terms_ref
 ):
     norm_terms((sum_a[...] + sum_b[...]) + (sum_c[...] + sum_d[...]), terms_ref)
-    grad_kernel(1, core_ref, query_ref, attention_ref, normed_ref, tab_ref, terms_ref, grad_ref, term_ref)
+    grad_kernel(attention_ref, normed_ref, weighted_ref, terms_ref, grad_ref, term_ref)
 
 
 class Sender:
@@ -402,12 +401,12 @@
     return lax.all_to_all(array, PLANE, 0, 0, tiled=True)
 
 
-def scan(core, place, own, other, tab, dec, decays, reverse, beside):
+def scan(core, place, own, other, across, dec, decays, reverse, beside):
     if reverse:
         totals = call(merge_backward, shape(HALF, DH, DH), core, own, other, dec, name="merge_b")
     else:
         totals, dec = call(
-            merge_forward, (shape(HALF, DH + 8, DH), shape(2 * HALF, DH)), core, own, other, tab, name="merge_f"
+            merge_forward, (shape(HALF, DH + 8, DH), shape(2 * HALF, DH)), core, own, other, across, name="merge_f"
         )
     parts = spread(totals)
     decays = parts if decays is None else decays
@@ -438,30 +437,33 @@
     small = big // 2
 
     full = shape(GROUP, 2 * WIDE, dtype=BF16)
-    tab, across, send, keys, value = call(
+    across, send, keys, value = call(
         first_kernel,
-        (shape(GROUP, 128), shape(16, GROUP), shape(WIDE + 8, DH), full, full),
+        (shape(16, GROUP), shape(WIDE + 16, DH), full, full),
         core, *(pltpu.with_memory_space_constraint(a, pltpu.HBM) for a in (keys, value, decay.T)),
         flops=small, name="first",
         specs=[SMEM, HBM, HBM, HBM], scratch=[pltpu.VMEM((16, GROUP), F32), pltpu.SemaphoreType.DMA((5,))],
     )
     other = swap(send)
-    own = call(second_kernel, shape(WIDE, DH), core, keys, value, tab, flops=small, name="second")
+    tab, own = call(
+        second_kernel, (shape(GROUP, 128), shape(WIDE, DH)), core, keys, value, across, flops=small, name="second"
+    )
 
     wide = shape(GROUP, WIDE)
     probs_shape = shape(HALF, GROUP, GROUP, dtype=BF16)
     weights_shape = shape(HALF, 6, DH, DH)
+    weighted_shape = shape(HALF, DH, GROUP, dtype=BF16)
 
     def intra_part(after, role, done):
         held, _ = lax.optimization_barrier((query, after))
         results = call(
-            functools.partial(intra_kernel, role), (wide, wide, probs_shape, weights_shape),
+            functools.partial(intra_kernel, role), (wide, wide, probs_shape, weights_shape, weighted_shape),
             core, held, keys, value, gate, gain, upstream, tab, across, flops=3 * big, name=f"intra{role}",
         )
         return (*done, results)
 
     state_own, state_other, dec, decays, intra = scan(
-        core, place, own, other, tab, None, None, False, intra_part
+        core, place, own, other, across, None, None, False, intra_part
     )
 
     narrow = shape(GROUP, DH)
@@ -483,12 +485,11 @@
     grads_shape = (shape(GROUP, WIDE, dtype=BF16), shape(WIDE, DH))
     grad_other, term_send, terms = call(
         grad_first, (*grads_shape, shape(GROUP, DH)),
-        core, query, att_other, intra[1][1], tab, sums, *moved, flops=small, name="grad1",
+        att_other, intra[1][1], intra[1][4], sums, *moved, flops=small, smem=0, name="grad1",
     )
     term_other = swap(term_send)
     grad_own, term_own = call(
-        functools.partial(grad_kernel, 0), grads_shape, core, query, att_own, intra[0][1], tab, terms,
-        flops=small, name="grad0",
+        grad_kernel, grads_shape, att_own, intra[0][1], intra[0][4], terms, flops=small, smem=0, name="grad0",
     )
 
     half = pltpu.VMEM((GROUP, WIDE), BF16)
@@ -501,7 +502,7 @@
         sent = done[:3]
         results = call(
             functools.partial(local_kernel, role), (whole, whole, whole, wide, wide),
-            core, held, keys, value, state, grad, *intra[role][2:], tab, *opened, factors, *sent,
+            core, held, keys, value, state, grad, *intra[role][2:4], tab, *opened, factors, *sent,
             flops=5 * big, name=f"local{role}", limit=10,
             specs=[SMEM] + [VMEM] * 11 + [HBM] * len(sent), outs=(HBM, HBM, HBM, VMEM, VMEM),
             scratch=[half] * 3 + [pltpu.SemaphoreType.DMA((8,))],
@@ -510,7 +511,7 @@
         return (*results[:3], *done[3:], *results[3:])
 
     after_own, after_other, _, _, (grad_query, mixed, grad_gate, *inner) = scan(
-        core, place, term_own, term_other, tab, dec, decays, True, local
+        core, place, term_own, term_other, across, dec, decays, True, local
     )
     ends = ()
     for role, state in ((0, after_own), (1, after_other)):

time: 103 us -> 103 us (level)
  no operation moved by 1% of the time
where the time goes in v6:
time: 103 us; the launch traced here: 102 us
  blocking collectives  48.1 us (47%)
  starting transfers between devices  28.5 us (28%)
  Pallas kernels  18.7 us (18%)
  waiting for transfers between devices  6.15 us (6%)
    all_to_all x4, blocking collectives, spread(): return lax.all_to_all(array, PLANE, 0, 0, tiled=True)  48.1 us
    pallas_call x23, Pallas kernels, call(): pl.pallas_call(kernel, out_shape=out, in_specs=specs or [SMEM] * smem + [...  18.7 us
    ppermute x7, starting transfers between devices, flipped(): return lax.ppermute(array, axis, [(i, i ^ flip) for i in range(4)])  16 us
    ppermute x4, starting transfers between devices, swap(): return lax.ppermute(array, 'core', [(0, 1), (1, 0)])  12.5 us
    ppermute x7, waiting for transfers between devices, flipped(): return lax.ppermute(array, axis, [(i, i ^ flip) for i in range(4)])  3.15 us
    ppermute x4, waiting for transfers between devices, swap(): return lax.ppermute(array, 'core', [(0, 1), (1, 0)])  3 us
  transfers between devices with their start and end apart: 11, of which 7 were waited for; matrix products, arithmetic and copies ran while one was open for 0% of the time, Pallas kernels for 13%

profile of v6, /device:TPU:1, one launch (start us, length us, event | category | flops | bytes accessed | tf_op | source)
XLA Modules:
  0.0 102.5 jit_solution(12199166454237009549)
XLA Ops:
  0.6 1.8 %first.1 = (f32[16,256]{1,0:T(8,128)S(1)}, f32[1040,128]{1,0:T(8,128)S(1)}, bf16[256,2048]{1,0:T(8,128)(2,1)S(1)}, bf16[256,2048]{1,0:T(8,128)(2,1)S(1)}) custom-call(s32[1]{0:T(128)} %bitcast.core_ref, bf16[256,2048]{1,0:T(8,128)(2,1)} %keys_hbm.1, bf16[256,2048]{1,0:T(8,128)(2,1)} %value_hbm.1, f32[16,256]{1,0:T(8,128)} %bitcast.7), custom_call_target="tpu_custom_call" | custom-call | flops 67108864 | bytes 6856708 | tf_op jit(solution)/shard_map/first/pallas_call | solution.py:28
  2.5 0.0 copy-start
  2.5 0.0 copy-start.1
  2.5 0.0 copy-start.2
  2.5 0.0 copy-start.3
  2.5 3.3 %collective-permute-start = (f32[1040,128]{1,0:T(8,128)S(1)}, f32[1040,128]{1,0:T(8,128)S(1)}, u32[]{:S(2)}, u32[]{:S(2)}) collective-permute-start(f32[1040,128]{1,0:T(8,128)S(1)} %get-tuple-element.103), channel_id=1, source_target_pairs={{0,4},{4,0},{1,5},{5,1},{2,6},{6,2},{3,7},{7,3},{8,12},{12,8},{9,1... | collective-permute-start | bytes 1597448 | tf_op jit(solution)/shard_map/ppermute | solution.py:393
  5.8 0.7 second.1
  6.5 0.9 collective-permute-done.other_ref
  7.4 0.1 merge_f.1
  7.5 13.6 %all_to_all.20.parts_ref.decays_ref = f32[8,136,128]{2,1,0:T(8,128)S(1)} all-to-all(f32[8,136,128]{2,1,0:T(8,128)S(1)} %get-tuple-element.104), channel_id=1, replica_groups=mesh['z1'=4,'z0'=2,'y'=4,'core'=2,'head'=4] {'z0','y'}, dimensions={0} | all-to-all | bytes 1114112 | tf_op jit(solution)/shard_map/all_to_all | solution.py:401
  21.2 3.1 %collective-permute-start.1 = (f32[136,128]{1,0:T(8,128)S(1)}, f32[136,128]{1,0:T(8,128)S(1)}, u32[]{:S(2)}, u32[]{:S(2)}) collective-permute-start(f32[136,128]{1,0:T(8,128)S(1)} %row_total.2.own_ref), channel_id=1, source_target_pairs={{0,64},{64,0},{128,192},{192,128},{1,65},{65,1},{129,193},{193,129... | collective-permute-start | bytes 208904 | tf_op jit(solution)/shard_map/ppermute | solution.py:397
  24.3 1.7 %intra0.1 = (f32[256,1024]{1,0:T(8,128)S(1)}, f32[256,1024]{1,0:T(8,128)S(1)}, bf16[8,256,256]{2,1,0:T(8,128)(2,1)S(1)}, f32[8,6,128,128]{3,2,1,0:T(8,128)S(1)}, bf16[8,128,256]{2,1,0:T(8,128)(2,1)S(1)}) custom-call(s32[1]{0:T(128)} %bitcast.core_ref, bf16[256,2048]{1,0:T(8,128)(2,1)S(1)} %copy-done, bf16[256,2048]{1,0:T(8,128)(2,1)S(1)} %get-tuple-element.99.keys_ref, ...), custom_call_target="tpu_custom_call" | custom-call | flops 402653184 | bytes 13787140 | tf_op jit(solution)/shard_map/intra0/pallas_call | solution.py:28
  26.0 0.7 collective-permute-done.1.near_ref
  26.7 3.8 %collective-permute-start.2 = (f32[128,128]{1,0:T(8,128)S(1)}, f32[128,128]{1,0:T(8,128)S(1)}, u32[]{:S(2)}, u32[]{:S(2)}) collective-permute-start(f32[128,128]{1,0:T(8,128)S(1)} %pair.2), channel_id=1, source_target_pairs={{0,192},{64,128},{128,64},{192,0},{1,193},{65,129},{129,65},{193,1... | collective-permute-start | bytes 196616 | tf_op jit(solution)/shard_map/ppermute | solution.py:397
  30.6 1.7 %intra1.1 = (f32[256,1024]{1,0:T(8,128)S(1)}, f32[256,1024]{1,0:T(8,128)S(1)}, bf16[8,256,256]{2,1,0:T(8,128)(2,1)S(1)}, f32[8,6,128,128]{3,2,1,0:T(8,128)S(1)}, bf16[8,128,256]{2,1,0:T(8,128)(2,1)S(1)}) custom-call(s32[1]{0:T(128)} %bitcast.core_ref, bf16[256,2048]{1,0:T(8,128)(2,1)S(1)} %copy-done, bf16[256,2048]{1,0:T(8,128)(2,1)S(1)} %get-tuple-element.99.keys_ref, ...), custom_call_target="tpu_custom_call" | custom-call | flops 402653184 | bytes 13787140 | tf_op jit(solution)/shard_map/intra1/pallas_call | solution.py:28
  32.3 0.2 collective-permute-done.2.far_ref
  32.5 0.1 enter.2
  32.5 11.2 %all_to_all.21.enter_ref = f32[8,128,128]{2,1,0:T(8,128)S(1)} all-to-all(f32[8,128,128]{2,1,0:T(8,128)S(1)} %enter.2), channel_id=1, replica_groups=mesh['z1'=4,'z0'=2,'y'=4,'core'=2,'head'=4] {'z0','y'}, dimensions={0} | all-to-all | bytes 1048576 | tf_op jit(solution)/shard_map/all_to_all | solution.py:401
  43.7 0.1 leave.2
  43.9 3.6 %collective-permute-start.3 = (f32[8,128,128]{2,1,0:T(8,128)S(1)}, f32[8,128,128]{2,1,0:T(8,128)S(1)}, u32[]{:S(2)}, u32[]{:S(2)}) collective-permute-start(f32[8,128,128]{2,1,0:T(8,128)S(1)} %get-tuple-element.131), channel_id=1, source_target_pairs={{0,4},{4,0},{1,5},{5,1},{2,6},{6,2},{3,7},{7,3},{8,12},{12,8},{9,1... | collective-permute-start | bytes 1572872 | tf_op jit(solution)/shard_map/ppermute | solution.py:393
  47.4 0.5 attend0.1
  48.0 1.0 collective-permute-done.3.state_ref
  49.0 0.7 attend1.1
  49.7 2.6 %collective-permute-start.6 = (f32[8,256]{1,0:T(8,128)S(1)}, f32[8,256]{1,0:T(8,128)S(1)}, u32[]{:S(2)}, u32[]{:S(2)}) collective-permute-start(f32[8,256]{1,0:T(8,128)S(1)} %get-tuple-element.138.sum_a), channel_id=1, source_target_pairs={{0,3},{1,2},{2,1},{3,0},{4,7},{5,6},{6,5},{7,4},{8,11},{9,10},{10,... | collective-permute-start | bytes 24584 | tf_op jit(solution)/shard_map/ppermute | solution.py:397
  52.2 0.5 collective-permute-start.5
  52.7 0.3 collective-permute-start.4
  53.0 0.9 opened.1
  53.9 2.3 %collective-permute-done.5.sum_c = f32[8,256]{1,0:T(8,128)S(1)} collective-permute-done((f32[8,256]{1,0:T(8,128)S(1)}, f32[8,256]{1,0:T(8,128)S(1)}, u32[]{:S(2)}, u32[]{:S(2)}) %collective-permute-start.5) | collective-permute-done | bytes 8224 | tf_op jit(solution)/shard_map/ppermute | solution.py:397
  56.2 0.0 collective-permute-done.4.sum_b
  56.2 0.7 grad1.1
  56.9 2.1 %collective-permute-start.7 = (f32[1024,128]{1,0:T(8,128)S(1)}, f32[1024,128]{1,0:T(8,128)S(1)}, u32[]{:S(2)}, u32[]{:S(2)}) collective-permute-start(f32[1024,128]{1,0:T(8,128)S(1)} %get-tuple-element.146), channel_id=1, source_target_pairs={{0,4},{4,0},{1,5},{5,1},{2,6},{6,2},{3,7},{7,3},{8,12},{12,8},{9,1... | collective-permute-start | bytes 1572872 | tf_op jit(solution)/shard_map/ppermute | solution.py:393
  59.0 0.5 grad0.1
  59.5 1.0 collective-permute-done.7.other_ref
  60.5 0.1 merge_b.1
  60.6 11.1 %all_to_all.22.parts_ref = f32[8,128,128]{2,1,0:T(8,128)S(1)} all-to-all(f32[8,128,128]{2,1,0:T(8,128)S(1)} %merge_b.1), channel_id=1, replica_groups=mesh['z1'=4,'z0'=2,'y'=4,'core'=2,'head'=4] {'z0','y'}, dimensions={0} | all-to-all | bytes 1048576 | tf_op jit(solution)/shard_map/all_to_all | solution.py:401
  71.8 2.3 %collective-permute-start.8 = (f32[136,128]{1,0:T(8,128)S(1)}, f32[136,128]{1,0:T(8,128)S(1)}, u32[]{:S(2)}, u32[]{:S(2)}) collective-permute-start(f32[136,128]{1,0:T(8,128)S(1)} %row_total.3.own_ref), channel_id=1, source_target_pairs={{0,64},{64,0},{128,192},{192,128},{1,65},{65,1},{129,193},{193,129... | collective-permute-start | bytes 208904 | tf_op jit(solution)/shard_map/ppermute | solution.py:397
  74.1 2.9 %local0.1 = (bf16[256,2048]{1,0:T(8,128)(2,1)}, bf16[256,2048]{1,0:T(8,128)(2,1)}, bf16[256,2048]{1,0:T(8,128)(2,1)}, f32[256,1024]{1,0:T(8,128)S(1)}, f32[256,1024]{1,0:T(8,128)S(1)}) custom-call(s32[1]{0:T(128)} %bitcast.core_ref, bf16[256,2048]{1,0:T(8,128)(2,1)S(1)} %copy-done, bf16[256,2048]{1,0:T(8,128)(2,1)S(1)} %get-tuple-element.99.keys_ref, ...), custom_call_target="tpu_custom_call" | custom-call | flops 671088640 | bytes 21233668 | tf_op jit(solution)/shard_map/local0/pallas_call | solution.py:28
  77.0 0.0 collective-permute-done.8.near_ref
  77.0 3.5 %collective-permute-start.9 = (f32[128,128]{1,0:T(8,128)S(1)}, f32[128,128]{1,0:T(8,128)S(1)}, u32[]{:S(2)}, u32[]{:S(2)}) collective-permute-start(f32[128,128]{1,0:T(8,128)S(1)} %pair.3), channel_id=1, source_target_pairs={{0,192},{64,128},{128,64},{192,0},{1,193},{65,129},{129,65},{193,1... | collective-permute-start | bytes 196616 | tf_op jit(solution)/shard_map/ppermute | solution.py:397
  80.5 2.9 %local1.1 = (bf16[256,2048]{1,0:T(8,128)(2,1)}, bf16[256,2048]{1,0:T(8,128)(2,1)}, bf16[256,2048]{1,0:T(8,128)(2,1)}, f32[256,1024]{1,0:T(8,128)S(1)}, f32[256,1024]{1,0:T(8,128)S(1)}) custom-call(s32[1]{0:T(128)} %bitcast.core_ref, bf16[256,2048]{1,0:T(8,128)(2,1)S(1)} %copy-done, ...), custom_call_target="tpu_custom_call", output_to_operand_aliasing={{0}: (12, {}), {1}: (13, {}), {2}: (14, {})} | custom-call | flops 671088640 | bytes 24379396 | tf_op jit(solution)/shard_map/local1/pallas_call | solution.py:28
  83.4 0.0 collective-permute-done.9.far_ref
  83.5 0.1 enter.3
  83.5 12.2 %all_to_all.23.enter_ref = f32[8,128,128]{2,1,0:T(8,128)S(1)} all-to-all(f32[8,128,128]{2,1,0:T(8,128)S(1)} %enter.3), channel_id=1, replica_groups=mesh['z1'=4,'z0'=2,'y'=4,'core'=2,'head'=4] {'z0','y'}, dimensions={0} | all-to-all | bytes 1048576 | tf_op jit(solution)/shard_map/all_to_all | solution.py:401
  95.7 0.1 leave.3
  95.8 3.5 %collective-permute-start.10 = (f32[8,128,128]{2,1,0:T(8,128)S(1)}, f32[8,128,128]{2,1,0:T(8,128)S(1)}, u32[]{:S(2)}, u32[]{:S(2)}) collective-permute-start(f32[8,128,128]{2,1,0:T(8,128)S(1)} %get-tuple-element.178), channel_id=1, source_target_pairs={{0,4},{4,0},{1,5},{5,1},{2,6},{6,2},{3,7},{7,3},{8,12},{12,8},{9,1... | collective-permute-start | bytes 1572872 | tf_op jit(solution)/shard_map/ppermute | solution.py:393
  99.4 1.4 %last0.1 = (bf16[256,2048]{1,0:T(8,128)(2,1)}, bf16[256,2048]{1,0:T(8,128)(2,1)}) custom-call(s32[1]{0:T(128)} %bitcast.core_ref, bf16[256,2048]{1,0:T(8,128)(2,1)S(1)} %get-tuple-element.99.keys_ref, bf16[256,2048]{1,0:T(8,128)(2,1)S(1)} %get-tuple-element.100.value_ref, f32[8,128,128]{2,1,0:T(8,128)S(1)} %get-tuple-element.181.state_ref, ...), custom_call_target="tpu_custom_call" | custom-call | flops 134217728 | bytes 9043972 | tf_op jit(solution)/shard_map/last0/pallas_call | solution.py:28
  100.8 0.1 collective-permute-done.10.state_ref
  100.9 1.4 %last1.1 = (bf16[256,2048]{1,0:T(8,128)(2,1)}, bf16[256,2048]{1,0:T(8,128)(2,1)}) custom-call(s32[1]{0:T(128)} %bitcast.core_ref, bf16[256,2048]{1,0:T(8,128)(2,1)S(1)} %get-tuple-element.99.keys_ref, bf16[256,2048]{1,0:T(8,128)(2,1)S(1)} %get-tuple-element.100.value_ref, ...), custom_call_target="tpu_custom_call", output_to_operand_aliasing={{0}: (7, {}), {1}: (8, {})} | custom-call | flops 134217728 | bytes 11141124 | tf_op jit(solution)/shard_map/last1/pallas_call | solution.py:28
  (9 shorter events, 0.1 us)
Async XLA Ops:
  2.5 21.8 %copy-start = (bf16[256,2048]{1,0:T(8,128)(2,1)S(1)}, bf16[256,2048]{1,0:T(8,128)(2,1)}, u32[]{:S(2)}) copy-start(bf16[256,2048]{1,0:T(8,128)(2,1)} %query_ref.7) | copy-start | bytes 3145732
  2.5 21.8 %copy-start.1 = (bf16[256,2048]{1,0:T(8,128)(2,1)S(1)}, bf16[256,2048]{1,0:T(8,128)(2,1)}, u32[]{:S(2)}) copy-start(bf16[256,2048]{1,0:T(8,128)(2,1)} %gate_ref.5) | copy-start | bytes 3145732
  2.5 21.8 %copy-start.2 = (bf16[256,2048]{1,0:T(8,128)(2,1)S(1)}, bf16[256,2048]{1,0:T(8,128)(2,1)}, u32[]{:S(2)}) copy-start(bf16[256,2048]{1,0:T(8,128)(2,1)} %upstream_ref.1) | copy-start | bytes 3145732
  2.5 21.8 %copy-start.3 = (f32[2048]{0:T(1024)S(1)}, f32[2048]{0:T(1024)}, u32[]{:S(2)}) copy-start(f32[2048]{0:T(1024)} %param.12) | copy-start | bytes 24580
  2.5 4.9 %collective-permute-start = (f32[1040,128]{1,0:T(8,128)S(1)}, f32[1040,128]{1,0:T(8,128)S(1)}, u32[]{:S(2)}, u32[]{:S(2)}) collective-permute-start(f32[1040,128]{1,0:T(8,128)S(1)} %get-tuple-element.103), channel_id=1, source_target_pairs={{0,4},{4,0},{1,5},{5,1},{2,6},{6,2},{3,7},{7,3},{8,12},{12,8},{9,1... | collective-permute-start | bytes 1597448 | tf_op jit(solution)/shard_map/ppermute | solution.py:393
  21.2 5.5 %collective-permute-start.1 = (f32[136,128]{1,0:T(8,128)S(1)}, f32[136,128]{1,0:T(8,128)S(1)}, u32[]{:S(2)}, u32[]{:S(2)}) collective-permute-start(f32[136,128]{1,0:T(8,128)S(1)} %row_total.2.own_ref), channel_id=1, source_target_pairs={{0,64},{64,0},{128,192},{192,128},{1,65},{65,1},{129,193},{193,129... | collective-permute-start | bytes 208904 | tf_op jit(solution)/shard_map/ppermute | solution.py:397
  26.7 5.7 %collective-permute-start.2 = (f32[128,128]{1,0:T(8,128)S(1)}, f32[128,128]{1,0:T(8,128)S(1)}, u32[]{:S(2)}, u32[]{:S(2)}) collective-permute-start(f32[128,128]{1,0:T(8,128)S(1)} %pair.2), channel_id=1, source_target_pairs={{0,192},{64,128},{128,64},{192,0},{1,193},{65,129},{129,65},{193,1... | collective-permute-start | bytes 196616 | tf_op jit(solution)/shard_map/ppermute | solution.py:397
  43.9 5.1 %collective-permute-start.3 = (f32[8,128,128]{2,1,0:T(8,128)S(1)}, f32[8,128,128]{2,1,0:T(8,128)S(1)}, u32[]{:S(2)}, u32[]{:S(2)}) collective-permute-start(f32[8,128,128]{2,1,0:T(8,128)S(1)} %get-tuple-element.131), channel_id=1, source_target_pairs={{0,4},{4,0},{1,5},{5,1},{2,6},{6,2},{3,7},{7,3},{8,12},{12,8},{9,1... | collective-permute-start | bytes 1572872 | tf_op jit(solution)/shard_map/ppermute | solution.py:393
  49.7 4.3 %collective-permute-start.6 = (f32[8,256]{1,0:T(8,128)S(1)}, f32[8,256]{1,0:T(8,128)S(1)}, u32[]{:S(2)}, u32[]{:S(2)}) collective-permute-start(f32[8,256]{1,0:T(8,128)S(1)} %get-tuple-element.138.sum_a), channel_id=1, source_target_pairs={{0,3},{1,2},{2,1},{3,0},{4,7},{5,6},{6,5},{7,4},{8,11},{9,10},{10,... | collective-permute-start | bytes 24584 | tf_op jit(solution)/shard_map/ppermute | solution.py:397
  52.2 4.0 %collective-permute-start.5 = (f32[8,256]{1,0:T(8,128)S(1)}, f32[8,256]{1,0:T(8,128)S(1)}, u32[]{:S(2)}, u32[]{:S(2)}) collective-permute-start(f32[8,256]{1,0:T(8,128)S(1)} %get-tuple-element.138.sum_a), channel_id=1, source_target_pairs={{0,2},{1,3},{2,0},{3,1},{4,6},{5,7},{6,4},{7,5},{8,10},{9,11},{10,... | collective-permute-start | bytes 24584 | tf_op jit(solution)/shard_map/ppermute | solution.py:397
  52.7 3.5 %collective-permute-start.4 = (f32[8,256]{1,0:T(8,128)S(1)}, f32[8,256]{1,0:T(8,128)S(1)}, u32[]{:S(2)}, u32[]{:S(2)}) collective-permute-start(f32[8,256]{1,0:T(8,128)S(1)} %get-tuple-element.138.sum_a), channel_id=1, source_target_pairs={{0,1},{1,0},{2,3},{3,2},{4,5},{5,4},{6,7},{7,6},{8,9},{9,8},{10,11... | collective-permute-start | bytes 24584 | tf_op jit(solution)/shard_map/ppermute | solution.py:397
  56.9 3.6 %collective-permute-start.7 = (f32[1024,128]{1,0:T(8,128)S(1)}, f32[1024,128]{1,0:T(8,128)S(1)}, u32[]{:S(2)}, u32[]{:S(2)}) collective-permute-start(f32[1024,128]{1,0:T(8,128)S(1)} %get-tuple-element.146), channel_id=1, source_target_pairs={{0,4},{4,0},{1,5},{5,1},{2,6},{6,2},{3,7},{7,3},{8,12},{12,8},{9,1... | collective-permute-start | bytes 1572872 | tf_op jit(solution)/shard_map/ppermute | solution.py:393
  71.8 5.2 %collective-permute-start.8 = (f32[136,128]{1,0:T(8,128)S(1)}, f32[136,128]{1,0:T(8,128)S(1)}, u32[]{:S(2)}, u32[]{:S(2)}) collective-permute-start(f32[136,128]{1,0:T(8,128)S(1)} %row_total.3.own_ref), channel_id=1, source_target_pairs={{0,64},{64,0},{128,192},{192,128},{1,65},{65,1},{129,193},{193,129... | collective-permute-start | bytes 208904 | tf_op jit(solution)/shard_map/ppermute | solution.py:397
  77.0 6.4 %collective-permute-start.9 = (f32[128,128]{1,0:T(8,128)S(1)}, f32[128,128]{1,0:T(8,128)S(1)}, u32[]{:S(2)}, u32[]{:S(2)}) collective-permute-start(f32[128,128]{1,0:T(8,128)S(1)} %pair.3), channel_id=1, source_target_pairs={{0,192},{64,128},{128,64},{192,0},{1,193},{65,129},{129,65},{193,1... | collective-permute-start | bytes 196616 | tf_op jit(solution)/shard_map/ppermute | solution.py:397
  95.8 5.1 %collective-permute-start.10 = (f32[8,128,128]{2,1,0:T(8,128)S(1)}, f32[8,128,128]{2,1,0:T(8,128)S(1)}, u32[]{:S(2)}, u32[]{:S(2)}) collective-permute-start(f32[8,128,128]{2,1,0:T(8,128)S(1)} %get-tuple-element.178), channel_id=1, source_target_pairs={{0,4},{4,0},{1,5},{5,1},{2,6},{6,2},{3,7},{7,3},{8,12},{12,8},{9,1... | collective-permute-start | bytes 1572872 | tf_op jit(solution)/shard_map/ppermute | solution.py:393

commit v7 on v6

--- a/solution.py
+++ b/solution.py
@@ -209,18 +209,28 @@
 
 
 def intra_kernel(
-    role, core_ref, query_ref, keys_ref, value_ref, gate_ref, gain_ref, mixed_ref, tab_ref, across_ref,
-    intra_ref, normed_ref, turned_ref, weights_ref, weighted_ref,
+    role, core_ref, query_hbm, gate_hbm, mixed_hbm, keys_ref, value_ref, gain_ref, tab_ref, across_ref,
+    intra_ref, normed_ref, turned_ref, weights_ref, weighted_ref, query_ref, gate_ref, mixed_ref, sems,
 ):
     core = core_ref[0]
     tab = tab_ref[...]
+    half = pl.ds(pl.multiple_of((core if role == 0 else 1 - core) * WIDE, WIDE), WIDE)
+    copies = [
+        pltpu.make_async_copy(source.at[:, half], target, sems.at[at])
+        for at, (source, target) in enumerate(
+            ((query_hbm, query_ref), (gate_hbm, gate_ref), (mixed_hbm, mixed_ref))
+        )
+    ]
+    for copy in copies:
+        copy.start()
     rows = lax.broadcasted_iota(jnp.int32, (DH, DH), 0)
     cols = lax.broadcasted_iota(jnp.int32, (DH, DH), 1)
     lower, upper = rows >= cols, rows <= cols
+    copies[0].wait()
     for i in range(HALF):
         at = columns(role, core, i)
         to = slice(i * DH, (i + 1) * DH)
-        query, keys = query_ref[:, at], keys_ref[:, at]
+        query, keys = query_ref[:, to], keys_ref[:, at]
         down = lanes(tab, 0, role, i)
         across = across_ref[role * HALF + i : role * HALF + i + 1, :]
         weights = (
@@ -237,8 +247,13 @@
         probs = masked(dot(query, keys, 1, 1), weights[:3])
         turned_ref[i] = masked(dot(keys, query, 1, 1), weights[3:], upper=True)
         intra_ref[:, to] = dot(probs, value_ref[:, at], 1, 0)
-        opening = jax.nn.sigmoid(gate_ref[:, at].astype(F32))
-        normed_ref[:, to] = mixed_ref[:, at].astype(F32) * opening * gain_ref[:, at]
+    copies[1].wait()
+    copies[2].wait()
+    for i in range(HALF):
+        at = columns(role, core, i)
+        to = slice(i * DH, (i + 1) * DH)
+        opening = jax.nn.sigmoid(gate_ref[:, to].astype(F32))
+        normed_ref[:, to] = mixed_ref[:, to].astype(F32) * opening * gain_ref[:, at]
 
 
 def attend_kernel(role, core_ref, query_ref, state_ref, intra_ref, normed_ref, tab_ref, *refs):
@@ -450,15 +465,18 @@
     )
 
     wide = shape(GROUP, WIDE)
+    half = pltpu.VMEM((GROUP, WIDE), BF16)
     probs_shape = shape(HALF, GROUP, GROUP, dtype=BF16)
     weights_shape = shape(HALF, 6, DH, DH)
     weighted_shape = shape(HALF, DH, GROUP, dtype=BF16)
 
     def intra_part(after, role, done):
-        held, _ = lax.optimization_barrier((query, after))
+        table, _ = lax.optimization_barrier((tab, after))
+        far = [pltpu.with_memory_space_constraint(array, pltpu.HBM) for array in (query, gate, upstream)]
         results = call(
             functools.partial(intra_kernel, role), (wide, wide, probs_shape, weights_shape, weighted_shape),
-            core, held, keys, value, gate, gain, upstream, tab, across, flops=3 * big, name=f"intra{role}",
+            core, *far, keys, value, gain, table, across, flops=3 * big, name=f"intra{role}", limit=8,
+            specs=[SMEM] + [HBM] * 3 + [VMEM] * 5, scratch=[half] * 3 + [pltpu.SemaphoreType.DMA((3,))],
         )
         return (*done, results)
 
@@ -492,7 +510,6 @@
         grad_kernel, grads_shape, att_own, intra[0][1], intra[0][4], terms, flops=small, smem=0, name="grad0",
     )
 
-    half = pltpu.VMEM((GROUP, WIDE), BF16)
 
     whole = pltpu.HBM((GROUP, 2 * WIDE), BF16)
 

time: 103 us -> 103 us (level)
  starting transfers between devices: 28.5 us -> 26.4 us
  Pallas kernels: 18.7 us -> 20.7 us
    ppermute x7, starting transfers between devices: 16 us -> 13.9 us  [flipped(): return lax.ppermute(array, axis, [(i, i ^ flip) for i in range(4)])]
    pallas_call x23, Pallas kernels: 18.7 us -> 20.7 us  [call(): pl.pallas_call(kernel, out_shape=out, in_specs=specs or [SMEM] * smem + [...]
  transfers between devices with their start and end apart: 11 -> 11, of which waited for: 7 -> 6; matrix products, arithmetic and copies ran while one was open for 0% -> 0% of each run, Pallas kernels for 13% -> 15%
where the time goes in v7:
time: 103 us; the launch traced here: 102 us
  blocking collectives  48.4 us (47%)
  starting transfers between devices  26.4 us (26%)
  Pallas kernels  20.7 us (20%)
  waiting for transfers between devices  5.93 us (6%)
    all_to_all x4, blocking collectives, spread(): return lax.all_to_all(array, PLANE, 0, 0, tiled=True)  48.4 us
    pallas_call x23, Pallas kernels, call(): pl.pallas_call(kernel, out_shape=out, in_specs=specs or [SMEM] * smem + [...  20.7 us
    ppermute x7, starting transfers between devices, flipped(): return lax.ppermute(array, axis, [(i, i ^ flip) for i in range(4)])  13.9 us
    ppermute x4, starting transfers between devices, swap(): return lax.ppermute(array, 'core', [(0, 1), (1, 0)])  12.5 us
    ppermute x4, waiting for transfers between devices, swap(): return lax.ppermute(array, 'core', [(0, 1), (1, 0)])  2.99 us
    ppermute x7, waiting for transfers between devices, flipped(): return lax.ppermute(array, axis, [(i, i ^ flip) for i in range(4)])  2.94 us
  transfers between devices with their start and end apart: 11, of which 6 were waited for; matrix products, arithmetic and copies ran while one was open for 0% of the time, Pallas kernels for 15%

profile of v7, /device:TPU:1, one launch (start us, length us, event | category | flops | bytes accessed | tf_op | source)
XLA Modules:
  0.0 102.4 jit_solution(16238405632943957153)
XLA Ops:
  0.6 1.8 %first.1 = (f32[16,256]{1,0:T(8,128)S(1)}, f32[1040,128]{1,0:T(8,128)S(1)}, bf16[256,2048]{1,0:T(8,128)(2,1)S(1)}, bf16[256,2048]{1,0:T(8,128)(2,1)S(1)}) custom-call(s32[1]{0:T(128)} %bitcast.core_ref, bf16[256,2048]{1,0:T(8,128)(2,1)} %keys_hbm.1, bf16[256,2048]{1,0:T(8,128)(2,1)} %value_hbm.1, f32[16,256]{1,0:T(8,128)} %bitcast.7), custom_call_target="tpu_custom_call" | custom-call | flops 67108864 | bytes 6856708 | tf_op jit(solution)/shard_map/first/pallas_call | solution.py:28
  2.5 0.0 copy-start.3
  2.5 3.3 %collective-permute-start = (f32[1040,128]{1,0:T(8,128)S(1)}, f32[1040,128]{1,0:T(8,128)S(1)}, u32[]{:S(2)}, u32[]{:S(2)}) collective-permute-start(f32[1040,128]{1,0:T(8,128)S(1)} %get-tuple-element.103), channel_id=1, source_target_pairs={{0,4},{4,0},{1,5},{5,1},{2,6},{6,2},{3,7},{7,3},{8,12},{12,8},{9,1... | collective-permute-start | bytes 1597448 | tf_op jit(solution)/shard_map/ppermute | solution.py:408
  5.8 0.7 second.1
  6.5 0.9 collective-permute-done.other_ref
  7.4 0.1 merge_f.1
  7.5 13.6 %all_to_all.20.parts_ref.decays_ref = f32[8,136,128]{2,1,0:T(8,128)S(1)} all-to-all(f32[8,136,128]{2,1,0:T(8,128)S(1)} %get-tuple-element.104), channel_id=1, replica_groups=mesh['z1'=4,'z0'=2,'y'=4,'core'=2,'head'=4] {'z0','y'}, dimensions={0} | all-to-all | bytes 1114112 | tf_op jit(solution)/shard_map/all_to_all | solution.py:416
  21.1 3.1 %collective-permute-start.1 = (f32[136,128]{1,0:T(8,128)S(1)}, f32[136,128]{1,0:T(8,128)S(1)}, u32[]{:S(2)}, u32[]{:S(2)}) collective-permute-start(f32[136,128]{1,0:T(8,128)S(1)} %row_total.2.own_ref), channel_id=1, source_target_pairs={{0,64},{64,0},{128,192},{192,128},{1,65},{65,1},{129,193},{193,129... | collective-permute-start | bytes 208904 | tf_op jit(solution)/shard_map/ppermute | solution.py:412
  24.2 2.7 %intra0.1 = (f32[256,1024]{1,0:T(8,128)S(1)}, f32[256,1024]{1,0:T(8,128)S(1)}, bf16[8,256,256]{2,1,0:T(8,128)(2,1)S(1)}, f32[8,6,128,128]{3,2,1,0:T(8,128)S(1)}, bf16[8,128,256]{2,1,0:T(8,128)(2,1)S(1)}) custom-call(s32[1]{0:T(128)} %bitcast.core_ref, bf16[256,2048]{1,0:T(8,128)(2,1)} %query_ref.5, bf16[256,2048]{1,0:T(8,128)(2,1)} %gate_ref.1, ...), custom_call_target="tpu_custom_call" | custom-call | flops 402653184 | bytes 13787140 | tf_op jit(solution)/shard_map/intra0/pallas_call | solution.py:28
  27.0 0.0 collective-permute-done.1.near_ref
  27.0 3.5 %collective-permute-start.2 = (f32[128,128]{1,0:T(8,128)S(1)}, f32[128,128]{1,0:T(8,128)S(1)}, u32[]{:S(2)}, u32[]{:S(2)}) collective-permute-start(f32[128,128]{1,0:T(8,128)S(1)} %pair.2), channel_id=1, source_target_pairs={{0,192},{64,128},{128,64},{192,0},{1,193},{65,129},{129,65},{193,1... | collective-permute-start | bytes 196616 | tf_op jit(solution)/shard_map/ppermute | solution.py:412
  30.5 2.7 %intra1.1 = (f32[256,1024]{1,0:T(8,128)S(1)}, f32[256,1024]{1,0:T(8,128)S(1)}, bf16[8,256,256]{2,1,0:T(8,128)(2,1)S(1)}, f32[8,6,128,128]{3,2,1,0:T(8,128)S(1)}, bf16[8,128,256]{2,1,0:T(8,128)(2,1)S(1)}) custom-call(s32[1]{0:T(128)} %bitcast.core_ref, bf16[256,2048]{1,0:T(8,128)(2,1)} %query_ref.5, bf16[256,2048]{1,0:T(8,128)(2,1)} %gate_ref.1, ...), custom_call_target="tpu_custom_call" | custom-call | flops 402653184 | bytes 13787140 | tf_op jit(solution)/shard_map/intra1/pallas_call | solution.py:28
  33.2 0.0 copy-start
  33.3 0.0 collective-permute-done.2.far_ref
  33.3 0.1 enter.2
  33.3 11.5 %all_to_all.21.enter_ref = f32[8,128,128]{2,1,0:T(8,128)S(1)} all-to-all(f32[8,128,128]{2,1,0:T(8,128)S(1)} %enter.2), channel_id=1, replica_groups=mesh['z1'=4,'z0'=2,'y'=4,'core'=2,'head'=4] {'z0','y'}, dimensions={0} | all-to-all | bytes 1048576 | tf_op jit(solution)/shard_map/all_to_all | solution.py:416
  44.9 0.1 leave.2
  45.0 3.5 %collective-permute-start.3 = (f32[8,128,128]{2,1,0:T(8,128)S(1)}, f32[8,128,128]{2,1,0:T(8,128)S(1)}, u32[]{:S(2)}, u32[]{:S(2)}) collective-permute-start(f32[8,128,128]{2,1,0:T(8,128)S(1)} %get-tuple-element.131), channel_id=1, source_target_pairs={{0,4},{4,0},{1,5},{5,1},{2,6},{6,2},{3,7},{7,3},{8,12},{12,8},{9,1... | collective-permute-start | bytes 1572872 | tf_op jit(solution)/shard_map/ppermute | solution.py:408
  48.5 0.5 attend0.1
  49.1 1.0 collective-permute-done.3.state_ref
  50.1 0.7 attend1.1
  50.7 2.6 %collective-permute-start.6 = (f32[8,256]{1,0:T(8,128)S(1)}, f32[8,256]{1,0:T(8,128)S(1)}, u32[]{:S(2)}, u32[]{:S(2)}) collective-permute-start(f32[8,256]{1,0:T(8,128)S(1)} %get-tuple-element.138.sum_a), channel_id=1, source_target_pairs={{0,3},{1,2},{2,1},{3,0},{4,7},{5,6},{6,5},{7,4},{8,11},{9,10},{10,... | collective-permute-start | bytes 24584 | tf_op jit(solution)/shard_map/ppermute | solution.py:412
  53.3 0.5 collective-permute-start.5
  53.8 0.3 collective-permute-start.4
  54.1 0.0 copy-done.2
  54.1 0.9 opened.1
  55.0 0.0 collective-permute-done.6.sum_d
  55.0 2.3 %collective-permute-done.5.sum_c = f32[8,256]{1,0:T(8,128)S(1)} collective-permute-done((f32[8,256]{1,0:T(8,128)S(1)}, f32[8,256]{1,0:T(8,128)S(1)}, u32[]{:S(2)}, u32[]{:S(2)}) %collective-permute-start.5) | collective-permute-done | bytes 8224 | tf_op jit(solution)/shard_map/ppermute | solution.py:412
  57.3 0.0 collective-permute-done.4.sum_b
  57.3 0.7 grad1.1
  58.0 2.1 %collective-permute-start.7 = (f32[1024,128]{1,0:T(8,128)S(1)}, f32[1024,128]{1,0:T(8,128)S(1)}, u32[]{:S(2)}, u32[]{:S(2)}) collective-permute-start(f32[1024,128]{1,0:T(8,128)S(1)} %get-tuple-element.146), channel_id=1, source_target_pairs={{0,4},{4,0},{1,5},{5,1},{2,6},{6,2},{3,7},{7,3},{8,12},{12,8},{9,1... | collective-permute-start | bytes 1572872 | tf_op jit(solution)/shard_map/ppermute | solution.py:408
  60.1 0.5 grad0.1
  60.6 1.0 collective-permute-done.7.other_ref
  61.6 0.1 merge_b.1
  61.7 11.1 %all_to_all.22.parts_ref = f32[8,128,128]{2,1,0:T(8,128)S(1)} all-to-all(f32[8,128,128]{2,1,0:T(8,128)S(1)} %merge_b.1), channel_id=1, replica_groups=mesh['z1'=4,'z0'=2,'y'=4,'core'=2,'head'=4] {'z0','y'}, dimensions={0} | all-to-all | bytes 1048576 | tf_op jit(solution)/shard_map/all_to_all | solution.py:416
  72.9 1.3 %collective-permute-start.8 = (f32[136,128]{1,0:T(8,128)S(1)}, f32[136,128]{1,0:T(8,128)S(1)}, u32[]{:S(2)}, u32[]{:S(2)}) collective-permute-start(f32[136,128]{1,0:T(8,128)S(1)} %row_total.3.own_ref), channel_id=1, source_target_pairs={{0,64},{64,0},{128,192},{192,128},{1,65},{65,1},{129,193},{193,129... | collective-permute-start | bytes 208904 | tf_op jit(solution)/shard_map/ppermute | solution.py:412
  74.2 2.9 %local0.1 = (bf16[256,2048]{1,0:T(8,128)(2,1)}, bf16[256,2048]{1,0:T(8,128)(2,1)}, bf16[256,2048]{1,0:T(8,128)(2,1)}, f32[256,1024]{1,0:T(8,128)S(1)}, f32[256,1024]{1,0:T(8,128)S(1)}) custom-call(s32[1]{0:T(128)} %bitcast.core_ref, bf16[256,2048]{1,0:T(8,128)(2,1)S(1)} %copy-done, bf16[256,2048]{1,0:T(8,128)(2,1)S(1)} %get-tuple-element.99.keys_ref, ...), custom_call_target="tpu_custom_call" | custom-call | flops 671088640 | bytes 21233668 | tf_op jit(solution)/shard_map/local0/pallas_call | solution.py:28
  77.1 0.6 collective-permute-done.8.near_ref
  77.8 2.7 %collective-permute-start.9 = (f32[128,128]{1,0:T(8,128)S(1)}, f32[128,128]{1,0:T(8,128)S(1)}, u32[]{:S(2)}, u32[]{:S(2)}) collective-permute-start(f32[128,128]{1,0:T(8,128)S(1)} %pair.3), channel_id=1, source_target_pairs={{0,192},{64,128},{128,64},{192,0},{1,193},{65,129},{129,65},{193,1... | collective-permute-start | bytes 196616 | tf_op jit(solution)/shard_map/ppermute | solution.py:412
  80.5 2.9 %local1.1 = (bf16[256,2048]{1,0:T(8,128)(2,1)}, bf16[256,2048]{1,0:T(8,128)(2,1)}, bf16[256,2048]{1,0:T(8,128)(2,1)}, f32[256,1024]{1,0:T(8,128)S(1)}, f32[256,1024]{1,0:T(8,128)S(1)}) custom-call(s32[1]{0:T(128)} %bitcast.core_ref, bf16[256,2048]{1,0:T(8,128)(2,1)S(1)} %copy-done, ...), custom_call_target="tpu_custom_call", output_to_operand_aliasing={{0}: (12, {}), {1}: (13, {}), {2}: (14, {})} | custom-call | flops 671088640 | bytes 24379396 | tf_op jit(solution)/shard_map/local1/pallas_call | solution.py:28
  83.4 0.0 collective-permute-done.9.far_ref
  83.4 0.1 enter.3
  83.5 12.2 %all_to_all.23.enter_ref = f32[8,128,128]{2,1,0:T(8,128)S(1)} all-to-all(f32[8,128,128]{2,1,0:T(8,128)S(1)} %enter.3), channel_id=1, replica_groups=mesh['z1'=4,'z0'=2,'y'=4,'core'=2,'head'=4] {'z0','y'}, dimensions={0} | all-to-all | bytes 1048576 | tf_op jit(solution)/shard_map/all_to_all | solution.py:416
  95.7 0.1 leave.3
  95.8 3.6 %collective-permute-start.10 = (f32[8,128,128]{2,1,0:T(8,128)S(1)}, f32[8,128,128]{2,1,0:T(8,128)S(1)}, u32[]{:S(2)}, u32[]{:S(2)}) collective-permute-start(f32[8,128,128]{2,1,0:T(8,128)S(1)} %get-tuple-element.178), channel_id=1, source_target_pairs={{0,4},{4,0},{1,5},{5,1},{2,6},{6,2},{3,7},{7,3},{8,12},{12,8},{9,1... | collective-permute-start | bytes 1572872 | tf_op jit(solution)/shard_map/ppermute | solution.py:408
  99.3 1.4 %last0.1 = (bf16[256,2048]{1,0:T(8,128)(2,1)}, bf16[256,2048]{1,0:T(8,128)(2,1)}) custom-call(s32[1]{0:T(128)} %bitcast.core_ref, bf16[256,2048]{1,0:T(8,128)(2,1)S(1)} %get-tuple-element.99.keys_ref, bf16[256,2048]{1,0:T(8,128)(2,1)S(1)} %get-tuple-element.100.value_ref, f32[8,128,128]{2,1,0:T(8,128)S(1)} %get-tuple-element.181.state_ref, ...), custom_call_target="tpu_custom_call" | custom-call | flops 134217728 | bytes 9043972 | tf_op jit(solution)/shard_map/last0/pallas_call | solution.py:28
  100.7 0.1 collective-permute-done.10.state_ref
  100.9 1.4 %last1.1 = (bf16[256,2048]{1,0:T(8,128)(2,1)}, bf16[256,2048]{1,0:T(8,128)(2,1)}) custom-call(s32[1]{0:T(128)} %bitcast.core_ref, bf16[256,2048]{1,0:T(8,128)(2,1)S(1)} %get-tuple-element.99.keys_ref, bf16[256,2048]{1,0:T(8,128)(2,1)S(1)} %get-tuple-element.100.value_ref, ...), custom_call_target="tpu_custom_call", output_to_operand_aliasing={{0}: (7, {}), {1}: (8, {})} | custom-call | flops 134217728 | bytes 11141124 | tf_op jit(solution)/shard_map/last1/pallas_call | solution.py:28
  (9 shorter events, 0.1 us)
Async XLA Ops:
  2.5 21.8 %copy-start.3 = (f32[2048]{0:T(1024)S(1)}, f32[2048]{0:T(1024)}, u32[]{:S(2)}) copy-start(f32[2048]{0:T(1024)} %param.12) | copy-start | bytes 24580
  2.5 4.9 %collective-permute-start = (f32[1040,128]{1,0:T(8,128)S(1)}, f32[1040,128]{1,0:T(8,128)S(1)}, u32[]{:S(2)}, u32[]{:S(2)}) collective-permute-start(f32[1040,128]{1,0:T(8,128)S(1)} %get-tuple-element.103), channel_id=1, source_target_pairs={{0,4},{4,0},{1,5},{5,1},{2,6},{6,2},{3,7},{7,3},{8,12},{12,8},{9,1... | collective-permute-start | bytes 1597448 | tf_op jit(solution)/shard_map/ppermute | solution.py:408
  21.1 5.8 %collective-permute-start.1 = (f32[136,128]{1,0:T(8,128)S(1)}, f32[136,128]{1,0:T(8,128)S(1)}, u32[]{:S(2)}, u32[]{:S(2)}) collective-permute-start(f32[136,128]{1,0:T(8,128)S(1)} %row_total.2.own_ref), channel_id=1, source_target_pairs={{0,64},{64,0},{128,192},{192,128},{1,65},{65,1},{129,193},{193,129... | collective-permute-start | bytes 208904 | tf_op jit(solution)/shard_map/ppermute | solution.py:412
  27.0 6.3 %collective-permute-start.2 = (f32[128,128]{1,0:T(8,128)S(1)}, f32[128,128]{1,0:T(8,128)S(1)}, u32[]{:S(2)}, u32[]{:S(2)}) collective-permute-start(f32[128,128]{1,0:T(8,128)S(1)} %pair.2), channel_id=1, source_target_pairs={{0,192},{64,128},{128,64},{192,0},{1,193},{65,129},{129,65},{193,1... | collective-permute-start | bytes 196616 | tf_op jit(solution)/shard_map/ppermute | solution.py:412
  33.2 15.3 %copy-start = (bf16[256,2048]{1,0:T(8,128)(2,1)S(1)}, bf16[256,2048]{1,0:T(8,128)(2,1)}, u32[]{:S(2)}) copy-start(bf16[256,2048]{1,0:T(8,128)(2,1)} %query_ref.5) | copy-start | bytes 3145732
  45.0 5.1 %collective-permute-start.3 = (f32[8,128,128]{2,1,0:T(8,128)S(1)}, f32[8,128,128]{2,1,0:T(8,128)S(1)}, u32[]{:S(2)}, u32[]{:S(2)}) collective-permute-start(f32[8,128,128]{2,1,0:T(8,128)S(1)} %get-tuple-element.131), channel_id=1, source_target_pairs={{0,4},{4,0},{1,5},{5,1},{2,6},{6,2},{3,7},{7,3},{8,12},{12,8},{9,1... | collective-permute-start | bytes 1572872 | tf_op jit(solution)/shard_map/ppermute | solution.py:408
  48.5 5.6 %copy-start.1 = (bf16[256,2048]{1,0:T(8,128)(2,1)S(1)}, bf16[256,2048]{1,0:T(8,128)(2,1)}, u32[]{:S(2)}) copy-start(bf16[256,2048]{1,0:T(8,128)(2,1)} %gate_ref.1) | copy-start | bytes 3145732
  48.5 5.6 %copy-start.2 = (bf16[256,2048]{1,0:T(8,128)(2,1)S(1)}, bf16[256,2048]{1,0:T(8,128)(2,1)}, u32[]{:S(2)}) copy-start(bf16[256,2048]{1,0:T(8,128)(2,1)} %upstream_ref.1) | copy-start | bytes 3145732
  50.7 4.3 %collective-permute-start.6 = (f32[8,256]{1,0:T(8,128)S(1)}, f32[8,256]{1,0:T(8,128)S(1)}, u32[]{:S(2)}, u32[]{:S(2)}) collective-permute-start(f32[8,256]{1,0:T(8,128)S(1)} %get-tuple-element.138.sum_a), channel_id=1, source_target_pairs={{0,3},{1,2},{2,1},{3,0},{4,7},{5,6},{6,5},{7,4},{8,11},{9,10},{10,... | collective-permute-start | bytes 24584 | tf_op jit(solution)/shard_map/ppermute | solution.py:412
  53.3 4.0 %collective-permute-start.5 = (f32[8,256]{1,0:T(8,128)S(1)}, f32[8,256]{1,0:T(8,128)S(1)}, u32[]{:S(2)}, u32[]{:S(2)}) collective-permute-start(f32[8,256]{1,0:T(8,128)S(1)} %get-tuple-element.138.sum_a), channel_id=1, source_target_pairs={{0,2},{1,3},{2,0},{3,1},{4,6},{5,7},{6,4},{7,5},{8,10},{9,11},{10,... | collective-permute-start | bytes 24584 | tf_op jit(solution)/shard_map/ppermute | solution.py:412
  53.8 3.5 %collective-permute-start.4 = (f32[8,256]{1,0:T(8,128)S(1)}, f32[8,256]{1,0:T(8,128)S(1)}, u32[]{:S(2)}, u32[]{:S(2)}) collective-permute-start(f32[8,256]{1,0:T(8,128)S(1)} %get-tuple-element.138.sum_a), channel_id=1, source_target_pairs={{0,1},{1,0},{2,3},{3,2},{4,5},{5,4},{6,7},{7,6},{8,9},{9,8},{10,11... | collective-permute-start | bytes 24584 | tf_op jit(solution)/shard_map/ppermute | solution.py:412
  58.0 3.6 %collective-permute-start.7 = (f32[1024,128]{1,0:T(8,128)S(1)}, f32[1024,128]{1,0:T(8,128)S(1)}, u32[]{:S(2)}, u32[]{:S(2)}) collective-permute-start(f32[1024,128]{1,0:T(8,128)S(1)} %get-tuple-element.146), channel_id=1, source_target_pairs={{0,4},{4,0},{1,5},{5,1},{2,6},{6,2},{3,7},{7,3},{8,12},{12,8},{9,1... | collective-permute-start | bytes 1572872 | tf_op jit(solution)/shard_map/ppermute | solution.py:408
  72.9 4.9 %collective-permute-start.8 = (f32[136,128]{1,0:T(8,128)S(1)}, f32[136,128]{1,0:T(8,128)S(1)}, u32[]{:S(2)}, u32[]{:S(2)}) collective-permute-start(f32[136,128]{1,0:T(8,128)S(1)} %row_total.3.own_ref), channel_id=1, source_target_pairs={{0,64},{64,0},{128,192},{192,128},{1,65},{65,1},{129,193},{193,129... | collective-permute-start | bytes 208904 | tf_op jit(solution)/shard_map/ppermute | solution.py:412
  77.8 5.6 %collective-permute-start.9 = (f32[128,128]{1,0:T(8,128)S(1)}, f32[128,128]{1,0:T(8,128)S(1)}, u32[]{:S(2)}, u32[]{:S(2)}) collective-permute-start(f32[128,128]{1,0:T(8,128)S(1)} %pair.3), channel_id=1, source_target_pairs={{0,192},{64,128},{128,64},{192,0},{1,193},{65,129},{129,65},{193,1... | collective-permute-start | bytes 196616 | tf_op jit(solution)/shard_map/ppermute | solution.py:412
  95.8 5.1 %collective-permute-start.10 = (f32[8,128,128]{2,1,0:T(8,128)S(1)}, f32[8,128,128]{2,1,0:T(8,128)S(1)}, u32[]{:S(2)}, u32[]{:S(2)}) collective-permute-start(f32[8,128,128]{2,1,0:T(8,128)S(1)} %get-tuple-element.178), channel_id=1, source_target_pairs={{0,4},{4,0},{1,5},{5,1},{2,6},{6,2},{3,7},{7,3},{8,12},{12,8},{9,1... | collective-permute-start | bytes 1572872 | tf_op jit(solution)/shard_map/ppermute | solution.py:408

commit v8 on v6

--- a/solution.py
+++ b/solution.py
@@ -59,6 +59,23 @@
     return pl.ds(pl.multiple_of(side * WIDE + i * DH, DH), DH)
 
 
+def pairs(role, core, i):
+    side = core if role == 0 else 1 - core
+    return pl.ds(pl.multiple_of(side * WIDE + i * DH, 2 * DH), 2 * DH)
+
+
+def both_lanes(tab, which, role, i):
+    parts = [jnp.broadcast_to(lanes(tab, which, role, at), (GROUP, DH)) for at in (i, i + 1)]
+    return jnp.concatenate(parts, axis=1)
+
+
+def diagonal(first, second):
+    blank = jnp.zeros_like(first)
+    return jnp.concatenate(
+        [jnp.concatenate([first, blank], axis=1), jnp.concatenate([blank, second], axis=1)], axis=0
+    )
+
+
 def lanes(tab, which, role, i):
     at = which * 16 + role * HALF + i
     return tab[:, at : at + 1]
@@ -180,17 +197,16 @@
             state = jnp.exp(decays_ref[at, DH : DH + 1, :]) * state + parts_ref[at, :DH, :]
 
 
-def leave_kernel(reverse, core_ref, enter_ref, own_ref, other_ref, dec_ref, keep_ref, send_ref):
+def leave_kernel(reverse, send, core_ref, enter_ref, own_ref, other_ref, dec_ref, out_ref):
     first = core_ref[0] == (1 if reverse else 0)
+    straight = ~first if send else first
     base = HALF if reverse else 0
     for i in range(HALF):
         own = own_ref[i * DH : (i + 1) * DH, :]
         other = other_ref[i * DH : (i + 1) * DH, :]
-        nearer = jnp.where(first, own, other)
         x = enter_ref[i]
-        y = dec_ref[base + i : base + i + 1, :] * x + nearer
-        keep_ref[i] = jnp.where(first, x, y)
-        send_ref[i] = jnp.where(first, y, x)
+        y = dec_ref[base + i : base + i + 1, :] * x + jnp.where(first, own, other)
+        out_ref[i] = jnp.where(straight, x, y)
 
 
 LOW, HIGH = slice(0, DH), slice(DH, GROUP)
@@ -374,18 +390,17 @@
     core = core_ref[0]
     tab = tab_ref[...]
     sender = Sender(role, core, sems)
-    for i in range(HALF):
-        at = columns(role, core, i)
-        to = slice(i * DH, (i + 1) * DH)
-        state = state_ref[i].astype(BF16)
-        toward_end = lanes(tab, 2, role, i)
-        grad_keys = part_keys[:, to] + dot(value_ref[:, at], state, 1, 1) * toward_end
-        grad_value = part_value[:, to] + dot(keys_ref[:, at], state, 1, 0) * toward_end
+    for i in range(0, HALF, 2):
+        at = pairs(role, core, i)
+        to = slice(i * DH, (i + 2) * DH)
+        states = diagonal(state_ref[i].astype(BF16), state_ref[i + 1].astype(BF16))
+        toward_end = both_lanes(tab, 2, role, i)
+        grad_keys = part_keys[:, to] + dot(value_ref[:, at], states, 1, 1) * toward_end
         keys_buf[:, to] = grad_keys.astype(BF16)
+        sender.send(keys_buf, keys_out, i * DH, 2 * DH)
+        grad_value = part_value[:, to] + dot(keys_ref[:, at], states, 1, 0) * toward_end
         value_buf[:, to] = grad_value.astype(BF16)
-        if i % 2 == 1:
-            for buf, out in ((keys_buf, keys_out), (value_buf, value_out)):
-                sender.send(buf, out, (i - 1) * DH, 2 * DH)
+        sender.send(value_buf, value_out, i * DH, 2 * DH)
     sender.wait()
 
 
@@ -420,10 +435,12 @@
         functools.partial(enter_kernel, reverse), shape(8, DH, DH), place, parts, decays, near, far, name="enter"
     )
     entering = spread(entering)
-    keep, send = call(
-        functools.partial(leave_kernel, reverse),
-        (shape(HALF, DH, DH), shape(HALF, DH, DH)),
-        core, entering, own, other, dec, name="leave",
+    send, keep = (
+        call(
+            functools.partial(leave_kernel, reverse, away), shape(HALF, DH, DH), core, entering, own, other, dec,
+            name="leave" if away else "keep",
+        )
+        for away in (True, False)
     )
     return keep, swap(send), dec, decays, done
 

time: 103 us -> 103 us (level)
    pallas_call x23 -> x25, Pallas kernels: 18.7 us -> 18.7 us  [call(): pl.pallas_call(kernel, out_shape=out, in_specs=specs or [SMEM] * smem + [...]
where the time goes in v8:
time: 103 us; the launch traced here: 102 us
  blocking collectives  48.1 us (47%)
  starting transfers between devices  28.5 us (28%)
  Pallas kernels  18.7 us (18%)
  waiting for transfers between devices  5.99 us (6%)
    all_to_all x4, blocking collectives, spread(): return lax.all_to_all(array, PLANE, 0, 0, tiled=True)  48.1 us
    pallas_call x25, Pallas kernels, call(): pl.pallas_call(kernel, out_shape=out, in_specs=specs or [SMEM] * smem + [...  18.7 us
    ppermute x7, starting transfers between devices, flipped(): return lax.ppermute(array, axis, [(i, i ^ flip) for i in range(4)])  16 us
    ppermute x4, starting transfers between devices, swap(): return lax.ppermute(array, 'core', [(0, 1), (1, 0)])  12.5 us
    ppermute x7, waiting for transfers between devices, flipped(): return lax.ppermute(array, axis, [(i, i ^ flip) for i in range(4)])  3.16 us
    ppermute x4, waiting for transfers between devices, swap(): return lax.ppermute(array, 'core', [(0, 1), (1, 0)])  2.83 us
  transfers between devices with their start and end apart: 11, of which 7 were waited for; matrix products, arithmetic and copies ran while one was open for 0% of the time, Pallas kernels for 13%

profile of v8, /device:TPU:1, one launch (start us, length us, event | category | flops | bytes accessed | tf_op | source)
XLA Modules:
  0.0 102.3 jit_solution(8084258930549684235)
XLA Ops:
  0.6 1.8 %first.1 = (f32[16,256]{1,0:T(8,128)S(1)}, f32[1040,128]{1,0:T(8,128)S(1)}, bf16[256,2048]{1,0:T(8,128)(2,1)S(1)}, bf16[256,2048]{1,0:T(8,128)(2,1)S(1)}) custom-call(s32[1]{0:T(128)} %bitcast.core_ref, bf16[256,2048]{1,0:T(8,128)(2,1)} %keys_hbm.1, bf16[256,2048]{1,0:T(8,128)(2,1)} %value_hbm.1, f32[16,256]{1,0:T(8,128)} %bitcast.7), custom_call_target="tpu_custom_call" | custom-call | flops 67108864 | bytes 6856708 | tf_op jit(solution)/shard_map/first/pallas_call | solution.py:28
  2.5 0.0 copy-start
  2.5 0.0 copy-start.1
  2.5 0.0 copy-start.2
  2.5 0.0 copy-start.3
  2.5 3.3 %collective-permute-start = (f32[1040,128]{1,0:T(8,128)S(1)}, f32[1040,128]{1,0:T(8,128)S(1)}, u32[]{:S(2)}, u32[]{:S(2)}) collective-permute-start(f32[1040,128]{1,0:T(8,128)S(1)} %get-tuple-element.99), channel_id=1, source_target_pairs={{0,4},{4,0},{1,5},{5,1},{2,6},{6,2},{3,7},{7,3},{8,12},{12,8},{9,1... | collective-permute-start | bytes 1597448 | tf_op jit(solution)/shard_map/ppermute | solution.py:408
  5.8 0.7 second.1
  6.5 0.9 collective-permute-done.other_ref
  7.4 0.1 merge_f.1
  7.5 13.6 %all_to_all.20.parts_ref.decays_ref = f32[8,136,128]{2,1,0:T(8,128)S(1)} all-to-all(f32[8,136,128]{2,1,0:T(8,128)S(1)} %get-tuple-element.100), channel_id=1, replica_groups=mesh['z1'=4,'z0'=2,'y'=4,'core'=2,'head'=4] {'z0','y'}, dimensions={0} | all-to-all | bytes 1114112 | tf_op jit(solution)/shard_map/all_to_all | solution.py:416
  21.2 3.1 %collective-permute-start.1 = (f32[136,128]{1,0:T(8,128)S(1)}, f32[136,128]{1,0:T(8,128)S(1)}, u32[]{:S(2)}, u32[]{:S(2)}) collective-permute-start(f32[136,128]{1,0:T(8,128)S(1)} %row_total.2.own_ref), channel_id=1, source_target_pairs={{0,64},{64,0},{128,192},{192,128},{1,65},{65,1},{129,193},{193,129... | collective-permute-start | bytes 208904 | tf_op jit(solution)/shard_map/ppermute | solution.py:412
  24.3 1.7 %intra0.1 = (f32[256,1024]{1,0:T(8,128)S(1)}, f32[256,1024]{1,0:T(8,128)S(1)}, bf16[8,256,256]{2,1,0:T(8,128)(2,1)S(1)}, f32[8,6,128,128]{3,2,1,0:T(8,128)S(1)}, bf16[8,128,256]{2,1,0:T(8,128)(2,1)S(1)}) custom-call(s32[1]{0:T(128)} %bitcast.core_ref, bf16[256,2048]{1,0:T(8,128)(2,1)S(1)} %copy-done, bf16[256,2048]{1,0:T(8,128)(2,1)S(1)} %get-tuple-element.95.keys_ref, ...), custom_call_target="tpu_custom_call" | custom-call | flops 402653184 | bytes 13787140 | tf_op jit(solution)/shard_map/intra0/pallas_call | solution.py:28
  26.0 0.7 collective-permute-done.1.near_ref
  26.7 3.8 %collective-permute-start.2 = (f32[128,128]{1,0:T(8,128)S(1)}, f32[128,128]{1,0:T(8,128)S(1)}, u32[]{:S(2)}, u32[]{:S(2)}) collective-permute-start(f32[128,128]{1,0:T(8,128)S(1)} %pair.2), channel_id=1, source_target_pairs={{0,192},{64,128},{128,64},{192,0},{1,193},{65,129},{129,65},{193,1... | collective-permute-start | bytes 196616 | tf_op jit(solution)/shard_map/ppermute | solution.py:412
  30.6 1.7 %intra1.1 = (f32[256,1024]{1,0:T(8,128)S(1)}, f32[256,1024]{1,0:T(8,128)S(1)}, bf16[8,256,256]{2,1,0:T(8,128)(2,1)S(1)}, f32[8,6,128,128]{3,2,1,0:T(8,128)S(1)}, bf16[8,128,256]{2,1,0:T(8,128)(2,1)S(1)}) custom-call(s32[1]{0:T(128)} %bitcast.core_ref, bf16[256,2048]{1,0:T(8,128)(2,1)S(1)} %copy-done, bf16[256,2048]{1,0:T(8,128)(2,1)S(1)} %get-tuple-element.95.keys_ref, ...), custom_call_target="tpu_custom_call" | custom-call | flops 402653184 | bytes 13787140 | tf_op jit(solution)/shard_map/intra1/pallas_call | solution.py:28
  32.3 0.2 collective-permute-done.2.far_ref
  32.5 0.1 enter.2
  32.5 11.2 %all_to_all.21.enter_ref = f32[8,128,128]{2,1,0:T(8,128)S(1)} all-to-all(f32[8,128,128]{2,1,0:T(8,128)S(1)} %enter.2), channel_id=1, replica_groups=mesh['z1'=4,'z0'=2,'y'=4,'core'=2,'head'=4] {'z0','y'}, dimensions={0} | all-to-all | bytes 1048576 | tf_op jit(solution)/shard_map/all_to_all | solution.py:416
  43.7 0.1 leave.2
  43.9 3.6 %collective-permute-start.3 = (f32[8,128,128]{2,1,0:T(8,128)S(1)}, f32[8,128,128]{2,1,0:T(8,128)S(1)}, u32[]{:S(2)}, u32[]{:S(2)}) collective-permute-start(f32[8,128,128]{2,1,0:T(8,128)S(1)} %leave.2), channel_id=1, source_target_pairs={{0,4},{4,0},{1,5},{5,1},{2,6},{6,2},{3,7},{7,3},{8,12},{12,8},{9,1... | collective-permute-start | bytes 1572872 | tf_op jit(solution)/shard_map/ppermute | solution.py:408
  47.4 0.1 keep.2.state_ref
  47.5 0.6 attend0.1
  48.1 0.8 collective-permute-done.3.state_ref
  49.0 0.7 attend1.1
  49.6 2.6 %collective-permute-start.6 = (f32[8,256]{1,0:T(8,128)S(1)}, f32[8,256]{1,0:T(8,128)S(1)}, u32[]{:S(2)}, u32[]{:S(2)}) collective-permute-start(f32[8,256]{1,0:T(8,128)S(1)} %get-tuple-element.132.sum_a), channel_id=1, source_target_pairs={{0,3},{1,2},{2,1},{3,0},{4,7},{5,6},{6,5},{7,4},{8,11},{9,10},{10,... | collective-permute-start | bytes 24584 | tf_op jit(solution)/shard_map/ppermute | solution.py:412
  52.2 0.5 collective-permute-start.5
  52.7 0.3 collective-permute-start.4
  53.0 0.9 opened.1
  53.9 0.0 collective-permute-done.6.sum_d
  53.9 2.3 %collective-permute-done.5.sum_c = f32[8,256]{1,0:T(8,128)S(1)} collective-permute-done((f32[8,256]{1,0:T(8,128)S(1)}, f32[8,256]{1,0:T(8,128)S(1)}, u32[]{:S(2)}, u32[]{:S(2)}) %collective-permute-start.5) | collective-permute-done | bytes 8224 | tf_op jit(solution)/shard_map/ppermute | solution.py:412
  56.2 0.7 grad1.1
  56.9 2.1 %collective-permute-start.7 = (f32[1024,128]{1,0:T(8,128)S(1)}, f32[1024,128]{1,0:T(8,128)S(1)}, u32[]{:S(2)}, u32[]{:S(2)}) collective-permute-start(f32[1024,128]{1,0:T(8,128)S(1)} %get-tuple-element.140), channel_id=1, source_target_pairs={{0,4},{4,0},{1,5},{5,1},{2,6},{6,2},{3,7},{7,3},{8,12},{12,8},{9,1... | collective-permute-start | bytes 1572872 | tf_op jit(solution)/shard_map/ppermute | solution.py:408
  59.0 0.5 grad0.1
  59.5 1.0 collective-permute-done.7.other_ref
  60.5 0.1 merge_b.1
  60.6 11.1 %all_to_all.22.parts_ref = f32[8,128,128]{2,1,0:T(8,128)S(1)} all-to-all(f32[8,128,128]{2,1,0:T(8,128)S(1)} %merge_b.1), channel_id=1, replica_groups=mesh['z1'=4,'z0'=2,'y'=4,'core'=2,'head'=4] {'z0','y'}, dimensions={0} | all-to-all | bytes 1048576 | tf_op jit(solution)/shard_map/all_to_all | solution.py:416
  71.8 2.3 %collective-permute-start.8 = (f32[136,128]{1,0:T(8,128)S(1)}, f32[136,128]{1,0:T(8,128)S(1)}, u32[]{:S(2)}, u32[]{:S(2)}) collective-permute-start(f32[136,128]{1,0:T(8,128)S(1)} %row_total.3.own_ref), channel_id=1, source_target_pairs={{0,64},{64,0},{128,192},{192,128},{1,65},{65,1},{129,193},{193,129... | collective-permute-start | bytes 208904 | tf_op jit(solution)/shard_map/ppermute | solution.py:412
  74.0 2.9 %local0.1 = (bf16[256,2048]{1,0:T(8,128)(2,1)}, bf16[256,2048]{1,0:T(8,128)(2,1)}, bf16[256,2048]{1,0:T(8,128)(2,1)}, f32[256,1024]{1,0:T(8,128)S(1)}, f32[256,1024]{1,0:T(8,128)S(1)}) custom-call(s32[1]{0:T(128)} %bitcast.core_ref, bf16[256,2048]{1,0:T(8,128)(2,1)S(1)} %copy-done, bf16[256,2048]{1,0:T(8,128)(2,1)S(1)} %get-tuple-element.95.keys_ref, ...), custom_call_target="tpu_custom_call" | custom-call | flops 671088640 | bytes 21233668 | tf_op jit(solution)/shard_map/local0/pallas_call | solution.py:28
  77.0 3.5 %collective-permute-start.9 = (f32[128,128]{1,0:T(8,128)S(1)}, f32[128,128]{1,0:T(8,128)S(1)}, u32[]{:S(2)}, u32[]{:S(2)}) collective-permute-start(f32[128,128]{1,0:T(8,128)S(1)} %pair.3), channel_id=1, source_target_pairs={{0,192},{64,128},{128,64},{192,0},{1,193},{65,129},{129,65},{193,1... | collective-permute-start | bytes 196616 | tf_op jit(solution)/shard_map/ppermute | solution.py:412
  80.5 2.9 %local1.1 = (bf16[256,2048]{1,0:T(8,128)(2,1)}, bf16[256,2048]{1,0:T(8,128)(2,1)}, bf16[256,2048]{1,0:T(8,128)(2,1)}, f32[256,1024]{1,0:T(8,128)S(1)}, f32[256,1024]{1,0:T(8,128)S(1)}) custom-call(s32[1]{0:T(128)} %bitcast.core_ref, bf16[256,2048]{1,0:T(8,128)(2,1)S(1)} %copy-done, ...), custom_call_target="tpu_custom_call", output_to_operand_aliasing={{0}: (12, {}), {1}: (13, {}), {2}: (14, {})} | custom-call | flops 671088640 | bytes 24379396 | tf_op jit(solution)/shard_map/local1/pallas_call | solution.py:28
  83.4 0.1 enter.3
  83.5 12.1 %all_to_all.23.enter_ref = f32[8,128,128]{2,1,0:T(8,128)S(1)} all-to-all(f32[8,128,128]{2,1,0:T(8,128)S(1)} %enter.3), channel_id=1, replica_groups=mesh['z1'=4,'z0'=2,'y'=4,'core'=2,'head'=4] {'z0','y'}, dimensions={0} | all-to-all | bytes 1048576 | tf_op jit(solution)/shard_map/all_to_all | solution.py:416
  95.6 0.1 leave.3
  95.7 3.5 %collective-permute-start.10 = (f32[8,128,128]{2,1,0:T(8,128)S(1)}, f32[8,128,128]{2,1,0:T(8,128)S(1)}, u32[]{:S(2)}, u32[]{:S(2)}) collective-permute-start(f32[8,128,128]{2,1,0:T(8,128)S(1)} %leave.3), channel_id=1, source_target_pairs={{0,4},{4,0},{1,5},{5,1},{2,6},{6,2},{3,7},{7,3},{8,12},{12,8},{9,1... | collective-permute-start | bytes 1572872 | tf_op jit(solution)/shard_map/ppermute | solution.py:408
  99.3 0.1 keep.3.state_ref
  99.3 1.3 %last0.1 = (bf16[256,2048]{1,0:T(8,128)(2,1)}, bf16[256,2048]{1,0:T(8,128)(2,1)}) custom-call(s32[1]{0:T(128)} %bitcast.core_ref, bf16[256,2048]{1,0:T(8,128)(2,1)S(1)} %get-tuple-element.95.keys_ref, bf16[256,2048]{1,0:T(8,128)(2,1)S(1)} %get-tuple-element.96.value_ref, f32[8,128,128]{2,1,0:T(8,128)S(1)} %keep.3.state_ref, ...), custom_call_target="tpu_custom_call" | custom-call | flops 134217728 | bytes 9043972 | tf_op jit(solution)/shard_map/last0/pallas_call | solution.py:28
  100.7 0.1 collective-permute-done.10.state_ref
  100.8 1.3 %last1.1 = (bf16[256,2048]{1,0:T(8,128)(2,1)}, bf16[256,2048]{1,0:T(8,128)(2,1)}) custom-call(s32[1]{0:T(128)} %bitcast.core_ref, bf16[256,2048]{1,0:T(8,128)(2,1)S(1)} %get-tuple-element.95.keys_ref, bf16[256,2048]{1,0:T(8,128)(2,1)S(1)} %get-tuple-element.96.value_ref, ...), custom_call_target="tpu_custom_call", output_to_operand_aliasing={{0}: (7, {}), {1}: (8, {})} | custom-call | flops 134217728 | bytes 11141124 | tf_op jit(solution)/shard_map/last1/pallas_call | solution.py:28
  (11 shorter events, 0.1 us)
Async XLA Ops:
  2.5 21.8 %copy-start = (bf16[256,2048]{1,0:T(8,128)(2,1)S(1)}, bf16[256,2048]{1,0:T(8,128)(2,1)}, u32[]{:S(2)}) copy-start(bf16[256,2048]{1,0:T(8,128)(2,1)} %query_ref.7) | copy-start | bytes 3145732
  2.5 21.8 %copy-start.1 = (bf16[256,2048]{1,0:T(8,128)(2,1)S(1)}, bf16[256,2048]{1,0:T(8,128)(2,1)}, u32[]{:S(2)}) copy-start(bf16[256,2048]{1,0:T(8,128)(2,1)} %gate_ref.5) | copy-start | bytes 3145732
  2.5 21.8 %copy-start.2 = (bf16[256,2048]{1,0:T(8,128)(2,1)S(1)}, bf16[256,2048]{1,0:T(8,128)(2,1)}, u32[]{:S(2)}) copy-start(bf16[256,2048]{1,0:T(8,128)(2,1)} %upstream_ref.1) | copy-start | bytes 3145732
  2.5 21.8 %copy-start.3 = (f32[2048]{0:T(1024)S(1)}, f32[2048]{0:T(1024)}, u32[]{:S(2)}) copy-start(f32[2048]{0:T(1024)} %param.12) | copy-start | bytes 24580
  2.5 4.9 %collective-permute-start = (f32[1040,128]{1,0:T(8,128)S(1)}, f32[1040,128]{1,0:T(8,128)S(1)}, u32[]{:S(2)}, u32[]{:S(2)}) collective-permute-start(f32[1040,128]{1,0:T(8,128)S(1)} %get-tuple-element.99), channel_id=1, source_target_pairs={{0,4},{4,0},{1,5},{5,1},{2,6},{6,2},{3,7},{7,3},{8,12},{12,8},{9,1... | collective-permute-start | bytes 1597448 | tf_op jit(solution)/shard_map/ppermute | solution.py:408
  21.2 5.5 %collective-permute-start.1 = (f32[136,128]{1,0:T(8,128)S(1)}, f32[136,128]{1,0:T(8,128)S(1)}, u32[]{:S(2)}, u32[]{:S(2)}) collective-permute-start(f32[136,128]{1,0:T(8,128)S(1)} %row_total.2.own_ref), channel_id=1, source_target_pairs={{0,64},{64,0},{128,192},{192,128},{1,65},{65,1},{129,193},{193,129... | collective-permute-start | bytes 208904 | tf_op jit(solution)/shard_map/ppermute | solution.py:412
  26.7 5.7 %collective-permute-start.2 = (f32[128,128]{1,0:T(8,128)S(1)}, f32[128,128]{1,0:T(8,128)S(1)}, u32[]{:S(2)}, u32[]{:S(2)}) collective-permute-start(f32[128,128]{1,0:T(8,128)S(1)} %pair.2), channel_id=1, source_target_pairs={{0,192},{64,128},{128,64},{192,0},{1,193},{65,129},{129,65},{193,1... | collective-permute-start | bytes 196616 | tf_op jit(solution)/shard_map/ppermute | solution.py:412
  43.9 5.1 %collective-permute-start.3 = (f32[8,128,128]{2,1,0:T(8,128)S(1)}, f32[8,128,128]{2,1,0:T(8,128)S(1)}, u32[]{:S(2)}, u32[]{:S(2)}) collective-permute-start(f32[8,128,128]{2,1,0:T(8,128)S(1)} %leave.2), channel_id=1, source_target_pairs={{0,4},{4,0},{1,5},{5,1},{2,6},{6,2},{3,7},{7,3},{8,12},{12,8},{9,1... | collective-permute-start | bytes 1572872 | tf_op jit(solution)/shard_map/ppermute | solution.py:408
  49.6 4.3 %collective-permute-start.6 = (f32[8,256]{1,0:T(8,128)S(1)}, f32[8,256]{1,0:T(8,128)S(1)}, u32[]{:S(2)}, u32[]{:S(2)}) collective-permute-start(f32[8,256]{1,0:T(8,128)S(1)} %get-tuple-element.132.sum_a), channel_id=1, source_target_pairs={{0,3},{1,2},{2,1},{3,0},{4,7},{5,6},{6,5},{7,4},{8,11},{9,10},{10,... | collective-permute-start | bytes 24584 | tf_op jit(solution)/shard_map/ppermute | solution.py:412
  52.2 4.0 %collective-permute-start.5 = (f32[8,256]{1,0:T(8,128)S(1)}, f32[8,256]{1,0:T(8,128)S(1)}, u32[]{:S(2)}, u32[]{:S(2)}) collective-permute-start(f32[8,256]{1,0:T(8,128)S(1)} %get-tuple-element.132.sum_a), channel_id=1, source_target_pairs={{0,2},{1,3},{2,0},{3,1},{4,6},{5,7},{6,4},{7,5},{8,10},{9,11},{10,... | collective-permute-start | bytes 24584 | tf_op jit(solution)/shard_map/ppermute | solution.py:412
  52.7 3.5 %collective-permute-start.4 = (f32[8,256]{1,0:T(8,128)S(1)}, f32[8,256]{1,0:T(8,128)S(1)}, u32[]{:S(2)}, u32[]{:S(2)}) collective-permute-start(f32[8,256]{1,0:T(8,128)S(1)} %get-tuple-element.132.sum_a), channel_id=1, source_target_pairs={{0,1},{1,0},{2,3},{3,2},{4,5},{5,4},{6,7},{7,6},{8,9},{9,8},{10,11... | collective-permute-start | bytes 24584 | tf_op jit(solution)/shard_map/ppermute | solution.py:412
  56.9 3.6 %collective-permute-start.7 = (f32[1024,128]{1,0:T(8,128)S(1)}, f32[1024,128]{1,0:T(8,128)S(1)}, u32[]{:S(2)}, u32[]{:S(2)}) collective-permute-start(f32[1024,128]{1,0:T(8,128)S(1)} %get-tuple-element.140), channel_id=1, source_target_pairs={{0,4},{4,0},{1,5},{5,1},{2,6},{6,2},{3,7},{7,3},{8,12},{12,8},{9,1... | collective-permute-start | bytes 1572872 | tf_op jit(solution)/shard_map/ppermute | solution.py:408
  71.8 5.2 %collective-permute-start.8 = (f32[136,128]{1,0:T(8,128)S(1)}, f32[136,128]{1,0:T(8,128)S(1)}, u32[]{:S(2)}, u32[]{:S(2)}) collective-permute-start(f32[136,128]{1,0:T(8,128)S(1)} %row_total.3.own_ref), channel_id=1, source_target_pairs={{0,64},{64,0},{128,192},{192,128},{1,65},{65,1},{129,193},{193,129... | collective-permute-start | bytes 208904 | tf_op jit(solution)/shard_map/ppermute | solution.py:412
  77.0 6.4 %collective-permute-start.9 = (f32[128,128]{1,0:T(8,128)S(1)}, f32[128,128]{1,0:T(8,128)S(1)}, u32[]{:S(2)}, u32[]{:S(2)}) collective-permute-start(f32[128,128]{1,0:T(8,128)S(1)} %pair.3), channel_id=1, source_target_pairs={{0,192},{64,128},{128,64},{192,0},{1,193},{65,129},{129,65},{193,1... | collective-permute-start | bytes 196616 | tf_op jit(solution)/shard_map/ppermute | solution.py:412
  95.7 5.1 %collective-permute-start.10 = (f32[8,128,128]{2,1,0:T(8,128)S(1)}, f32[8,128,128]{2,1,0:T(8,128)S(1)}, u32[]{:S(2)}, u32[]{:S(2)}) collective-permute-start(f32[8,128,128]{2,1,0:T(8,128)S(1)} %leave.3), channel_id=1, source_target_pairs={{0,4},{4,0},{1,5},{5,1},{2,6},{6,2},{3,7},{7,3},{8,12},{12,8},{9,1... | collective-permute-start | bytes 1572872 | tf_op jit(solution)/shard_map/ppermute | solution.py:408
